TPU v7x, 768 devices: a whole 4x8x12 slice. The times are simulated.
768 devices in a mesh: ctx: 12 (over z_lo, core), ch: 64 (over z_hi, y, x).
Axes of the slice: x: 4, y: 8, z: 12 (z_hi: 2, z_lo: 6; z = z_hi * 6 + z_lo), core: 2. Of those that a mesh axis runs over, the one named last changes fastest.
Arguments:
- streams: bfloat16 [3, 4608, 3072], P(None, 'ch', 'ctx'), may hold values from -6 to 6
- short_taps: float32 [3, 4608, 3], P(None, 'ch'), may hold values from -1 to 1
- filter_in: float32 [32, 64], replicated, may hold values from -1 to 1
- filter_mid: float32 [64, 64], replicated, may hold values from -0.75 to 0.75
- filter_out: float32 [64, 4608], P(None, 'ch'), may hold values from -2 to 2
- decay_rate: float32 [4608], P('ch'), as said below
- skip_gain: float32 [4608], P('ch'), may hold values from 0.5 to 1.5
- out_weight: bfloat16 [4608, 4608], P('ch'), may hold values from -0.09375 to 0.09375
- grad_out: bfloat16 [4608, 3072], P('ch', 'ctx'), may hold values from -6 to 6
Outputs:
- layer_out: bfloat16 [4608, 3072], P('ch', 'ctx')
- grad_streams: bfloat16 [3, 4608, 3072], P(None, 'ch', 'ctx')
- grad_filter_in: float32 [32, 64], replicated
- grad_filter_mid: float32 [64, 64], replicated
- grad_filter_out: float32 [64, 4608], P(None, 'ch')
- grad_out_weight: float32 [4608, 4608], P('ch')
Inputs may be any that keep to these rules, and one draw needn't show every extreme that they name: `decay_rate`: every channel's rate lies between 1 / 15360 and 1 / 30.
All inputs are finite; a program needn't handle non-finite values.
Results may differ from a plain program's by a relative error of at most 0.014.
Values may be sent and summed in bfloat16 or wider, within the bound.
No kernel may reach another device: no remote copies, remote signals or barrier semaphores. Data moves between devices by JAX's collectives and lax.ppermute only.
A program may use at most 64 MiB of HBM per device.

v0:
```python
import math

import jax
import jax.numpy as jnp
from jax import lax
from jax.sharding import PartitionSpec as P

precise = lax.Precision.HIGHEST


def passed_along(value, axis, by):
    peers = lax.axis_size(axis)
    pairs = [(i, i + by) for i in range(peers) if 0 <= i + by < peers]
    return lax.ppermute(value, axis, pairs)


def filter_values(filter_in, filter_mid, filter_out, decay_rate, length):
    band_count = filter_in.shape[0] // 2
    lag_index = jnp.arange(length)
    level_index = jnp.arange(1, band_count + 1)
    wrapped = level_index[:, None] * lag_index[None, :] % length
    phases = 2.0 * math.pi / length * wrapped.astype(jnp.float32)
    features = jnp.concatenate([jnp.cos(phases), jnp.sin(phases)], axis=0)
    hidden_one = jnp.sin(jnp.einsum("fh,fs->hs", filter_in, features, precision=precise))
    hidden_two = jnp.sin(jnp.einsum("gh,gs->hs", filter_mid, hidden_one, precision=precise))
    raw_out = jnp.einsum("hc,hs->cs", filter_out, hidden_two, precision=precise)
    lag_axis = lag_index.astype(jnp.float32)
    return (
        raw_out * jnp.exp(-decay_rate[:, None] * lag_axis[None, :]) * jnp.sqrt(decay_rate)[:, None]
    )


def fourier_tables(width_sub):
    double = 2 * width_sub
    row_index = jnp.arange(width_sub)
    col_index = jnp.arange(double)
    forward_phase = (
        2.0
        * math.pi
        / double
        * (row_index[:, None] * row_index[None, :] % double).astype(jnp.float32)
    )
    row_parity = (1 - 2 * (row_index % 2)).astype(jnp.float32)
    first_column = (row_index == 0)[None, :]
    forward_cos = jnp.cos(forward_phase)
    forward_sin = jnp.where(first_column, row_parity[:, None], -jnp.sin(forward_phase))
    inverse_phase = (
        2.0
        * math.pi
        / double
        * (row_index[:, None] * col_index[None, :] % double).astype(jnp.float32)
    )
    row_weight = jnp.where(row_index == 0, 1.0, 2.0).astype(jnp.float32)[:, None] / double
    col_parity = (1 - 2 * (col_index % 2)).astype(jnp.float32)
    inverse_cos = row_weight * jnp.cos(inverse_phase)
    inverse_sin = jnp.where(
        (row_index == 0)[:, None],
        col_parity[None, :] / double,
        -2.0 / double * jnp.sin(inverse_phase),
    )
    edge_mask = (row_index == 0).astype(jnp.float32)
    return (forward_cos, forward_sin, inverse_cos, inverse_sin, edge_mask)


def spectral_product(left_real, left_imag, right_real, right_imag, edge_mask):
    interior = 1.0 - edge_mask
    real_part = left_real * right_real - interior * left_imag * right_imag
    imag_part = (
        interior * (left_real * right_imag + left_imag * right_real)
        + edge_mask * left_imag * right_imag
    )
    return (real_part, imag_part)


def spectral_adjoint(left_real, left_imag, right_real, right_imag, edge_mask):
    interior = 1.0 - edge_mask
    real_part = left_real * right_real + interior * left_imag * right_imag
    imag_part = (
        interior * (left_real * right_imag - left_imag * right_real)
        + edge_mask * left_imag * right_imag
    )
    return (real_part, imag_part)


def shards(
    streams,
    short_taps,
    filter_in,
    filter_mid,
    filter_out,
    decay_rate,
    skip_gain,
    out_weight,
    grad_out,
):
    channels = streams.shape[1]
    tokens = streams.shape[2]
    cycle_size = lax.axis_size("ctx")
    cycle_index = lax.axis_index("ctx")
    length = tokens * cycle_size
    width_sub = min(256, tokens)
    pieces = tokens // width_sub
    lag_blocks = length // width_sub
    forward_cos, forward_sin, inverse_cos, inverse_sin, edge_mask = fourier_tables(width_sub)
    taps_width = short_taps.shape[2]

    def make_filter(first_w, middle_w, last_w):
        return filter_values(first_w, middle_w, last_w, decay_rate, length)

    long_filter, pullback = jax.vjp(make_filter, filter_in, filter_mid, filter_out)
    prefix = passed_along(streams[:, :, tokens - taps_width + 1 :], "ctx", 1)
    extended = jnp.concatenate([prefix, streams], axis=2).astype(jnp.float32)
    filtered = jnp.zeros(streams.shape, jnp.float32)
    for lag_step in range(taps_width):
        begin = taps_width - 1 - lag_step
        filtered = (
            filtered
            + short_taps[:, :, lag_step : lag_step + 1] * extended[:, :, begin : begin + tokens]
        )
    product = (filtered[1] * filtered[2]).astype(jnp.bfloat16)
    product_wide = product.astype(jnp.float32)

    def to_spectra(signal):
        return (
            jnp.dot(signal, forward_cos, precision=precise),
            jnp.dot(signal, forward_sin, precision=precise),
        )

    def conv_add(running, lag_real, lag_imag, src_real, src_imag, start):
        count = src_real.shape[1]

        def conv_one_source(source, accum):
            first_row = start + count - 1 - source
            window_real = lax.dynamic_slice_in_dim(lag_real, first_row, count + 1, 1)
            window_imag = lax.dynamic_slice_in_dim(lag_imag, first_row, count + 1, 1)
            piece_real, piece_imag = spectral_product(
                window_real, window_imag, src_real, src_imag, edge_mask
            )
            return (accum[0] + piece_real, accum[1] + piece_imag)

        return lax.fori_loop(0, count, conv_one_source, running)

    def grad_spectra(values):
        zero_row = jnp.zeros((values.shape[0], 1, width_sub), jnp.float32)
        lower_half = jnp.concatenate([zero_row, values], axis=1)
        upper_half = jnp.concatenate([values, zero_row], axis=1)
        stacked_full = jnp.concatenate([lower_half, upper_half], axis=2)
        return (
            jnp.dot(stacked_full, inverse_cos.T, precision=precise),
            jnp.dot(stacked_full, inverse_sin.T, precision=precise),
        )

    def adjoint_add(state, lag_real, lag_imag, own_real, own_imag, grad_real, grad_imag, start):
        count = own_real.shape[1]

        def adjoint_one_source(source, current):
            back_real, back_imag, lag_grad_real, lag_grad_imag = current
            first_row = start + count - 1 - source
            window_real = lax.dynamic_slice_in_dim(lag_real, first_row, count + 1, 1)
            window_imag = lax.dynamic_slice_in_dim(lag_imag, first_row, count + 1, 1)
            piece_real, piece_imag = spectral_adjoint(
                window_real, window_imag, grad_real, grad_imag, edge_mask
            )
            back_real = back_real + jnp.sum(piece_real, axis=1, keepdims=True)
            back_imag = back_imag + jnp.sum(piece_imag, axis=1, keepdims=True)
            term_real, term_imag = spectral_adjoint(
                own_real, own_imag, grad_real, grad_imag, edge_mask
            )
            lag_grad_real = lax.dynamic_update_slice_in_dim(
                lag_grad_real,
                lax.dynamic_slice_in_dim(lag_grad_real, first_row, count + 1, 1) + term_real,
                first_row,
                1,
            )
            lag_grad_imag = lax.dynamic_update_slice_in_dim(
                lag_grad_imag,
                lax.dynamic_slice_in_dim(lag_grad_imag, first_row, count + 1, 1) + term_imag,
                first_row,
                1,
            )
            return (back_real, back_imag, lag_grad_real, lag_grad_imag)

        return lax.fori_loop(0, count, adjoint_one_source, state)

    rows_here = long_filter.shape[0]
    spec_real, spec_imag = to_spectra(long_filter.reshape(rows_here, lag_blocks, width_sub))
    leading = jnp.zeros((rows_here, pieces, width_sub), jnp.float32)
    lag_real = jnp.concatenate([leading, spec_real], axis=1)
    lag_imag = jnp.concatenate([leading, spec_imag], axis=1)
    own_real, own_imag = to_spectra(product_wide.reshape(channels, pieces, width_sub))

    def from_raw(running, raw_block, offset):
        block_real, block_imag = to_spectra(
            raw_block.astype(jnp.float32).reshape(channels, pieces, width_sub)
        )
        return conv_add(running, lag_real, lag_imag, block_real, block_imag, offset * pieces)

    blank_sum = jnp.zeros((channels, pieces + 1, width_sub), jnp.float32)
    running = conv_add((blank_sum, blank_sum), lag_real, lag_imag, own_real, own_imag, 0)

    def forward_step(offset, state):
        current, moving = state
        moving = passed_along(moving, "ctx", 1)
        current = lax.cond(
            cycle_index >= offset,
            lambda inner: from_raw(inner, moving, offset),
            lambda inner: inner,
            current,
        )
        return (current, moving)

    running, moving = lax.fori_loop(1, cycle_size, forward_step, (running, product))
    sum_real, sum_imag = running
    double_out = jnp.dot(sum_real, inverse_cos, precision=precise) + jnp.dot(
        sum_imag, inverse_sin, precision=precise
    )
    joined = double_out[:, 1:, :width_sub] + double_out[:, :pieces, width_sub:]
    long_conv = joined.reshape(joined.shape[0], pieces * width_sub)
    long_out = long_conv + skip_gain[:, None] * product_wide
    gated_out = (filtered[0] * long_out).astype(jnp.bfloat16)
    piece = lax.all_gather(gated_out, "ch", axis=0, tiled=True)
    columns = out_weight
    out_total = jnp.dot(columns, piece, preferred_element_type=jnp.float32)
    weight_piece = jnp.einsum("dt,ct->dc", grad_out, piece, preferred_element_type=jnp.float32)
    out_total, weight_part = (out_total, weight_piece)
    layer_out = out_total.astype(jnp.bfloat16)
    columns = out_weight
    grad_gated = lax.psum_scatter(
        jnp.einsum("dc,dt->ct", columns, grad_out, preferred_element_type=jnp.float32),
        "ch",
        scatter_dimension=0,
        tiled=True,
    ).astype(jnp.bfloat16)
    grad_gated_wide = grad_gated.astype(jnp.float32)
    grad_long = (grad_gated_wide * filtered[0]).astype(jnp.bfloat16)
    grad_long_wide = grad_long.astype(jnp.float32)
    grad_first = grad_gated_wide * long_out

    def from_grad(state, raw_block, offset):
        grad_real, grad_imag = grad_spectra(
            raw_block.astype(jnp.float32).reshape(channels, pieces, width_sub)
        )
        return adjoint_add(
            state, lag_real, lag_imag, own_real, own_imag, grad_real, grad_imag, offset * pieces
        )

    zero_back = jnp.zeros((channels, pieces, width_sub), jnp.float32)
    zero_lags = jnp.zeros((channels, lag_blocks + pieces, width_sub), jnp.float32)
    backward = from_grad((zero_back, zero_back, zero_lags, zero_lags), grad_long, 0)

    def backward_step(offset, state):
        current, moving = state
        moving = passed_along(moving, "ctx", -1)
        current = lax.cond(
            cycle_index + offset < cycle_size,
            lambda inner: from_grad(inner, moving, offset),
            lambda inner: inner,
            current,
        )
        return (current, moving)

    backward, moving = lax.fori_loop(1, cycle_size, backward_step, (backward, grad_long))
    back_real, back_imag, lag_grad_real, lag_grad_imag = backward
    rows_here = back_real.shape[0]
    back_signal = jnp.dot(back_real, forward_cos.T, precision=precise) + jnp.dot(
        back_imag, forward_sin.T, precision=precise
    )
    lag_signal = jnp.dot(lag_grad_real[:, pieces:], forward_cos.T, precision=precise) + jnp.dot(
        lag_grad_imag[:, pieces:], forward_sin.T, precision=precise
    )
    back_conv = back_signal.reshape(rows_here, pieces * width_sub)
    grad_lag = lag_signal.reshape(rows_here, length)
    grad_product = back_conv + skip_gain[:, None] * grad_long_wide
    grad_filtered = jnp.stack([grad_first, grad_product * filtered[2], grad_product * filtered[1]])
    suffix = passed_along(grad_filtered[:, :, : taps_width - 1], "ctx", -1)
    grad_extended = jnp.concatenate([grad_filtered, suffix], axis=2)
    result = jnp.zeros(grad_filtered.shape, jnp.float32)
    for lag_step in range(taps_width):
        result = (
            result
            + short_taps[:, :, lag_step : lag_step + 1]
            * grad_extended[:, :, lag_step : lag_step + tokens]
        )
    grad_streams = result.astype(jnp.bfloat16)
    grad_filter_in, grad_filter_mid, grad_filter_out = pullback(grad_lag)
    grad_filter_out, weight_part = lax.psum((grad_filter_out, weight_part), "ctx")
    grad_filter_in, grad_filter_mid = lax.psum((grad_filter_in, grad_filter_mid), ("ctx", "ch"))
    return (layer_out, grad_streams, grad_filter_in, grad_filter_mid, grad_filter_out, weight_part)


def solution(mesh):
    return jax.shard_map(
        shards,
        mesh=mesh,
        in_specs=(
            P(None, "ch", "ctx"),
            P(None, "ch", None),
            P(),
            P(),
            P(None, "ch"),
            P("ch"),
            P("ch"),
            P("ch", None),
            P("ch", "ctx"),
        ),
        out_specs=(P("ch", "ctx"), P(None, "ch", "ctx"), P(), P(), P(None, "ch"), P("ch", None)),
        check_vma=False,
    )
```

profile of v0, /device:TPU:1, one launch (start us, length us, event | category | flops | bytes accessed | tf_op | source)
XLA Modules:
  0.0 1485.5 jit_solution(3566041087906726438)
XLA Ops:
  8.3 3.8 fusion.223
  13.0 5.4 collective-permute-start.2
  20.0 4.4 fusion.219
  24.4 4.6 fusion.220
  39.7 879.0 %reduce-scatter.2.cloned.1.call-done = f32[72,256]{1,0:T(8,128)} async-done(((f32[4608,256]{1,0:T(8,128)}), f32[72,256]{1,0:T(8,128)}) %reduce-scatter.2.cloned.1.call-update) | async-done | bytes 73744 | tf_op jit(solution)/shard_map/reduce_scatter | solution.py:228
  923.4 3.3 fusion.71
  926.6 4.7 add_reduce_fusion.2
  933.4 137.2 %while.33 = (s32[]{:T(128)}, f32[72,1,256]{2,1,0:T(1,128)S(1)}, f32[72,1,256]{2,1,0:T(1,128)S(1)}, f32[72,13,256]{2,0,1:T(8,128)}, f32[72,13,256]{2,0,1:T(8,128)...) while((s32[]{:T(128)}, f32[72,1,256]{2,1,0:T(1,128)S(1)}, ...), condition=%wide.region_12.13_spmd.clone.clone, body=%wide.region_7.12_spmd.clone.clone.sunk | while | flops 456891904 | bytes 4356845 | solution.py:262
  933.5 6.1 collective-permute-start.1
  941.9 7.6 conditional.9
  945.0 4.3 add_dynamic-update-slice_fusion
  951.7 3.1 collective-permute-done.1
  954.8 7.6 conditional.9
  957.9 4.3 add_dynamic-update-slice_fusion
  964.6 3.1 collective-permute-done.1
  967.7 7.5 conditional.9
  970.7 4.3 add_dynamic-update-slice_fusion
  977.5 3.1 collective-permute-done.1
  980.5 7.6 conditional.9
  980.6 3.0 fusion.30
  983.6 4.3 add_dynamic-update-slice_fusion
  990.3 3.1 collective-permute-done.1
  993.4 7.5 conditional.9
  996.5 4.3 add_dynamic-update-slice_fusion
  1003.2 3.1 collective-permute-done.1
  1006.3 7.6 conditional.9
  1009.4 4.3 add_dynamic-update-slice_fusion
  1016.1 3.1 collective-permute-done.1
  1019.2 7.6 conditional.9
  1019.2 3.0 fusion.30
  1022.2 4.3 add_dynamic-update-slice_fusion
  1029.0 3.1 collective-permute-done.1
  1032.0 7.6 conditional.9
  1032.1 3.0 fusion.30
  1035.1 4.3 add_dynamic-update-slice_fusion
  1041.8 3.1 collective-permute-done.1
  1044.9 7.6 conditional.9
  1048.0 4.3 add_dynamic-update-slice_fusion
  1054.7 3.1 collective-permute-done.1
  1057.8 7.6 conditional.9
  1060.9 4.3 add_dynamic-update-slice_fusion
  1067.6 3.1 collective-permute-done.1
  1074.0 79.3 %while.32 = (s32[]{:T(128)}, f32[72,2,256]{2,1,0:T(2,128)S(1)}, f32[72,2,256]{2,1,0:T(2,128)S(1)}, bf16[72,256]{1,0:T(8,128)(2,1)}, s32[]{:T(128)}, /*index=5*/f...) while((s32[]{:T(128)}, f32[72,2,256]{2,1,0:T(2,128)S(1)}, ...), condition=%wide.region_3.4_spmd.clone.clone, body=%wide.region_0.3_spmd.clone.clone.sunk | while | flops 114775040 | bytes 2270801 | solution.py:212
  1076.1 5.6 collective-permute-done
  1081.6 4.3 conditional.8
  1090.5 8.3 collective-permute-start
  1100.8 4.1 collective-permute-start
  1106.9 4.1 collective-permute-start
  1113.0 4.1 collective-permute-start
  1119.1 5.8 collective-permute-start
  1126.8 4.1 collective-permute-start
  1132.9 4.1 collective-permute-start
  1139.0 4.1 collective-permute-start
  1145.1 5.8 collective-permute-start
  1153.3 3.1 fusion.73
  1156.5 3.2 convolution_add_fusion.1
  1164.7 3.1 fusion.55
  1171.6 74.0 %psum.30 = f32[64,72]{1,0:T(8,128)} all-reduce(f32[64,72]{1,0:T(8,128)S(1)} %fusion.64), channel_id=1, replica_groups=mesh['ctx'=12,'ch'=64] {'ctx'}, use_global_device_ids=true, to_apply=%region_15.16 | all-reduce | flops 4608 | bytes 36864 | tf_op jit(solution)/shard_map/psum | solution.py:286
  1245.6 3.5 convolution_multiply_fusion.1
  1249.1 87.9 %all-gather.2.cloned.1.call-done = bf16[4608,256]{1,0:T(8,128)(2,1)} async-done(((bf16[72,256]{1,0:T(8,128)(2,1)}), bf16[4608,256]{1,0:T(8,128)(2,1)}) %all-gather.2.cloned.1.call-update) | async-done | bytes 2359312 | tf_op jit(solution)/shard_map/all_gather | solution.py:221
  1337.0 3.6 convolution_bitcast_fusion
  1340.6 3.4 convolution_multiply_fusion
  1346.7 109.8 %all-reduce.8 = (f32[32,64]{1,0:T(8,128)}, f32[64,64]{1,0:T(8,128)}) all-reduce(f32[32,64]{1,0:T(8,128)S(1)} %fusion.84, f32[64,64]{1,0:T(8,128)S(1)} %fusion.224), channel_id=1, replica_groups=mesh['ctx'=12,'ch'=64] {'ctx','ch'}, use_global_device_ids=true, to_apply=%region_13.14 | all-reduce | flops 6144 | bytes 49152 | tf_op jit(solution)/shard_map/psum | solution.py:287
  1460.5 15.8 %all-reduce.11.cloned.1.call-done = f32[72,4608]{1,0:T(8,128)} async-done(((f32[72,4608]{1,0:T(8,128)}), f32[72,4608]{1,0:T(8,128)}) %all-reduce.11.cloned.1.call-update) | async-done | bytes 1327120 | tf_op jit(solution)/shard_map/psum | solution.py:286
  (293 shorter events, 117.5 us)
Async XLA Ops:
  7.2 1.1 copy-start
  7.2 911.5 %reduce-scatter.2.cloned.1.call-start = ((), (), s32[]{:S(2)}) async-start(), calls=%async_computation.2 | async-start | bytes 4792320 | tf_op jit(solution)/shard_map/reduce_scatter | solution.py:228
  12.0 0.9 copy-start.14
  12.0 7.0 copy-start.27
  12.0 7.0 copy-start.26
  12.0 8.0 copy-start.23
  12.1 12.4 copy-start.18
  12.1 1324.9 %all-gather.2.cloned.1.call-start = ((), (), s32[]{:S(2)}) async-start(), calls=%async_computation.1 | async-start | bytes 2396160 | tf_op jit(solution)/shard_map/all_gather | solution.py:221
  13.0 26.3 %collective-permute-start.2 = (bf16[3,72,2]{2,1,0:T(8,128)(2,1)S(1)}, bf16[3,72,2]{2,1,0:T(8,128)(2,1)S(1)}, u32[]{:S(2)}, u32[]{:S(2)}) collective-permute-start(bf16[3,72,2]{2,1,0:T(8,128)(2,1)S(1)} %slice.60), channel_id=1, source_target_pairs={{0,64},{64,128},{128,192},{192,256},{256,320},{320,384},{384,448},... | collective-permute-start | bytes 2600 | tf_op jit(solution)/shard_map/ppermute | solution.py:14
  19.1 10.0 copy-start.24
  19.1 10.0 copy-start.20
  20.0 4.5 copy-start.8
  24.4 4.6 copy-start.2
  39.7 886.9 %copy-start.10 = (f32[3,72,256]{2,1,0:T(8,128)}, f32[3,72,256]{2,1,0:T(8,128)S(1)}, u32[]{:S(2)}) copy-start(f32[3,72,256]{2,1,0:T(8,128)S(1)} %fusion.112) | copy-start | bytes 663556
  919.6 7.0 copy-start.15
  933.5 8.4 collective-permute-start.1
  949.5 5.3 collective-permute-start.1
  962.4 5.3 collective-permute-start.1
  975.2 5.3 collective-permute-start.1
  988.1 5.3 collective-permute-start.1
  1001.0 5.3 collective-permute-start.1
  1013.9 5.3 collective-permute-start.1
  1026.8 5.3 collective-permute-start.1
  1039.6 5.3 collective-permute-start.1
  1052.5 5.3 collective-permute-start.1
  1065.4 5.3 collective-permute-start.1
  1074.0 7.6 collective-permute-start
  1086.5 3.3 collective-permute-start
  1090.5 9.7 collective-permute-start
  1100.8 5.5 collective-permute-start
  1106.9 5.5 collective-permute-start
  1113.0 5.5 collective-permute-start
  1119.1 7.1 collective-permute-start
  1126.8 5.5 collective-permute-start
  1132.9 5.5 collective-permute-start
  1139.0 5.5 collective-permute-start
  1145.1 7.1 collective-permute-start
  1153.3 6.4 copy-start.16
  1153.3 6.4 copy-start.22
  1153.3 6.4 copy-start.28
  1156.5 6.3 copy-start.5
  1162.7 313.6 %all-reduce.11.cloned.1.call-start = ((), (), s32[]{:S(2)}) async-start(), calls=%async_computation.3 | async-start | bytes 2654208 | tf_op jit(solution)/shard_map/psum | solution.py:286
  1164.6 3.3 copy-start.11
  1164.6 3.3 copy-start.12
  1164.6 3.3 copy-start.13
  1164.7 5.9 copy-start.25
  1167.8 77.8 %copy-start.7 = (f32[3072,64]{0,1:T(8,128)S(1)}, f32[3072,64]{0,1:T(8,128)}, u32[]{:S(2)}) copy-start(f32[3072,64]{0,1:T(8,128)} %get-tuple-element.987) | copy-start | bytes 2359300
  1167.8 77.8 %copy-start.21 = (f32[64,72]{1,0:T(8,128)S(1)}, f32[64,72]{1,0:T(8,128)}, u32[]{:S(2)}) copy-start(f32[64,72]{1,0:T(8,128)} %param.21) | copy-start | bytes 55300
  1167.9 169.0 %copy-start.17 = (bf16[72,256]{1,0:T(8,128)(2,1)S(1)}, bf16[72,256]{1,0:T(8,128)(2,1)}, u32[]{:S(2)}) copy-start(bf16[72,256]{1,0:T(8,128)(2,1)} %param.25) | copy-start | bytes 110596
  1168.6 287.9 %collective-permute-start.3 = (f32[3,72,2]{2,1,0:T(8,128)}, f32[3,72,2]{2,1,0:T(8,128)}, u32[]{:S(2)}, u32[]{:S(2)}) collective-permute-start(f32[3,72,2]{2,1,0:T(8,128)} %slice.84), channel_id=1, source_target_pairs={{64,0},{128,64},{192,128},{256,192},{320,256},{384,320},{448,384},... | collective-permute-start | bytes 5192 | tf_op jit(solution)/shard_map/ppermute | solution.py:14
  1249.0 91.5 %copy-start.4 = (f32[3072,64]{0,1:T(8,128)}, f32[3072,64]{0,1:T(8,128)S(1)}, u32[]{:S(2)}) copy-start(f32[3072,64]{0,1:T(8,128)S(1)} %convolution_multiply_fusion.1) | copy-start | bytes 2359300
  1249.1 91.5 %copy-start.6 = (f32[3072,64]{0,1:T(8,128)S(1)}, f32[3072,64]{0,1:T(8,128)}, u32[]{:S(2)}) copy-start(f32[3072,64]{0,1:T(8,128)} %get-tuple-element.985) | copy-start | bytes 2359300
  1249.1 91.5 %copy-start.19 = (f32[64,64]{1,0:T(8,128)S(1)}, f32[64,64]{1,0:T(8,128)}, u32[]{:S(2)}) copy-start(f32[64,64]{1,0:T(8,128)} %param.20) | copy-start | bytes 49156
  1340.5 3.5 copy-start.9
  1340.5 4.2 copy-start.3
  1344.0 115.4 %copy-start.1 = (bf16[4608,256]{1,0:T(8,128)(2,1)S(1)}, bf16[4608,256]{1,0:T(8,128)(2,1)}, u32[]{:S(2)}) copy-start(bf16[4608,256]{1,0:T(8,128)(2,1)} %all-gather.2.cloned.1.call-done) | copy-start | bytes 7077892
Sparse Core Ops, SparseCore 0:
  14.4 904.2 reduce-scatter.1
  1162.8 174.0 all-gather.1
  1340.8 135.4 all-reduce.10
where the time goes:
time: 1490 us
  waiting for transfers between devices  1030 us (69%)
  blocking collectives  184 us (12%)
  matrix products  136 us (9%)
  starting transfers between devices  81.1 us (5%)
  local copies, waits for them, and re-layouts  20.8 us (1%)
    reduce_scatter x1, waiting for transfers between devices, shards(): lax.psum_scatter(jnp.einsum('dc,dt->ct', columns, grad_out, preferred_ele...  879 us
    psum x1, blocking collectives, shards(): lax.psum((grad_filter_in, grad_filter_mid), ('ctx', 'ch'))  110 us
    all_gather x1, waiting for transfers between devices, shards(): piece = lax.all_gather(gated_out, 'ch', axis=0, tiled=True)  87.9 us
    ppermute x24, starting transfers between devices, passed_along(): return lax.ppermute(value, axis, pairs)  81 us
    psum x1, blocking collectives, shards(): lax.psum((grad_filter_out, weight_part), 'ctx')  74 us
    ppermute x24, waiting for transfers between devices, passed_along(): return lax.ppermute(value, axis, pairs)  50.4 us
    dot_general x11, matrix products, grad_spectra(): jnp.dot(stacked_full, inverse_sin.T, precision=precise)  47.8 us
    dot_general x11, matrix products, grad_spectra(): jnp.dot(stacked_full, inverse_cos.T, precision=precise)  33.3 us
  transfers between devices with their start and end apart: 27, of which 25 were waited for; matrix products, arithmetic and copies ran while one was open for 3% of the time, Pallas kernels for 0%

commit v1 on v0

v1 whole, which is shorter than its diff:
```python
import functools
import math

import jax
import jax.numpy as jnp
import numpy as np
from jax import lax
from jax.experimental import pallas as pl
from jax.experimental.pallas import tpu as pltpu
from jax.sharding import PartitionSpec as P

f32 = jnp.float32
bf16 = jnp.bfloat16

BLOCK = 256
ROWS = 8
VMEM_LIMIT = 40 * 1024 * 1024


def split_table(table):
    high = table.astype(np.float32).astype(jnp.bfloat16)
    low = (table - high.astype(np.float64)).astype(np.float32).astype(jnp.bfloat16)
    return high, low


@functools.lru_cache(maxsize=None)
def transform_tables():
    frequency = np.arange(BLOCK)
    token = np.arange(BLOCK)
    angle = np.pi * ((2 * frequency[None, :] + 1) * token[:, None] % (4 * BLOCK)) / (2 * BLOCK)
    forward = np.concatenate([np.cos(angle), -np.sin(angle)], axis=1)
    return split_table(forward) + split_table(forward.T / BLOCK)


@functools.lru_cache(maxsize=None)
def position_features(band_count, length):
    wrapped = (np.arange(1, band_count + 1)[:, None] * np.arange(length)[None, :]) % length
    phases = 2.0 * np.pi / length * wrapped
    return np.concatenate([np.cos(phases), np.sin(phases)], axis=0).astype(np.float32)


def halves(value):
    high = value.astype(bf16)
    return high, (value - high.astype(f32)).astype(bf16)


def plain_dot(left, right, dims):
    return lax.dot_general(left, right, (dims, ((), ())), preferred_element_type=f32)


def close_dot(left, right, dims=((1,), (0,))):
    left_high, left_low = halves(left)
    right_high, right_low = halves(right)
    return (
        plain_dot(left_high, right_high, dims)
        + plain_dot(left_high, right_low, dims)
        + plain_dot(left_low, right_high, dims)
    )


def table_dot(left, high, low):
    dims = ((1,), (0,))
    if left.dtype == bf16:
        return plain_dot(left, high, dims) + plain_dot(left, low, dims)
    left_high, left_low = halves(left)
    return (
        plain_dot(left_high, high, dims)
        + plain_dot(left_high, low, dims)
        + plain_dot(left_low, high, dims)
    )


def sine_and_cosine(value):
    turns = jnp.floor(value * (2.0 / math.pi) + 0.5)
    rest = value - turns * 1.5703125
    rest = rest - turns * 4.837512969970703125e-4
    rest = rest - turns * 7.54978994876864e-8
    square = rest * rest
    sine = rest + rest * square * (
        -1.6666654611e-1 + square * (8.3321608736e-3 + square * -1.9515295891e-4)
    )
    cosine = (
        1.0
        - 0.5 * square
        + square
        * square
        * (4.166664568298827e-2 + square * (-1.388731625493765e-3 + square * 2.443315711809948e-5))
    )
    quadrant = turns.astype(jnp.int32)
    odd = (quadrant & 1) == 1
    sine_out = jnp.where(odd, cosine, sine)
    cosine_out = jnp.where(odd, sine, cosine)
    sine_out = jnp.where((quadrant & 2) == 2, -sine_out, sine_out)
    cosine_out = jnp.where(((quadrant + 1) & 2) == 2, -cosine_out, cosine_out)
    return sine_out, cosine_out


def envelope(decay, block):
    lag = (lax.broadcasted_iota(jnp.int32, (ROWS, BLOCK), 1) + block * BLOCK).astype(f32)
    return jnp.exp(-decay * lag) * jnp.sqrt(decay)


def parity():
    odd = lax.broadcasted_iota(jnp.int32, (ROWS, BLOCK), 1) & 1
    return (1 - 2 * odd).astype(f32)


DECAY, SKIP, OUT = 9, 10, 11


def network_kernel(
    features, filter_in, filter_mid, params, table_high, table_low,
    hidden_one, slope_one, hidden_two, slope_two, spectra, taps_scratch,
):
    count = features.shape[1] // BLOCK
    hidden = filter_in.shape[1]
    decay = params[:, DECAY : DECAY + 1]
    last = params[:, OUT : OUT + hidden]
    for block in range(count):
        at = slice(block * BLOCK, (block + 1) * BLOCK)
        sine, cosine = sine_and_cosine(
            close_dot(filter_in[...], features[:, at], ((0,), (0,)))
        )
        hidden_one[:, at] = sine
        slope_one[:, at] = cosine
        sine, cosine = sine_and_cosine(close_dot(filter_mid[...], sine, ((0,), (0,))))
        hidden_two[:, at] = sine
        slope_two[:, at] = cosine
        raw = close_dot(last, sine)
        taps_scratch[block * ROWS : (block + 1) * ROWS, :] = raw * envelope(decay, block)
    spectrum = table_dot(taps_scratch[...], table_high[...], table_low[...])
    sign = parity()
    for block in range(count):
        real = spectrum[block * ROWS : (block + 1) * ROWS, :BLOCK]
        imag = spectrum[block * ROWS : (block + 1) * ROWS, BLOCK:]
        if block:
            before = slice((block - 1) * ROWS, block * ROWS)
            real = real - sign * spectrum[before, BLOCK:]
            imag = imag + sign * spectrum[before, :BLOCK]
        spectra[block, :, :BLOCK] = real
        spectra[block, :, BLOCK:] = imag


def rows_of(value, rows):
    return value.reshape(value.shape[0] // rows, rows, value.shape[1])


def forward_kernel(
    blocks, params, spectra, table_high, table_low, back_high, back_low,
    gated, filtered, long_out, own_spectra, sums,
):
    count = blocks.shape[0]
    wide = 3 * ROWS
    raw = blocks[...].astype(f32).reshape(count * wide, BLOCK)
    lane = lax.broadcasted_iota(jnp.int32, (count * wide, BLOCK), 1)
    lead = jnp.zeros((wide, BLOCK), f32)
    shifted = [raw]
    for by in (1, 2):
        rolled = pltpu.roll(raw, by, 1)
        before = jnp.concatenate([lead, rolled[:-wide]], axis=0)
        shifted.append(jnp.where(lane < by, before, rolled))
    shifted = [rows_of(value, wide) for value in shifted]
    streams = []
    for stream in range(3):
        at = slice(stream * ROWS, (stream + 1) * ROWS)
        total = None
        for tap in range(3):
            column = stream * 3 + tap
            term = params[:, column : column + 1][None] * shifted[tap][:, at, :]
            total = term if total is None else total + term
        filtered[:, at, :] = total
        streams.append(total)
    product = (streams[1] * streams[2]).astype(bf16).astype(f32).reshape(count * ROWS, BLOCK)
    spectrum = table_dot(product.astype(bf16), table_high[...], table_low[...])
    own_spectra[...] = rows_of(spectrum, ROWS)
    for block in range(count):
        real = jnp.zeros((ROWS, BLOCK), f32)
        imag = jnp.zeros((ROWS, BLOCK), f32)
        for source in range(block + 1):
            filter_real = spectra[block - source, :, :BLOCK]
            filter_imag = spectra[block - source, :, BLOCK:]
            own_real = own_spectra[source, :, :BLOCK]
            own_imag = own_spectra[source, :, BLOCK:]
            real = real + filter_real * own_real - filter_imag * own_imag
            imag = imag + filter_real * own_imag + filter_imag * own_real
        sums[block * ROWS : (block + 1) * ROWS, :BLOCK] = real
        sums[block * ROWS : (block + 1) * ROWS, BLOCK:] = imag
    conv = table_dot(sums[...], back_high[...], back_low[...])
    skip = params[:, SKIP : SKIP + 1][None]
    result = rows_of(conv, ROWS) + skip * rows_of(product, ROWS)
    long_out[...] = result
    gated[...] = (streams[0] * result).reshape(count * ROWS, BLOCK).astype(bf16)


def backward_kernel(
    blocks, params, spectra, filtered, long_out, own_spectra,
    hidden_one, slope_one, hidden_two, slope_two, features, filter_mid,
    table_high, table_low, back_high, back_low,
    grad_streams, grad_shared, grad_last, sums, lag_sums, grad_spectra,
):
    count = blocks.shape[0]
    hidden = filter_mid.shape[0]
    wide = 3 * ROWS
    grad_gated = blocks[...].astype(f32)[:, ROWS : 2 * ROWS, :]
    query = filtered[:, :ROWS, :]
    grad_long = (grad_gated * query).reshape(count * ROWS, BLOCK).astype(bf16)
    spectrum = table_dot(grad_long, table_high[...], table_low[...])
    grad_spectra[...] = rows_of(spectrum, ROWS)
    sign = parity()
    after = None
    for block in reversed(range(count)):
        back_real = jnp.zeros((ROWS, BLOCK), f32)
        back_imag = jnp.zeros((ROWS, BLOCK), f32)
        lag_real = jnp.zeros((ROWS, BLOCK), f32)
        lag_imag = jnp.zeros((ROWS, BLOCK), f32)
        for target in range(block, count):
            grad_real = grad_spectra[target, :, :BLOCK]
            grad_imag = grad_spectra[target, :, BLOCK:]
            filter_real = spectra[target - block, :, :BLOCK]
            filter_imag = spectra[target - block, :, BLOCK:]
            back_real = back_real + filter_real * grad_real + filter_imag * grad_imag
            back_imag = back_imag + filter_real * grad_imag - filter_imag * grad_real
            own_real = own_spectra[target - block, :, :BLOCK]
            own_imag = own_spectra[target - block, :, BLOCK:]
            lag_real = lag_real + own_real * grad_real + own_imag * grad_imag
            lag_imag = lag_imag + own_real * grad_imag - own_imag * grad_real
        at = slice(block * ROWS, (block + 1) * ROWS)
        sums[at, :BLOCK] = back_real
        sums[at, BLOCK:] = back_imag
        if after is None:
            lag_sums[at, :BLOCK] = lag_real
            lag_sums[at, BLOCK:] = lag_imag
        else:
            lag_sums[at, :BLOCK] = lag_real + sign * after[1]
            lag_sums[at, BLOCK:] = lag_imag - sign * after[0]
        after = (lag_real, lag_imag)
    back = table_dot(sums[...], back_high[...], back_low[...])
    skip = params[:, SKIP : SKIP + 1][None]
    grad_product = rows_of(back, ROWS) + skip * rows_of(grad_long.astype(f32), ROWS)
    grads = [
        grad_gated * long_out[...],
        grad_product * filtered[:, 2 * ROWS :, :],
        grad_product * filtered[:, ROWS : 2 * ROWS, :],
    ]
    lane = lax.broadcasted_iota(jnp.int32, (count * ROWS, BLOCK), 1)
    tail = jnp.zeros((ROWS, BLOCK), f32)
    adjoint = []
    for stream in range(3):
        value = grads[stream].reshape(count * ROWS, BLOCK)
        total = params[:, stream * 3 : stream * 3 + 1][None] * grads[stream]
        for by in (1, 2):
            rolled = pltpu.roll(value, BLOCK - by, 1)
            following = jnp.concatenate([rolled[ROWS:], tail], axis=0)
            moved = jnp.where(lane >= BLOCK - by, following, rolled)
            column = stream * 3 + by
            total = total + params[:, column : column + 1][None] * rows_of(moved, ROWS)
        adjoint.append(total)
    half = BLOCK // 2
    packed = [part[:, :, :half] for part in adjoint] + [part[:, :, half:] for part in adjoint]
    grad_streams[...] = jnp.concatenate(packed, axis=1).astype(bf16)

    lags = table_dot(lag_sums[...], back_high[...], back_low[...])
    decay = params[:, DECAY : DECAY + 1]
    last = params[:, OUT : OUT + hidden]
    raw = [
        lags[block * ROWS : (block + 1) * ROWS] * envelope(decay, block)
        for block in range(count)
    ]
    total_last = jnp.zeros((ROWS, hidden), f32)
    total_mid = jnp.zeros((hidden, hidden), f32)
    total_in = jnp.zeros((features.shape[0], hidden), f32)
    across = ((1,), (1,))
    for block in range(count):
        at = slice(block * BLOCK, (block + 1) * BLOCK)
        total_last = total_last + close_dot(raw[block], hidden_two[:, at], across)
        grad_two = close_dot(last, raw[block], ((0,), (0,))) * slope_two[:, at]
        total_mid = total_mid + close_dot(hidden_one[:, at], grad_two, across)
        grad_one = close_dot(filter_mid[...], grad_two) * slope_one[:, at]
        total_in = total_in + close_dot(features[:, at], grad_one, across)
    high, low = halves(jnp.concatenate([total_in, total_mid], axis=0))
    grad_shared[...] = jnp.concatenate([high, low], axis=0)
    high, low = halves(total_last)
    grad_last[...] = jnp.concatenate([high.astype(f32), low.astype(f32)], axis=0).astype(bf16)


def call(kernel, outs, scratch, *operands):
    return pl.pallas_call(
        kernel,
        out_shape=[jax.ShapeDtypeStruct(shape, kind) for shape, kind in outs],
        in_specs=[pl.BlockSpec(memory_space=pltpu.VMEM)] * len(operands),
        out_specs=[pl.BlockSpec(memory_space=pltpu.VMEM)] * len(outs),
        scratch_shapes=[pltpu.VMEM(shape, kind) for shape, kind in scratch],
        compiler_params=pltpu.CompilerParams(vmem_limit_bytes=VMEM_LIMIT),
    )(*operands)


def exchange(value, axis, groups=None):
    return lax.all_to_all(value, axis, 0, 0, tiled=True, axis_index_groups=groups)


def shards(
    streams, short_taps, filter_in, filter_mid, filter_out, decay_rate, skip_gain, out_weight,
    grad_out,
):
    channels, tokens = streams.shape[1:]
    blocks = lax.axis_size("ctx")
    owners = lax.axis_size("ch")
    me = lax.axis_index("ctx")
    length = blocks * tokens
    share = channels // blocks
    hidden = filter_in.shape[1]
    band_rows = filter_in.shape[0]
    side = int(math.isqrt(owners))
    near = [[a * side + i for i in range(side)] for a in range(side)]
    far = [[a * side + i for a in range(side)] for i in range(side)]
    group = side * channels
    pad_rows = ROWS - share
    tables = [jnp.asarray(t) for t in transform_tables()]
    features = jnp.asarray(position_features(band_rows // 2, length))

    weight_parts = out_weight.reshape(channels, side, group).transpose(1, 0, 2)
    sent = jnp.concatenate(
        [jnp.broadcast_to(grad_out[None], (side, channels, tokens)), weight_parts], axis=2
    )
    sent = exchange(sent, "ch", far)
    cotangent = sent[:, :, :tokens].reshape(group, tokens)
    weight = sent[:, :, tokens:].reshape(group, group)
    grad_terms = lax.dot_general(
        weight, cotangent, (((0,), (0,)), ((), ())), preferred_element_type=f32
    ).astype(bf16)
    grad_terms = exchange(grad_terms.reshape(side, channels, tokens), "ch", near)
    grad_gated = jnp.sum(grad_terms.astype(f32), axis=0).astype(bf16)

    by_share = streams.reshape(3, blocks, share, tokens).transpose(1, 0, 2, 3)
    by_share = jnp.pad(by_share, ((0, 0), (0, 0), (0, pad_rows), (0, 0)))
    sequence = exchange(by_share.reshape(blocks, 3 * ROWS, tokens), "ctx")

    params = jnp.concatenate(
        [
            short_taps.transpose(1, 0, 2).reshape(channels, 9),
            decay_rate[:, None],
            skip_gain[:, None],
            filter_out.T,
        ],
        axis=1,
    )
    params = lax.dynamic_slice_in_dim(params, me * share, share, 0)
    params = jnp.pad(params, ((0, pad_rows), (0, 128 - params.shape[1])))

    wave = (hidden, length)
    hidden_one, slope_one, hidden_two, slope_two, spectra = call(
        network_kernel,
        [(wave, f32)] * 4 + [((blocks, ROWS, 2 * tokens), f32)],
        [((blocks * ROWS, tokens), f32)],
        features, filter_in, filter_mid, params, tables[0], tables[1],
    )
    gated, filtered, long_out, own_spectra = call(
        forward_kernel,
        [
            ((blocks * ROWS, tokens), bf16),
            ((blocks, 3 * ROWS, tokens), f32),
            ((blocks, ROWS, tokens), f32),
            ((blocks, ROWS, 2 * tokens), f32),
        ],
        [((blocks * ROWS, 2 * tokens), f32)],
        sequence, params, spectra, *tables,
    )

    turned = jnp.pad(grad_gated.reshape(blocks, share, tokens), ((0, 0), (0, pad_rows), (0, 0)))
    turned = jnp.concatenate([gated.reshape(blocks, ROWS, tokens), turned], axis=1)
    turned = exchange(turned, "ctx")
    own_gated = turned[:, :share, :].reshape(channels, tokens)

    grad_packed, grad_shared, grad_last = call(
        backward_kernel,
        [
            ((blocks, 6 * ROWS, tokens // 2), bf16),
            ((2 * (band_rows + hidden), hidden), bf16),
            ((2 * ROWS, hidden), bf16),
        ],
        [
            ((blocks * ROWS, 2 * tokens), f32),
            ((blocks * ROWS, 2 * tokens), f32),
            ((blocks, ROWS, 2 * tokens), f32),
        ],
        turned, params, spectra, filtered, long_out, own_spectra,
        hidden_one, slope_one, hidden_two, slope_two, features, filter_mid, *tables,
    )

    shared_rows = grad_shared.size // tokens
    sent = jnp.concatenate([own_gated, grad_shared.reshape(shared_rows, tokens)], axis=0)
    sent = exchange(
        jnp.broadcast_to(sent[None], (side,) + sent.shape), "ch", near
    )
    all_gated = sent[:, :channels].reshape(group, tokens)
    shared = jnp.sum(sent[:, channels:].astype(f32), axis=0)
    shared = shared[: shared_rows // 2] + shared[shared_rows // 2 :]

    out_terms = jnp.dot(weight, all_gated, preferred_element_type=f32).astype(bf16)
    by_block = cotangent.reshape(side, blocks, share, tokens).transpose(1, 0, 2, 3)
    weight_terms = lax.dot_general(
        by_block.reshape(group, tokens), all_gated, (((1,), (1,)), ((), ())),
        preferred_element_type=f32,
    ).astype(bf16)

    def both_halves(value):
        high = lax.reduce_precision(value, 8, 7)
        return high.astype(bf16), (value - high).astype(bf16)

    portion = (band_rows + hidden) // blocks
    high, low = both_halves(shared.reshape(blocks, portion, hidden))
    rows = side * share
    small = jnp.concatenate(
        [high, low, jnp.broadcast_to(grad_last[None], (blocks,) + grad_last.shape)], axis=1
    )
    small = jnp.pad(small, ((0, 0), (0, rows - small.shape[1]), (0, 0)))
    sent = jnp.concatenate([weight_terms.reshape(blocks, rows, group), small, grad_packed], axis=2)
    sent = exchange(sent, "ctx")
    weight_share = jnp.sum(sent[:, :, :group].astype(f32), axis=0).astype(bf16)
    small = sent[:, :, group : group + hidden].astype(f32)
    shared = jnp.sum(small[:, :portion] + small[:, portion : 2 * portion], axis=0)
    last_at = 2 * portion
    grad_last = small[:, last_at : last_at + share] + small[:, last_at + ROWS : last_at + ROWS + share]
    grad_filter_out = grad_last.reshape(channels, hidden).T
    packed = sent[:, :, group + hidden :].reshape(blocks, 2, 3, ROWS, tokens // 2)
    grad_streams = (
        packed[:, :, :, :share].transpose(2, 0, 3, 1, 4).reshape(3, channels, tokens)
    )

    high, low = both_halves(shared)
    width = 3 * tokens
    tail = jnp.concatenate([high, low], axis=0).reshape(2 * portion * hidden // tokens, tokens)
    weight_rows = jnp.pad(
        weight_share.reshape(side, share, group), ((0, 0), (0, 0), (0, width - group))
    ).reshape(side, share * 3, tokens)
    sent = jnp.concatenate(
        [
            out_terms.reshape(side, channels, tokens),
            weight_rows,
            jnp.broadcast_to(tail[None], (side,) + tail.shape),
        ],
        axis=1,
    )
    sent = exchange(sent, "ch", far)
    layer_out = jnp.sum(sent[:, :channels].astype(f32), axis=0).astype(bf16)
    weight_rows = sent[:, channels : channels + 3 * share].reshape(side, share, width)[:, :, :group]
    weight_rows = weight_rows.transpose(1, 0, 2).reshape(share, owners * channels)
    tail = jnp.sum(sent[:, channels + 3 * share :].astype(f32), axis=0)
    tail = tail.reshape(2, portion * hidden)
    high, low = both_halves(tail[0] + tail[1])

    tail = jnp.concatenate([high, low])
    spare = -tail.size % (share * 128)
    tail = jnp.pad(tail, (0, spare)).reshape(share, -1)
    sent = lax.all_gather(jnp.concatenate([weight_rows, tail], axis=1), "ctx", axis=0)
    grad_out_weight = sent[:, :, : weight_rows.shape[1]].reshape(channels, -1).astype(f32)
    tail = sent[:, :, weight_rows.shape[1] :].reshape(blocks, -1).astype(f32)
    size = portion * hidden
    shared = (tail[:, :size] + tail[:, size : 2 * size]).reshape(band_rows + hidden, hidden)
    return (
        layer_out, grad_streams, shared[:band_rows], shared[band_rows:], grad_filter_out,
        grad_out_weight,
    )


def solution(mesh):
    return jax.shard_map(
        shards,
        mesh=mesh,
        in_specs=(
            P(None, "ch", "ctx"),
            P(None, "ch", None),
            P(),
            P(),
            P(None, "ch"),
            P("ch"),
            P("ch"),
            P("ch", None),
            P("ch", "ctx"),
        ),
        out_specs=(P("ch", "ctx"), P(None, "ch", "ctx"), P(), P(), P(None, "ch"), P("ch", None)),
        check_vma=False,
    )
```

time: 1490 us -> 250 us (0.17)
  waiting for transfers between devices: 1030 us -> 89.8 us
  blocking collectives: 184 us -> 41.8 us
  matrix products: 136 us -> 2.03 us
    reduce_scatter x1 -> x0, waiting for transfers between devices: 879 us -> none  [shards(): lax.psum_scatter(jnp.einsum('dc,dt->ct', columns, grad_out, preferred_ele...]
    psum x2 -> x0, blocking collectives: 184 us -> none  [the longest x1 110 us: shards(): lax.psum((grad_filter_in, grad_filter_mid), ('ctx', 'ch'))]
    dot_general x43 -> x3, matrix products: 131 us -> 2.03 us  [the longest x1 1.2 us: shards(): lax.dot_general(weight, cotangent, (((0,), (0,)), ((), ())), preferred_el...]
    all_to_all x0 -> x6, waiting for transfers between devices: none -> 89.8 us  [exchange(): lax.all_to_all(value, axis, 0, 0, tiled=True, axis_index_groups=groups)]
    all_gather x1 -> x0, waiting for transfers between devices: 87.9 us -> none  [shards(): piece = lax.all_gather(gated_out, 'ch', axis=0, tiled=True)]
    ppermute x24 -> x0, starting transfers between devices: 81 us -> none  [passed_along(): return lax.ppermute(value, axis, pairs)]
    all_to_all x0 -> x6, starting transfers between devices: none -> 77.1 us  [exchange(): lax.all_to_all(value, axis, 0, 0, tiled=True, axis_index_groups=groups)]
    ppermute x24 -> x0, waiting for transfers between devices: 50.4 us -> none  [passed_along(): return lax.ppermute(value, axis, pairs)]
  transfers between devices with their start and end apart: 27 -> 6, of which waited for: 25 -> 5; matrix products, arithmetic and copies ran while one was open for 3% -> 2% of each run, Pallas kernels for 0% -> 2%
where the time goes in v1:
time: 250 us; the launch traced here: 249 us
  waiting for transfers between devices  89.8 us (36%)
  starting transfers between devices  77.1 us (31%)
  blocking collectives  41.8 us (17%)
  local copies, waits for them, and re-layouts  21 us (8%)
  Pallas kernels  9.6 us (4%)
  other arithmetic  6.81 us (3%)
    all_to_all x6, waiting for transfers between devices, exchange(): lax.all_to_all(value, axis, 0, 0, tiled=True, axis_index_groups=groups)  89.8 us
    all_to_all x6, starting transfers between devices, exchange(): lax.all_to_all(value, axis, 0, 0, tiled=True, axis_index_groups=groups)  77.1 us
    all_gather x1, blocking collectives, shards(): lax.all_gather(jnp.concatenate([weight_rows, tail], axis=1), 'ctx', axis=0)  28.8 us
    all_to_all x1, blocking collectives, exchange(): lax.all_to_all(value, axis, 0, 0, tiled=True, axis_index_groups=groups)  13 us
    unnamed x66, local copies, waits for them, and re-layouts  11.7 us
    pallas_call x3, Pallas kernels, call(): pl.pallas_call(kernel, out_shape=[jax.ShapeDtypeStruct(shape, kind) for s...  9.6 us
  transfers between devices with their start and end apart: 6, of which 5 were waited for; matrix products, arithmetic and copies ran while one was open for 2% of the time, Pallas kernels for 2%

profile of v1, /device:TPU:1, one launch (start us, length us, event | category | flops | bytes accessed | tf_op | source)
XLA Modules:
  0.0 249.3 jit_solution(14419588799695794436)
XLA Ops:
  0.6 1.7 reshape.101
  2.4 0.1 copy.74
  2.5 1.0 pad_maximum_fusion
  3.6 20.3 %all-to-all-start = ((bf16[8,72,832]{2,1,0:T(8,128)(2,1)}), bf16[8,72,832]{2,1,0:T(8,128)(2,1)S(1)}, u32[]{:S(2)}, u32[]{:S(2)}) async-start(bf16[8,72,832]{2,1,0:T(8,128)(2,1)} %pad_maximum_fusion), calls=%async_computation | async-start | bytes 2064384 | tf_op jit(solution)/shard_map/all_to_all | solution.py:298
  24.0 0.7 pad_bitcast_fusion
  24.7 26.0 %all-to-all-done = bf16[8,72,832]{2,1,0:T(8,128)(2,1)S(1)} async-done(((bf16[8,72,832]{2,1,0:T(8,128)(2,1)}), bf16[8,72,832]{2,1,0:T(8,128)(2,1)S(1)}, u32[]{:S(2)}, u32[]{:S(2)}) %all-to-all-start) | async-done | bytes 958496 | tf_op jit(solution)/shard_map/all_to_all | solution.py:298
  50.7 31.0 %all-to-all-start.1 = ((bf16[12,24,256]{2,1,0:T(8,128)(2,1)}), bf16[12,24,256]{2,1,0:T(8,128)(2,1)S(1)}, u32[]{:S(2)}, u32[]{:S(2)}) async-start(bf16[12,24,256]{2,1,0:T(8,128)(2,1)} %pad_bitcast_fusion), calls=%async_computation.1 | async-start | bytes 294912 | tf_op jit(solution)/shard_map/all_to_all | solution.py:298
  81.8 1.2 fusion
  83.0 9.4 %all-to-all-done.1.blocks = bf16[12,24,256]{2,1,0:T(8,128)(2,1)S(1)} async-done(((bf16[12,24,256]{2,1,0:T(8,128)(2,1)}), bf16[12,24,256]{2,1,0:T(8,128)(2,1)S(1)}, u32[]{:S(2)}, u32[]{:S(2)}) %all-to-all-start.1) | async-done | bytes 147488 | tf_op jit(solution)/shard_map/all_to_all | solution.py:298
  92.4 5.0 %all-to-all-start.2 = ((bf16[8,72,256]{2,1,0:T(8,128)(2,1)}), bf16[8,72,256]{2,1,0:T(8,128)(2,1)}, u32[]{:S(2)}, u32[]{:S(2)}) async-start(bf16[8,72,256]{2,1,0:T(8,128)(2,1)} %bitcast.10), calls=%async_computation.2 | async-start | bytes 589824 | tf_op jit(solution)/shard_map/all_to_all | solution.py:298
  97.4 0.1 copy.56
  97.5 0.1 copy.55
  97.6 0.1 copy.57
  97.7 0.1 copy.58
  97.8 0.1 fusion.16
  98.0 4.8 %shard_map.181 = (f32[64,3072]{1,0:T(8,128)S(1)}, f32[64,3072]{1,0:T(8,128)S(1)}, f32[64,3072]{1,0:T(8,128)S(1)}, f32[64,3072]{1,0:T(8,128)S(1)}, f32[12,8,512]{2,1,0:T(8,128)S(1)}) custom-call(f32[32,3072]{1,0:T(8,128)S(1)} %copy-done.2, f32[32,64]{1,0:T(8,128)S(1)} %copy-done.21, f32[64,64]{1,0:T(8,128)S(1)} %copy-done.13, f32[8,128]{1,0:T(8,128)S(1)} %pad.25.params, ...), custom_call_target="tpu_custom_call" | custom-call | tf_op jit(solution)/shard_map/pallas_call | solution.py:287
  102.8 0.9 copy-done.5
  103.7 0.9 copy-done.7
  104.6 0.8 shard_map.182
  105.4 0.7 copy-done.9
  106.1 0.6 copy-done.15
  106.8 0.6 copy-done.20
  107.4 1.0 reduce_sum.63
  108.4 0.8 fusion.7
  109.2 13.0 %all_to_all.35.blocks = bf16[12,16,256]{2,1,0:T(8,128)(2,1)S(1)} all-to-all(bf16[12,16,256]{2,1,0:T(8,128)(2,1)S(1)} %fusion.7), channel_id=1, replica_groups=mesh['ctx'=12,'ch'=64] {'ctx'}, dimensions={0} | all-to-all | bytes 196608 | tf_op jit(solution)/shard_map/all_to_all | solution.py:298
  122.2 0.6 reshape.109
  122.8 1.1 copy-done.6
  124.0 1.1 copy-done.8
  125.1 1.0 copy-done.10
  126.1 0.8 copy-done.14
  126.8 0.9 copy-done.16
  127.7 0.7 copy-done.18
  128.4 4.0 %shard_map.183 = (bf16[12,48,128]{2,1,0:T(8,128)(2,1)S(1)}, bf16[192,64]{1,0:T(8,128)(2,1)S(1)}, bf16[16,64]{1,0:T(8,128)(2,1)S(1)}) custom-call(bf16[12,16,256]{2,1,0:T(8,128)(2,1)S(1)} %all_to_all.35.blocks, f32[8,128]{1,0:T(8,128)S(1)} %copy-done.18, f32[12,8,512]{2,1,0:T(8,128)S(1)} %get-tuple-element.18.spectra, f32[12,24,256]{2,1,0:T(8,128)S(1)} %copy-done.10, ...), custom_call_target="tpu_custom_call" | custom-call | tf_op jit(solution)/shard_map/pallas_call | solution.py:287
  132.4 0.7 copy-done.11
  133.1 0.6 copy-done.19
  133.7 1.0 reshape.110
  134.7 0.8 pad_maximum_fusion.3
  135.4 0.8 broadcast_in_dim.34
  136.3 5.4 %all-to-all-start.4 = ((bf16[8,120,256]{2,1,0:T(8,128)(2,1)}), bf16[8,120,256]{2,1,0:T(8,128)(2,1)S(1)}, u32[]{:S(2)}, u32[]{:S(2)}) async-start(bf16[8,120,256]{2,1,0:T(8,128)(2,1)} %broadcast_in_dim.34), calls=%async_computation.4 | async-start | bytes 983040 | tf_op jit(solution)/shard_map/all_to_all | solution.py:298
  141.8 0.1 copy.60
  141.9 0.1 reshape.113
  142.0 7.8 %all-to-all-done.4 = bf16[8,120,256]{2,1,0:T(8,128)(2,1)S(1)} async-done(((bf16[8,120,256]{2,1,0:T(8,128)(2,1)}), bf16[8,120,256]{2,1,0:T(8,128)(2,1)S(1)}, u32[]{:S(2)}, u32[]{:S(2)}) %all-to-all-start.4) | async-done | bytes 491552 | tf_op jit(solution)/shard_map/all_to_all | solution.py:298
  149.8 0.1 reshape.115
  149.9 0.4 convolution_convert_fusion
  150.4 1.1 pad_maximum_fusion.1
  151.5 5.7 %all-to-all-start.5 = ((bf16[12,48,768]{2,1,0:T(8,128)(2,1)}), bf16[12,48,768]{2,1,0:T(8,128)(2,1)S(1)}, u32[]{:S(2)}, u32[]{:S(2)}) async-start(bf16[12,48,768]{2,1,0:T(8,128)(2,1)} %pad_maximum_fusion.1), calls=%async_computation.5 | async-start | bytes 1769472 | tf_op jit(solution)/shard_map/all_to_all | solution.py:298
  157.2 0.4 convolution_convert_fusion.1
  157.6 32.3 %all-to-all-done.5 = bf16[12,48,768]{2,1,0:T(8,128)(2,1)S(1)} async-done(((bf16[12,48,768]{2,1,0:T(8,128)(2,1)}), bf16[12,48,768]{2,1,0:T(8,128)(2,1)S(1)}, u32[]{:S(2)}, u32[]{:S(2)}) %all-to-all-start.5) | async-done | bytes 884768 | tf_op jit(solution)/shard_map/all_to_all | solution.py:298
  189.9 0.1 slice_reduce_fusion
  190.1 0.1 slice_convert_fusion.1
  190.2 0.1 broadcast_in_dim.36
  190.3 0.8 pad_maximum_fusion.2
  191.1 9.6 %all-to-all-start.6 = ((bf16[8,94,256]{2,1,0:T(8,128)(2,1)}), bf16[8,94,256]{2,1,0:T(8,128)(2,1)S(1)}, u32[]{:S(2)}, u32[]{:S(2)}) async-start(bf16[8,94,256]{2,1,0:T(8,128)(2,1)} %pad_maximum_fusion.2), calls=%async_computation.6 | async-start | bytes 786432 | tf_op jit(solution)/shard_map/all_to_all | solution.py:298
  200.7 0.1 copy.76
  200.8 0.7 reshape.119
  201.6 0.7 copy.65
  202.3 14.3 %all-to-all-done.6 = bf16[8,94,256]{2,1,0:T(8,128)(2,1)S(1)} async-done(((bf16[8,94,256]{2,1,0:T(8,128)(2,1)}), bf16[8,94,256]{2,1,0:T(8,128)(2,1)S(1)}, u32[]{:S(2)}, u32[]{:S(2)}) %all-to-all-start.6) | async-done | bytes 385056 | tf_op jit(solution)/shard_map/all_to_all | solution.py:298
  216.8 0.1 reshape.121
  216.9 28.8 %all-gather.1 = bf16[12,6,4864]{2,1,0:T(8,128)(2,1)S(1)} all-gather(bf16[1,6,4864]{2,1,0:T(8,128)(2,1)S(1)} %maximum_bitcast_fusion), channel_id=2, replica_groups=mesh['ctx'=12,'ch'=64] {'ctx'}, dimensions={0}, use_global_device_ids=true | all-gather | bytes 758784 | tf_op jit(solution)/shard_map/all_gather | solution.py:455
  245.8 0.1 slice_convert_fusion
  246.0 0.7 slice.112
  246.7 0.7 slice.114
  247.4 1.3 reshape.125
  248.6 0.7 slice_reduce_fusion.1
  (91 shorter events, 0.7 us)
Async XLA Ops:
  0.6 1.8 copy-start.24
  2.5 21.4 %copy-start.23 = (bf16[3,72,256]{2,1,0:T(8,128)(2,1)S(1)}, bf16[3,72,256]{2,1,0:T(8,128)(2,1)}, u32[]{:S(2)}) copy-start(bf16[3,72,256]{2,1,0:T(8,128)(2,1)} %param.14) | copy-start | bytes 331780
  3.6 47.1 %all-to-all-start = ((bf16[8,72,832]{2,1,0:T(8,128)(2,1)}), bf16[8,72,832]{2,1,0:T(8,128)(2,1)S(1)}, u32[]{:S(2)}, u32[]{:S(2)}) async-start(bf16[8,72,832]{2,1,0:T(8,128)(2,1)} %pad_maximum_fusion), calls=%async_computation | async-start | bytes 2064384 | tf_op jit(solution)/shard_map/all_to_all | solution.py:298
  24.6 72.8 %copy-start.26 = (f32[3,72,3]{1,2,0:T(4,128)S(1)}, f32[3,72,3]{1,2,0:T(4,128)}, u32[]{:S(2)}) copy-start(f32[3,72,3]{1,2,0:T(4,128)} %param.15) | copy-start | bytes 7780
  24.6 72.9 %copy-start.25 = (f32[64,72]{1,0:T(8,128)S(1)}, f32[64,72]{1,0:T(8,128)}, u32[]{:S(2)}) copy-start(f32[64,72]{1,0:T(8,128)} %param.18) | copy-start | bytes 55300
  24.6 73.0 %copy-start.27 = (f32[72]{0:T(128)S(1)}, f32[72]{0:T(128)}, u32[]{:S(2)}) copy-start(f32[72]{0:T(128)} %param.19) | copy-start | bytes 868
  24.6 73.1 %copy-start.28 = (f32[72]{0:T(128)S(1)}, f32[72]{0:T(128)}, u32[]{:S(2)}) copy-start(f32[72]{0:T(128)} %param.20) | copy-start | bytes 868
  50.7 47.2 %copy-start.22 = (bf16[8,72,832]{2,1,0:T(8,128)(2,1)}, bf16[8,72,832]{2,1,0:T(8,128)(2,1)S(1)}, u32[]{:S(2)}) copy-start(bf16[8,72,832]{2,1,0:T(8,128)(2,1)S(1)} %all-to-all-done) | copy-start | bytes 2875396
  50.7 41.7 %all-to-all-start.1 = ((bf16[12,24,256]{2,1,0:T(8,128)(2,1)}), bf16[12,24,256]{2,1,0:T(8,128)(2,1)S(1)}, u32[]{:S(2)}, u32[]{:S(2)}) async-start(bf16[12,24,256]{2,1,0:T(8,128)(2,1)} %pad_bitcast_fusion), calls=%async_computation.1 | async-start | bytes 294912 | tf_op jit(solution)/shard_map/all_to_all | solution.py:298
  81.7 16.2 %copy-start = (bf16[256,512]{1,0:T(8,128)(2,1)S(1)}, bf16[256,512]{1,0:T(8,128)(2,1)}, u32[]{:S(2)}) copy-start(bf16[256,512]{1,0:T(8,128)(2,1)} %constant.30.clone.table_low) | copy-start | bytes 786436
  81.7 16.2 %copy-start.1 = (bf16[256,512]{1,0:T(8,128)(2,1)S(1)}, bf16[256,512]{1,0:T(8,128)(2,1)}, u32[]{:S(2)}) copy-start(bf16[256,512]{1,0:T(8,128)(2,1)} %constant.29.clone.table_high) | copy-start | bytes 786436
  81.7 16.2 %copy-start.2 = (f32[32,3072]{1,0:T(8,128)S(1)}, f32[32,3072]{1,0:T(8,128)}, u32[]{:S(2)}) copy-start(f32[32,3072]{1,0:T(8,128)} %constant.33.clone.features) | copy-start | bytes 1179652
  81.7 16.2 %copy-start.13 = (f32[64,64]{1,0:T(8,128)S(1)}, f32[64,64]{1,0:T(8,128)}, u32[]{:S(2)}) copy-start(f32[64,64]{1,0:T(8,128)} %filter_mid.3) | copy-start | bytes 49156
  81.7 16.2 %copy-start.21 = (f32[32,64]{1,0:T(8,128)S(1)}, f32[32,64]{1,0:T(8,128)}, u32[]{:S(2)}) copy-start(f32[32,64]{1,0:T(8,128)} %filter_in.1) | copy-start | bytes 24580
  81.7 22.9 %copy-start.3 = (bf16[512,256]{1,0:T(8,128)(2,1)S(1)}, bf16[512,256]{1,0:T(8,128)(2,1)}, u32[]{:S(2)}) copy-start(bf16[512,256]{1,0:T(8,128)(2,1)} %constant.32.clone.back_low) | copy-start | bytes 786436
  81.8 22.9 %copy-start.4 = (bf16[512,256]{1,0:T(8,128)(2,1)S(1)}, bf16[512,256]{1,0:T(8,128)(2,1)}, u32[]{:S(2)}) copy-start(bf16[512,256]{1,0:T(8,128)(2,1)} %constant.31.clone.back_high) | copy-start | bytes 786436
  92.4 15.0 %all-to-all-start.2 = ((bf16[8,72,256]{2,1,0:T(8,128)(2,1)}), bf16[8,72,256]{2,1,0:T(8,128)(2,1)}, u32[]{:S(2)}, u32[]{:S(2)}) async-start(bf16[8,72,256]{2,1,0:T(8,128)(2,1)} %bitcast.10), calls=%async_computation.2 | async-start | bytes 589824 | tf_op jit(solution)/shard_map/all_to_all | solution.py:298
  98.0 6.6 %copy-start.17 = (f32[8,128]{1,0:T(8,128)}, f32[8,128]{1,0:T(8,128)S(1)}, u32[]{:S(2)}) copy-start(f32[8,128]{1,0:T(8,128)S(1)} %pad.25.params) | copy-start | bytes 12292
  102.8 0.9 copy-start.5
  103.7 0.9 copy-start.7
  105.4 0.7 copy-start.9
  106.1 0.6 copy-start.15
  106.8 0.6 copy-start.20
  122.8 1.1 copy-start.6
  124.0 1.1 copy-start.8
  125.1 1.0 copy-start.10
  126.1 0.8 copy-start.14
  126.8 0.9 copy-start.16
  127.7 0.7 copy-start.18
  132.4 0.7 copy-start.11
  133.1 0.6 copy-start.19
  133.7 8.0 %slice-start = ((bf16[8,72,832]{2,1,0:T(8,128)(2,1)}), bf16[8,72,256]{2,1,0:T(8,128)(2,1)S(1)}, s32[]{:S(2)}) async-start(bf16[8,72,832]{2,1,0:T(8,128)(2,1)} %copy-done.22), calls=%async_computation.7 | async-start | bytes 589824 | tf_op jit(solution)/shard_map/slice | solution.py:326
  136.3 13.5 %all-to-all-start.4 = ((bf16[8,120,256]{2,1,0:T(8,128)(2,1)}), bf16[8,120,256]{2,1,0:T(8,128)(2,1)S(1)}, u32[]{:S(2)}, u32[]{:S(2)}) async-start(bf16[8,120,256]{2,1,0:T(8,128)(2,1)} %broadcast_in_dim.34), calls=%async_computation.4 | async-start | bytes 983040 | tf_op jit(solution)/shard_map/all_to_all | solution.py:298
  141.8 8.5 %copy-start.12 = (bf16[12,48,128]{2,1,0:T(8,128)(2,1)S(1)}, bf16[12,48,128]{2,1,0:T(8,128)(2,1)}, u32[]{:S(2)}) copy-start(bf16[12,48,128]{2,1,0:T(8,128)(2,1)} %copy-done.11) | copy-start | bytes 442372
  151.5 5.7 %slice-start.1 = ((bf16[8,72,832]{2,1,0:T(8,128)(2,1)}), bf16[8,72,576]{2,1,0:T(8,128)(2,1)S(1)}, s32[]{:S(2)}) async-start(bf16[8,72,832]{2,1,0:T(8,128)(2,1)} %copy-done.22), calls=%async_computation.8 | async-start | bytes 1474560 | tf_op jit(solution)/shard_map/slice | solution.py:327
  151.5 38.4 %all-to-all-start.5 = ((bf16[12,48,768]{2,1,0:T(8,128)(2,1)}), bf16[12,48,768]{2,1,0:T(8,128)(2,1)S(1)}, u32[]{:S(2)}, u32[]{:S(2)}) async-start(bf16[12,48,768]{2,1,0:T(8,128)(2,1)} %pad_maximum_fusion.1), calls=%async_computation.5 | async-start | bytes 1769472 | tf_op jit(solution)/shard_map/all_to_all | solution.py:298
  191.1 25.5 %all-to-all-start.6 = ((bf16[8,94,256]{2,1,0:T(8,128)(2,1)}), bf16[8,94,256]{2,1,0:T(8,128)(2,1)S(1)}, u32[]{:S(2)}, u32[]{:S(2)}) async-start(bf16[8,94,256]{2,1,0:T(8,128)(2,1)} %pad_maximum_fusion.2), calls=%async_computation.6 | async-start | bytes 786432 | tf_op jit(solution)/shard_map/all_to_all | solution.py:298

commit v2 on v1

--- a/solution.py
+++ b/solution.py
@@ -14,7 +14,7 @@
 
 BLOCK = 256
 ROWS = 8
-VMEM_LIMIT = 40 * 1024 * 1024
+VMEM_LIMIT = 16 * 1024 * 1024
 
 
 def split_table(table):
@@ -108,9 +108,25 @@
 DECAY, SKIP, OUT = 9, 10, 11
 
 
+def start_copies(pairs, semaphores):
+    copies = [
+        pltpu.make_async_copy(source, target, semaphores.at[i])
+        for i, (source, target) in enumerate(pairs)
+    ]
+    for copy in copies:
+        copy.start()
+    return copies
+
+
+def wait_copies(copies):
+    for copy in copies:
+        copy.wait()
+
+
 def network_kernel(
     features, filter_in, filter_mid, params, table_high, table_low,
-    hidden_one, slope_one, hidden_two, slope_two, spectra, taps_scratch,
+    kept_one, kept_slope_one, kept_two, kept_slope_two, kept_spectra,
+    hidden_one, slope_one, hidden_two, slope_two, spectra, taps_scratch, semaphores,
 ):
     count = features.shape[1] // BLOCK
     hidden = filter_in.shape[1]
@@ -128,6 +144,15 @@
         slope_two[:, at] = cosine
         raw = close_dot(last, sine)
         taps_scratch[block * ROWS : (block + 1) * ROWS, :] = raw * envelope(decay, block)
+    copies = start_copies(
+        [
+            (hidden_one, kept_one),
+            (slope_one, kept_slope_one),
+            (hidden_two, kept_two),
+            (slope_two, kept_slope_two),
+        ],
+        semaphores,
+    )
     spectrum = table_dot(taps_scratch[...], table_high[...], table_low[...])
     sign = parity()
     for block in range(count):
@@ -139,6 +164,9 @@
             imag = imag + sign * spectrum[before, :BLOCK]
         spectra[block, :, :BLOCK] = real
         spectra[block, :, BLOCK:] = imag
+    last_copy = pltpu.make_async_copy(spectra, kept_spectra, semaphores.at[4])
+    last_copy.start()
+    wait_copies(copies + [last_copy])
 
 
 def rows_of(value, rows):
@@ -147,7 +175,8 @@
 
 def forward_kernel(
     blocks, params, spectra, table_high, table_low, back_high, back_low,
-    gated, filtered, long_out, own_spectra, sums,
+    kept_gated, kept_filtered, kept_long_out, kept_spectra,
+    gated, filtered, long_out, own_spectra, sums, semaphores,
 ):
     count = blocks.shape[0]
     wide = 3 * ROWS
@@ -190,18 +219,45 @@
     result = rows_of(conv, ROWS) + skip * rows_of(product, ROWS)
     long_out[...] = result
     gated[...] = (streams[0] * result).reshape(count * ROWS, BLOCK).astype(bf16)
+    wait_copies(
+        start_copies(
+            [
+                (gated, kept_gated),
+                (filtered, kept_filtered),
+                (long_out, kept_long_out),
+                (own_spectra, kept_spectra),
+            ],
+            semaphores,
+        )
+    )
 
 
 def backward_kernel(
-    blocks, params, spectra, filtered, long_out, own_spectra,
-    hidden_one, slope_one, hidden_two, slope_two, features, filter_mid,
-    table_high, table_low, back_high, back_low,
-    grad_streams, grad_shared, grad_last, sums, lag_sums, grad_spectra,
+    kept_spectra, kept_filtered, kept_long_out, kept_own_spectra,
+    kept_one, kept_slope_one, kept_two, kept_slope_two,
+    blocks, params, features, filter_mid, table_high, table_low, back_high, back_low,
+    kept_grad_streams, grad_shared, grad_last,
+    spectra, filtered, long_out, own_spectra, hidden_one, slope_one, hidden_two, slope_two,
+    grad_streams, sums, lag_sums, grad_spectra, semaphores,
 ):
+    copies = start_copies(
+        [
+            (kept_filtered, filtered),
+            (kept_spectra, spectra),
+            (kept_own_spectra, own_spectra),
+            (kept_long_out, long_out),
+            (kept_two, hidden_two),
+            (kept_slope_two, slope_two),
+            (kept_one, hidden_one),
+            (kept_slope_one, slope_one),
+        ],
+        semaphores,
+    )
     count = blocks.shape[0]
     hidden = filter_mid.shape[0]
     wide = 3 * ROWS
     grad_gated = blocks[...].astype(f32)[:, ROWS : 2 * ROWS, :]
+    wait_copies(copies[:4])
     query = filtered[:, :ROWS, :]
     grad_long = (grad_gated * query).reshape(count * ROWS, BLOCK).astype(bf16)
     spectrum = table_dot(grad_long, table_high[...], table_low[...])
@@ -258,6 +314,9 @@
     half = BLOCK // 2
     packed = [part[:, :, :half] for part in adjoint] + [part[:, :, half:] for part in adjoint]
     grad_streams[...] = jnp.concatenate(packed, axis=1).astype(bf16)
+    streams_copy = pltpu.make_async_copy(grad_streams, kept_grad_streams, semaphores.at[8])
+    streams_copy.start()
+    wait_copies(copies[4:])
 
     lags = table_dot(lag_sums[...], back_high[...], back_low[...])
     decay = params[:, DECAY : DECAY + 1]
@@ -277,21 +336,48 @@
         total_mid = total_mid + close_dot(hidden_one[:, at], grad_two, across)
         grad_one = close_dot(filter_mid[...], grad_two) * slope_one[:, at]
         total_in = total_in + close_dot(features[:, at], grad_one, across)
-    high, low = halves(jnp.concatenate([total_in, total_mid], axis=0))
-    grad_shared[...] = jnp.concatenate([high, low], axis=0)
+    grad_shared[...] = jnp.concatenate([total_in, total_mid], axis=0).astype(bf16)
     high, low = halves(total_last)
     grad_last[...] = jnp.concatenate([high.astype(f32), low.astype(f32)], axis=0).astype(bf16)
-
-
-def call(kernel, outs, scratch, *operands):
+    streams_copy.wait()
+
+
+def pack_kernel(far_weight, far_cotangent, packed, weight, cotangent, semaphores):
+    wait_copies(
+        start_copies([(far_weight, weight), (far_cotangent, cotangent)], semaphores)
+    )
+    side = packed.shape[0]
+    channels, tokens = cotangent.shape
+    for i in range(side):
+        packed[i, :, :tokens] = cotangent[...]
+        pieces = [
+            weight[:, (a * side + i) * channels : (a * side + i + 1) * channels]
+            for a in range(side)
+        ]
+        packed[i, :, tokens:] = jnp.concatenate(pieces, axis=1)
+
+
+NEAR, FAR = pltpu.VMEM, pltpu.HBM
+
+
+def call(kernel, outs, scratch, copies, *operands):
+    semaphores = [pltpu.SemaphoreType.DMA((copies,))] if copies else []
     return pl.pallas_call(
         kernel,
-        out_shape=[jax.ShapeDtypeStruct(shape, kind) for shape, kind in outs],
-        in_specs=[pl.BlockSpec(memory_space=pltpu.VMEM)] * len(operands),
-        out_specs=[pl.BlockSpec(memory_space=pltpu.VMEM)] * len(outs),
-        scratch_shapes=[pltpu.VMEM(shape, kind) for shape, kind in scratch],
+        out_shape=[
+            pltpu.HBM(shape, kind) if place is FAR else jax.ShapeDtypeStruct(shape, kind)
+            for place, shape, kind in outs
+        ],
+        in_specs=[pl.BlockSpec(memory_space=place) for place, _ in operands],
+        out_specs=[pl.BlockSpec(memory_space=place) for place, _, _ in outs],
+        scratch_shapes=[pltpu.VMEM(shape, kind) for shape, kind in scratch] + semaphores,
         compiler_params=pltpu.CompilerParams(vmem_limit_bytes=VMEM_LIMIT),
-    )(*operands)
+    )(
+        *[
+            pltpu.with_memory_space_constraint(operand, FAR) if place is FAR else operand
+            for place, operand in operands
+        ]
+    )
 
 
 def exchange(value, axis, groups=None):
@@ -311,24 +397,27 @@
     hidden = filter_in.shape[1]
     band_rows = filter_in.shape[0]
     side = int(math.isqrt(owners))
-    near = [[a * side + i for i in range(side)] for a in range(side)]
-    far = [[a * side + i for a in range(side)] for i in range(side)]
+    near_groups = [[a * side + i for i in range(side)] for a in range(side)]
+    far_groups = [[a * side + i for a in range(side)] for i in range(side)]
     group = side * channels
     pad_rows = ROWS - share
     tables = [jnp.asarray(t) for t in transform_tables()]
     features = jnp.asarray(position_features(band_rows // 2, length))
 
-    weight_parts = out_weight.reshape(channels, side, group).transpose(1, 0, 2)
-    sent = jnp.concatenate(
-        [jnp.broadcast_to(grad_out[None], (side, channels, tokens)), weight_parts], axis=2
-    )
-    sent = exchange(sent, "ch", far)
+    (sent,) = call(
+        pack_kernel,
+        [(NEAR, (side, channels, tokens + group), bf16)],
+        [(out_weight.shape, bf16), (grad_out.shape, bf16)],
+        2,
+        (FAR, out_weight), (FAR, grad_out),
+    )
+    sent = exchange(sent, "ch", near_groups)
     cotangent = sent[:, :, :tokens].reshape(group, tokens)
     weight = sent[:, :, tokens:].reshape(group, group)
     grad_terms = lax.dot_general(
         weight, cotangent, (((0,), (0,)), ((), ())), preferred_element_type=f32
     ).astype(bf16)
-    grad_terms = exchange(grad_terms.reshape(side, channels, tokens), "ch", near)
+    grad_terms = exchange(grad_terms.reshape(side, channels, tokens), "ch", far_groups)
     grad_gated = jnp.sum(grad_terms.astype(f32), axis=0).astype(bf16)
 
     by_share = streams.reshape(3, blocks, share, tokens).transpose(1, 0, 2, 3)
@@ -347,23 +436,28 @@
     params = lax.dynamic_slice_in_dim(params, me * share, share, 0)
     params = jnp.pad(params, ((0, pad_rows), (0, 128 - params.shape[1])))
 
-    wave = (hidden, length)
-    hidden_one, slope_one, hidden_two, slope_two, spectra = call(
-        network_kernel,
-        [(wave, f32)] * 4 + [((blocks, ROWS, 2 * tokens), f32)],
-        [((blocks * ROWS, tokens), f32)],
-        features, filter_in, filter_mid, params, tables[0], tables[1],
-    )
+    def near(*values):
+        return [(NEAR, value) for value in values]
+
+    def far_like(shapes):
+        return [(FAR,) + shape for shape in shapes]
+
+    wave = ((hidden, length), f32)
+    spectrum = ((blocks, ROWS, 2 * tokens), f32)
+    kept_waves = [wave] * 4 + [spectrum]
+    *waves, spectra = call(
+        network_kernel, far_like(kept_waves), kept_waves + [((blocks * ROWS, tokens), f32)], 5,
+        *near(features, filter_in, filter_mid, params, tables[0], tables[1]),
+    )
+    kept = [
+        ((blocks * ROWS, tokens), bf16),
+        ((blocks, 3 * ROWS, tokens), f32),
+        ((blocks, ROWS, tokens), f32),
+        spectrum,
+    ]
     gated, filtered, long_out, own_spectra = call(
-        forward_kernel,
-        [
-            ((blocks * ROWS, tokens), bf16),
-            ((blocks, 3 * ROWS, tokens), f32),
-            ((blocks, ROWS, tokens), f32),
-            ((blocks, ROWS, 2 * tokens), f32),
-        ],
-        [((blocks * ROWS, 2 * tokens), f32)],
-        sequence, params, spectra, *tables,
+        forward_kernel, far_like(kept), kept + [((blocks * ROWS, 2 * tokens), f32)], 4,
+        *near(sequence, params, spectra, *tables),
     )
 
     turned = jnp.pad(grad_gated.reshape(blocks, share, tokens), ((0, 0), (0, pad_rows), (0, 0)))
@@ -371,60 +465,94 @@
     turned = exchange(turned, "ctx")
     own_gated = turned[:, :share, :].reshape(channels, tokens)
 
+    packed_streams = ((blocks, 6 * ROWS, tokens // 2), bf16)
     grad_packed, grad_shared, grad_last = call(
         backward_kernel,
         [
-            ((blocks, 6 * ROWS, tokens // 2), bf16),
-            ((2 * (band_rows + hidden), hidden), bf16),
-            ((2 * ROWS, hidden), bf16),
+            (FAR,) + packed_streams,
+            (NEAR, (band_rows + hidden, hidden), bf16),
+            (NEAR, (2 * ROWS, hidden), bf16),
         ],
-        [
-            ((blocks * ROWS, 2 * tokens), f32),
-            ((blocks * ROWS, 2 * tokens), f32),
-            ((blocks, ROWS, 2 * tokens), f32),
-        ],
-        turned, params, spectra, filtered, long_out, own_spectra,
-        hidden_one, slope_one, hidden_two, slope_two, features, filter_mid, *tables,
+        [spectrum, kept[1], kept[2], spectrum]
+        + [wave] * 4
+        + [packed_streams]
+        + [((blocks * ROWS, 2 * tokens), f32)] * 2
+        + [spectrum],
+        9,
+        *[(FAR, value) for value in (spectra, filtered, long_out, own_spectra, *waves)],
+        *near(turned, params, features, filter_mid, *tables),
     )
 
     shared_rows = grad_shared.size // tokens
     sent = jnp.concatenate([own_gated, grad_shared.reshape(shared_rows, tokens)], axis=0)
     sent = exchange(
-        jnp.broadcast_to(sent[None], (side,) + sent.shape), "ch", near
+        jnp.broadcast_to(sent[None], (side,) + sent.shape), "ch", far_groups
     )
     all_gated = sent[:, :channels].reshape(group, tokens)
     shared = jnp.sum(sent[:, channels:].astype(f32), axis=0)
-    shared = shared[: shared_rows // 2] + shared[shared_rows // 2 :]
 
     out_terms = jnp.dot(weight, all_gated, preferred_element_type=f32).astype(bf16)
-    by_block = cotangent.reshape(side, blocks, share, tokens).transpose(1, 0, 2, 3)
-    weight_terms = lax.dot_general(
-        by_block.reshape(group, tokens), all_gated, (((1,), (1,)), ((), ())),
-        preferred_element_type=f32,
-    ).astype(bf16)
-
     def both_halves(value):
         high = lax.reduce_precision(value, 8, 7)
         return high.astype(bf16), (value - high).astype(bf16)
 
+    chips = blocks // 2
+    core = me % 2
+    rows = side * share
     portion = (band_rows + hidden) // blocks
-    high, low = both_halves(shared.reshape(blocks, portion, hidden))
-    rows = side * share
-    small = jnp.concatenate(
-        [high, low, jnp.broadcast_to(grad_last[None], (blocks,) + grad_last.shape)], axis=1
-    )
-    small = jnp.pad(small, ((0, 0), (0, rows - small.shape[1]), (0, 0)))
-    sent = jnp.concatenate([weight_terms.reshape(blocks, rows, group), small, grad_packed], axis=2)
-    sent = exchange(sent, "ctx")
+    by_core = cotangent.reshape(side, chips, 2, share, tokens).transpose(2, 1, 0, 3, 4)
+    shared = shared.reshape(chips, 2, portion, hidden)
+    grad_packed = grad_packed.reshape((chips, 2) + grad_packed.shape[1:])
+
+    def parts_for(which):
+        left = lax.dynamic_index_in_dim(by_core, which, 0, False).reshape(chips * rows, tokens)
+        terms = lax.dot_general(
+            left, all_gated, (((1,), (1,)), ((), ())), preferred_element_type=f32
+        ).reshape(chips, rows, group)
+        return (
+            terms,
+            lax.dynamic_index_in_dim(shared, which, 1, False),
+            lax.dynamic_index_in_dim(grad_packed, which, 1, False),
+        )
+
+    def joined(terms, shared, lasts, packed):
+        high, low = both_halves(shared)
+        small = jnp.concatenate([high, low] + lasts, axis=1)
+        small = jnp.pad(small, ((0, 0), (0, rows - small.shape[1]), (0, 0)))
+        return jnp.concatenate([terms.astype(bf16), small] + packed, axis=2)
+
+    last_here = jnp.broadcast_to(grad_last[None], (chips,) + grad_last.shape)
+    terms, shared_part, packed = parts_for(1 - core)
+    sent = joined(terms, shared_part, [last_here], [packed])
+    sent = lax.ppermute(sent, "ctx", [(k, k ^ 1) for k in range(blocks)])
+    terms, shared_part, packed = parts_for(core)
+    terms = terms + sent[:, :, :group].astype(f32)
+    small = sent[:, :, group : group + hidden]
+    shared_part = (
+        shared_part
+        + small[:, :portion].astype(f32)
+        + small[:, portion : 2 * portion].astype(f32)
+    )
+    last_at = 2 * portion
+    last_there = small[:, last_at : last_at + 2 * ROWS]
+    packed_there = sent[:, :, group + hidden :]
+    second = core == 1
+
+    def in_order(here, there):
+        return [jnp.where(second, there, here), jnp.where(second, here, there)]
+
+    sent = joined(
+        terms, shared_part, in_order(last_here, last_there), in_order(packed, packed_there)
+    )
+    sent = exchange(sent, "ctx", [[2 * z + c for z in range(chips)] for c in range(2)])
     weight_share = jnp.sum(sent[:, :, :group].astype(f32), axis=0).astype(bf16)
     small = sent[:, :, group : group + hidden].astype(f32)
     shared = jnp.sum(small[:, :portion] + small[:, portion : 2 * portion], axis=0)
-    last_at = 2 * portion
-    grad_last = small[:, last_at : last_at + share] + small[:, last_at + ROWS : last_at + ROWS + share]
-    grad_filter_out = grad_last.reshape(channels, hidden).T
-    packed = sent[:, :, group + hidden :].reshape(blocks, 2, 3, ROWS, tokens // 2)
+    lasts = small[:, last_at : last_at + 4 * ROWS].reshape(blocks, 2, ROWS, hidden)[:, :, :share]
+    grad_filter_out = jnp.sum(lasts, axis=1).reshape(channels, hidden).T
+    packed = sent[:, :, group + hidden :].reshape(chips, 2, 3, ROWS, 2, tokens // 2)
     grad_streams = (
-        packed[:, :, :, :share].transpose(2, 0, 3, 1, 4).reshape(3, channels, tokens)
+        packed[:, :, :, :share].transpose(2, 0, 4, 3, 1, 5).reshape(3, channels, tokens)
     )
 
     high, low = both_halves(shared)
@@ -441,10 +569,11 @@
         ],
         axis=1,
     )
-    sent = exchange(sent, "ch", far)
+    sent = exchange(sent, "ch", near_groups)
     layer_out = jnp.sum(sent[:, :channels].astype(f32), axis=0).astype(bf16)
     weight_rows = sent[:, channels : channels + 3 * share].reshape(side, share, width)[:, :, :group]
-    weight_rows = weight_rows.transpose(1, 0, 2).reshape(share, owners * channels)
+    weight_rows = weight_rows.reshape(side, share, side, channels).transpose(1, 2, 0, 3)
+    weight_rows = weight_rows.reshape(share, owners * channels)
     tail = jnp.sum(sent[:, channels + 3 * share :].astype(f32), axis=0)
     tail = tail.reshape(2, portion * hidden)
     high, low = both_halves(tail[0] + tail[1])

time: 250 us -> 202 us (0.81)
  waiting for transfers between devices: 89.8 us -> 66.4 us
  starting transfers between devices: 77.1 us -> 58 us
  local copies, waits for them, and re-layouts: 21 us -> 8.27 us
  Pallas kernels: 9.6 us -> 16.3 us
  blocking collectives: 41.8 us -> 44.4 us
    all_to_all x6, waiting for transfers between devices: 89.8 us -> 64.9 us  [exchange(): lax.all_to_all(value, axis, 0, 0, tiled=True, axis_index_groups=groups)]
    all_to_all x6, starting transfers between devices: 77.1 us -> 52.3 us  [exchange(): lax.all_to_all(value, axis, 0, 0, tiled=True, axis_index_groups=groups)]
    unnamed x66 -> x35, local copies, waits for them, and re-layouts: 11.7 us -> 1.84 us
    pallas_call x3 -> x4, Pallas kernels: 9.6 us -> 16.3 us  [call(): pl.pallas_call(kernel, out_shape=[pltpu.HBM(shape, kind) if place is FAR...]
    ppermute x0 -> x1, starting transfers between devices: none -> 5.75 us  [shards(): sent = lax.ppermute(sent, 'ctx', [(k, k ^ 1) for k in range(blocks)])]
    all_to_all x1, blocking collectives: 13 us -> 18 us  [exchange(): lax.all_to_all(value, axis, 0, 0, tiled=True, axis_index_groups=groups)]
  transfers between devices with their start and end apart: 6 -> 7, of which waited for: 5 -> 7; matrix products, arithmetic and copies ran while one was open for 2% -> 2% of each run, Pallas kernels for 2% -> 4%
where the time goes in v2:
time: 202 us
  waiting for transfers between devices  66.4 us (33%)
  starting transfers between devices  58 us (29%)
  blocking collectives  44.4 us (22%)
  Pallas kernels  16.3 us (8%)
  local copies, waits for them, and re-layouts  8.27 us (4%)
  other arithmetic  4.78 us (2%)
  matrix products  2.21 us (1%)
    all_to_all x6, waiting for transfers between devices, exchange(): lax.all_to_all(value, axis, 0, 0, tiled=True, axis_index_groups=groups)  64.9 us
    all_to_all x6, starting transfers between devices, exchange(): lax.all_to_all(value, axis, 0, 0, tiled=True, axis_index_groups=groups)  52.3 us
    all_gather x1, blocking collectives, shards(): lax.all_gather(jnp.concatenate([weight_rows, tail], axis=1), 'ctx', axis=0)  26.4 us
    all_to_all x1, blocking collectives, exchange(): lax.all_to_all(value, axis, 0, 0, tiled=True, axis_index_groups=groups)  18 us
    pallas_call x4, Pallas kernels, call(): pl.pallas_call(kernel, out_shape=[pltpu.HBM(shape, kind) if place is FAR...  16.3 us
    ppermute x1, starting transfers between devices, shards(): sent = lax.ppermute(sent, 'ctx', [(k, k ^ 1) for k in range(blocks)])  5.75 us
  transfers between devices with their start and end apart: 7, of which 7 were waited for; matrix products, arithmetic and copies ran while one was open for 2% of the time, Pallas kernels for 4%

profile of v2, /device:TPU:1, one launch (start us, length us, event | category | flops | bytes accessed | tf_op | source)
XLA Modules:
  0.0 201.7 jit_solution(13003273498003639116)
XLA Ops:
  0.6 2.7 %shard_map.181 = bf16[8,72,832]{2,1,0:T(8,128)(2,1)} custom-call(bf16[72,4608]{1,0:T(8,128)(2,1)} %far_weight.1, bf16[72,256]{1,0:T(8,128)(2,1)} %far_cotangent.1), custom_call_target="tpu_custom_call" | custom-call | tf_op jit(solution)/shard_map/pallas_call | solution.py:365
  3.3 5.9 %all-to-all-start = ((bf16[8,72,832]{2,1,0:T(8,128)(2,1)}), bf16[8,72,832]{2,1,0:T(8,128)(2,1)S(1)}, u32[]{:S(2)}, u32[]{:S(2)}) async-start(bf16[8,72,832]{2,1,0:T(8,128)(2,1)} %shard_map.181), calls=%async_computation | async-start | bytes 2064384 | tf_op jit(solution)/shard_map/all_to_all | solution.py:384
  9.3 0.7 pad_bitcast_fusion
  10.0 8.6 %all-to-all-done = bf16[8,72,832]{2,1,0:T(8,128)(2,1)S(1)} async-done(((bf16[8,72,832]{2,1,0:T(8,128)(2,1)}), bf16[8,72,832]{2,1,0:T(8,128)(2,1)S(1)}, u32[]{:S(2)}, u32[]{:S(2)}) %all-to-all-start) | async-done | bytes 958496 | tf_op jit(solution)/shard_map/all_to_all | solution.py:384
  18.5 18.3 %all-to-all-start.1 = ((bf16[12,24,256]{2,1,0:T(8,128)(2,1)}), bf16[12,24,256]{2,1,0:T(8,128)(2,1)S(1)}, u32[]{:S(2)}, u32[]{:S(2)}) async-start(bf16[12,24,256]{2,1,0:T(8,128)(2,1)} %pad_bitcast_fusion), calls=%async_computation.1 | async-start | bytes 294912 | tf_op jit(solution)/shard_map/all_to_all | solution.py:384
  36.9 0.0 copy-start.2
  36.9 0.0 copy-start.6
  36.9 0.0 copy-start.7
  36.9 0.0 copy-start.3
  36.9 0.0 copy-start.4
  36.9 1.2 fusion
  38.1 9.4 %all-to-all-done.1.blocks = bf16[12,24,256]{2,1,0:T(8,128)(2,1)S(1)} async-done(((bf16[12,24,256]{2,1,0:T(8,128)(2,1)}), bf16[12,24,256]{2,1,0:T(8,128)(2,1)S(1)}, u32[]{:S(2)}, u32[]{:S(2)}) %all-to-all-start.1) | async-done | bytes 147488 | tf_op jit(solution)/shard_map/all_to_all | solution.py:384
  47.5 13.5 %all-to-all-start.2 = ((bf16[8,72,256]{2,1,0:T(8,128)(2,1)}), bf16[8,72,256]{2,1,0:T(8,128)(2,1)S(1)}, u32[]{:S(2)}, u32[]{:S(2)}) async-start(bf16[8,72,256]{2,1,0:T(8,128)(2,1)} %bitcast.9), calls=%async_computation.2 | async-start | bytes 589824 | tf_op jit(solution)/shard_map/all_to_all | solution.py:384
  61.1 0.1 copy.56
  61.2 0.1 copy.55
  61.2 0.0 copy-done.12
  61.2 0.1 copy.57
  61.3 0.1 copy.58
  61.4 0.1 fusion.18
  61.5 0.0 copy-done.1
  61.6 6.3 %shard_map.182 = (f32[64,3072]{1,0:T(8,128)}, f32[64,3072]{1,0:T(8,128)}, f32[64,3072]{1,0:T(8,128)}, f32[64,3072]{1,0:T(8,128)}, f32[12,8,512]{2,1,0:T(8,128)}) custom-call(f32[32,3072]{1,0:T(8,128)S(1)} %copy-done.2, f32[32,64]{1,0:T(8,128)S(1)} %copy-done.7, f32[64,64]{1,0:T(8,128)S(1)} %copy-done.6, f32[8,128]{1,0:T(8,128)S(1)} %pad.25.params, ...), custom_call_target="tpu_custom_call" | custom-call | tf_op jit(solution)/shard_map/pallas_call | solution.py:365
  67.9 0.9 copy-done.5
  68.8 1.7 shard_map.183
  70.5 6.0 %all-to-all-done.2 = bf16[8,72,256]{2,1,0:T(8,128)(2,1)S(1)} async-done(((bf16[8,72,256]{2,1,0:T(8,128)(2,1)}), bf16[8,72,256]{2,1,0:T(8,128)(2,1)S(1)}, u32[]{:S(2)}, u32[]{:S(2)}) %all-to-all-start.2) | async-done | bytes 294944 | tf_op jit(solution)/shard_map/all_to_all | solution.py:384
  76.6 0.8 fusion.5
  77.4 18.0 %all_to_all.35.blocks = bf16[12,16,256]{2,1,0:T(8,128)(2,1)S(1)} all-to-all(bf16[12,16,256]{2,1,0:T(8,128)(2,1)S(1)} %fusion.5), channel_id=1, replica_groups=mesh['ctx'=12,'ch'=64] {'ctx'}, dimensions={0} | all-to-all | bytes 196608 | tf_op jit(solution)/shard_map/all_to_all | solution.py:384
  95.5 5.7 %shard_map.184 = (bf16[12,48,128]{2,1,0:T(8,128)(2,1)}, bf16[96,64]{1,0:T(8,128)(2,1)S(1)}, bf16[16,64]{1,0:T(8,128)(2,1)S(1)}) custom-call(f32[12,8,512]{2,1,0:T(8,128)} %get-tuple-element.18.spectra.kept_spectra, f32[12,24,256]{2,1,0:T(8,128)} %get-tuple-element.20.kept_filtered, f32[12,8,256]{2,1,0:T(8,128)} %get-tuple-element.21.kept_long_out, ...), custom_call_target="tpu_custom_call" | custom-call | tf_op jit(solution)/shard_map/pallas_call | solution.py:365
  101.2 0.1 reshape.118
  101.3 0.8 broadcast_in_dim.27
  102.1 3.5 %all-to-all-start.4 = ((bf16[8,96,256]{2,1,0:T(8,128)(2,1)}), bf16[8,96,256]{2,1,0:T(8,128)(2,1)S(1)}, u32[]{:S(2)}, u32[]{:S(2)}) async-start(bf16[8,96,256]{2,1,0:T(8,128)(2,1)} %broadcast_in_dim.27), calls=%async_computation.4 | async-start | bytes 786432 | tf_op jit(solution)/shard_map/all_to_all | solution.py:384
  105.6 0.1 copy.59
  105.8 0.1 dot_general.20
  105.9 16.0 %all-to-all-done.4 = bf16[8,96,256]{2,1,0:T(8,128)(2,1)S(1)} async-done(((bf16[8,96,256]{2,1,0:T(8,128)(2,1)}), bf16[8,96,256]{2,1,0:T(8,128)(2,1)S(1)}, u32[]{:S(2)}, u32[]{:S(2)}) %all-to-all-start.4) | async-done | bytes 393248 | tf_op jit(solution)/shard_map/all_to_all | solution.py:384
  121.9 0.1 reshape.121
  122.0 0.3 convolution_convert_fusion
  122.3 0.9 pad_maximum_fusion.1
  123.2 5.8 %collective-permute-start = (bf16[6,48,768]{2,1,0:T(8,128)(2,1)}, bf16[6,48,768]{2,1,0:T(8,128)(2,1)S(1)}, u32[]{:S(2)}, u32[]{:S(2)}) collective-permute-start(bf16[6,48,768]{2,1,0:T(8,128)(2,1)} %pad_maximum_fusion.1), channel_id=1, source_target_pairs={{0,64},{64,0},{128,192},{192,128},{256,320},{320,256},{384,448},{4... | collective-permute-start | bytes 1327112 | tf_op jit(solution)/shard_map/ppermute | solution.py:527
  129.0 0.1 dot_general.18
  129.1 1.5 collective-permute-done
  130.6 0.1 reduce-precision_convert_fusion
  130.7 0.1 broadcast_select_fusion.1
  130.8 0.3 add_convert_fusion
  131.1 0.9 pad_maximum_fusion
  132.0 7.0 %all-to-all-start.5 = ((bf16[6,48,896]{2,1,0:T(8,128)(2,1)}), bf16[6,48,896]{2,1,0:T(8,128)(2,1)S(1)}, u32[]{:S(2)}, u32[]{:S(2)}) async-start(bf16[6,48,896]{2,1,0:T(8,128)(2,1)} %pad_maximum_fusion), calls=%async_computation.5 | async-start | bytes 1032192 | tf_op jit(solution)/shard_map/all_to_all | solution.py:384
  139.0 0.1 slice.134
  139.1 0.4 convolution_convert_fusion.1
  139.5 19.8 %all-to-all-done.5 = bf16[6,48,896]{2,1,0:T(8,128)(2,1)S(1)} async-done(((bf16[6,48,896]{2,1,0:T(8,128)(2,1)}), bf16[6,48,896]{2,1,0:T(8,128)(2,1)S(1)}, u32[]{:S(2)}, u32[]{:S(2)}) %all-to-all-start.5) | async-done | bytes 516128 | tf_op jit(solution)/shard_map/all_to_all | solution.py:384
  159.3 0.1 slice_reduce_fusion
  159.4 0.1 slice_convert_fusion.1
  159.6 0.1 broadcast_in_dim.29
  159.7 0.8 pad_maximum_fusion.2
  160.5 4.1 %all-to-all-start.6 = ((bf16[8,94,256]{2,1,0:T(8,128)(2,1)}), bf16[8,94,256]{2,1,0:T(8,128)(2,1)S(1)}, u32[]{:S(2)}, u32[]{:S(2)}) async-start(bf16[8,94,256]{2,1,0:T(8,128)(2,1)} %pad_maximum_fusion.2), calls=%async_computation.6 | async-start | bytes 786432 | tf_op jit(solution)/shard_map/all_to_all | solution.py:384
  164.6 0.1 copy.64
  164.7 0.7 reshape.126
  165.5 0.7 copy.67
  166.2 5.0 %all-to-all-done.6 = bf16[8,94,256]{2,1,0:T(8,128)(2,1)S(1)} async-done(((bf16[8,94,256]{2,1,0:T(8,128)(2,1)}), bf16[8,94,256]{2,1,0:T(8,128)(2,1)S(1)}, u32[]{:S(2)}, u32[]{:S(2)}) %all-to-all-start.6) | async-done | bytes 385056 | tf_op jit(solution)/shard_map/all_to_all | solution.py:384
  171.3 0.1 reshape.128
  171.5 0.2 reshape.129
  171.7 26.4 %all-gather.1 = bf16[12,6,4864]{2,1,0:T(8,128)(2,1)S(1)} all-gather(bf16[1,6,4864]{2,1,0:T(8,128)(2,1)S(1)} %maximum_bitcast_fusion), channel_id=2, replica_groups=mesh['ctx'=12,'ch'=64] {'ctx'}, dimensions={0}, use_global_device_ids=true | all-gather | bytes 758784 | tf_op jit(solution)/shard_map/all_gather | solution.py:584
  198.2 0.1 slice_convert_fusion
  198.4 0.7 slice.128
  199.1 0.7 slice.130
  199.7 1.3 reshape.134
  201.0 0.7 slice_reduce_fusion.1
  (70 shorter events, 0.8 us)
Async XLA Ops:
  0.6 8.6 %copy-start.9 = (bf16[3,72,256]{2,1,0:T(8,128)(2,1)S(1)}, bf16[3,72,256]{2,1,0:T(8,128)(2,1)}, u32[]{:S(2)}) copy-start(bf16[3,72,256]{2,1,0:T(8,128)(2,1)} %param.14) | copy-start | bytes 331780
  3.3 15.2 %all-to-all-start = ((bf16[8,72,832]{2,1,0:T(8,128)(2,1)}), bf16[8,72,832]{2,1,0:T(8,128)(2,1)S(1)}, u32[]{:S(2)}, u32[]{:S(2)}) async-start(bf16[8,72,832]{2,1,0:T(8,128)(2,1)} %shard_map.181), calls=%async_computation | async-start | bytes 2064384 | tf_op jit(solution)/shard_map/all_to_all | solution.py:384
  9.9 51.1 %copy-start.11 = (f32[3,72,3]{1,2,0:T(4,128)S(1)}, f32[3,72,3]{1,2,0:T(4,128)}, u32[]{:S(2)}) copy-start(f32[3,72,3]{1,2,0:T(4,128)} %param.15) | copy-start | bytes 7780
  9.9 51.2 %copy-start.10 = (f32[64,72]{1,0:T(8,128)S(1)}, f32[64,72]{1,0:T(8,128)}, u32[]{:S(2)}) copy-start(f32[64,72]{1,0:T(8,128)} %param.18) | copy-start | bytes 55300
  9.9 51.3 %copy-start.12 = (f32[72]{0:T(128)S(1)}, f32[72]{0:T(128)}, u32[]{:S(2)}) copy-start(f32[72]{0:T(128)} %param.19) | copy-start | bytes 868
  9.9 51.4 %copy-start.13 = (f32[72]{0:T(128)S(1)}, f32[72]{0:T(128)}, u32[]{:S(2)}) copy-start(f32[72]{0:T(128)} %param.20) | copy-start | bytes 868
  18.5 29.0 %all-to-all-start.1 = ((bf16[12,24,256]{2,1,0:T(8,128)(2,1)}), bf16[12,24,256]{2,1,0:T(8,128)(2,1)S(1)}, u32[]{:S(2)}, u32[]{:S(2)}) async-start(bf16[12,24,256]{2,1,0:T(8,128)(2,1)} %pad_bitcast_fusion), calls=%async_computation.1 | async-start | bytes 294912 | tf_op jit(solution)/shard_map/all_to_all | solution.py:384
  36.9 24.7 %copy-start = (bf16[256,512]{1,0:T(8,128)(2,1)S(1)}, bf16[256,512]{1,0:T(8,128)(2,1)}, u32[]{:S(2)}) copy-start(bf16[256,512]{1,0:T(8,128)(2,1)} %constant.63.clone.table_low) | copy-start | bytes 786436
  36.9 24.7 %copy-start.1 = (bf16[256,512]{1,0:T(8,128)(2,1)S(1)}, bf16[256,512]{1,0:T(8,128)(2,1)}, u32[]{:S(2)}) copy-start(bf16[256,512]{1,0:T(8,128)(2,1)} %constant.62.clone.table_high) | copy-start | bytes 786436
  36.9 24.7 %copy-start.2 = (f32[32,3072]{1,0:T(8,128)S(1)}, f32[32,3072]{1,0:T(8,128)}, u32[]{:S(2)}) copy-start(f32[32,3072]{1,0:T(8,128)} %constant.66.clone.features) | copy-start | bytes 1179652
  36.9 24.7 %copy-start.6 = (f32[64,64]{1,0:T(8,128)S(1)}, f32[64,64]{1,0:T(8,128)}, u32[]{:S(2)}) copy-start(f32[64,64]{1,0:T(8,128)} %filter_mid.3) | copy-start | bytes 49156
  36.9 24.7 %copy-start.7 = (f32[32,64]{1,0:T(8,128)S(1)}, f32[32,64]{1,0:T(8,128)}, u32[]{:S(2)}) copy-start(f32[32,64]{1,0:T(8,128)} %filter_in.1) | copy-start | bytes 24580
  36.9 31.0 %copy-start.3 = (bf16[512,256]{1,0:T(8,128)(2,1)S(1)}, bf16[512,256]{1,0:T(8,128)(2,1)}, u32[]{:S(2)}) copy-start(bf16[512,256]{1,0:T(8,128)(2,1)} %constant.65.clone.back_low) | copy-start | bytes 786436
  36.9 31.0 %copy-start.4 = (bf16[512,256]{1,0:T(8,128)(2,1)S(1)}, bf16[512,256]{1,0:T(8,128)(2,1)}, u32[]{:S(2)}) copy-start(bf16[512,256]{1,0:T(8,128)(2,1)} %constant.64.clone.back_high) | copy-start | bytes 786436
  47.5 29.0 %all-to-all-start.2 = ((bf16[8,72,256]{2,1,0:T(8,128)(2,1)}), bf16[8,72,256]{2,1,0:T(8,128)(2,1)S(1)}, u32[]{:S(2)}, u32[]{:S(2)}) async-start(bf16[8,72,256]{2,1,0:T(8,128)(2,1)} %bitcast.9), calls=%async_computation.2 | async-start | bytes 589824 | tf_op jit(solution)/shard_map/all_to_all | solution.py:384
  67.9 0.9 copy-start.5
  101.3 4.5 %copy-start.8 = (bf16[12,48,128]{2,1,0:T(8,128)(2,1)S(1)}, bf16[12,48,128]{2,1,0:T(8,128)(2,1)}, u32[]{:S(2)}) copy-start(bf16[12,48,128]{2,1,0:T(8,128)(2,1)} %get-tuple-element.29) | copy-start | bytes 442372
  102.1 19.7 %all-to-all-start.4 = ((bf16[8,96,256]{2,1,0:T(8,128)(2,1)}), bf16[8,96,256]{2,1,0:T(8,128)(2,1)S(1)}, u32[]{:S(2)}, u32[]{:S(2)}) async-start(bf16[8,96,256]{2,1,0:T(8,128)(2,1)} %broadcast_in_dim.27), calls=%async_computation.4 | async-start | bytes 786432 | tf_op jit(solution)/shard_map/all_to_all | solution.py:384
  123.2 7.4 %collective-permute-start = (bf16[6,48,768]{2,1,0:T(8,128)(2,1)}, bf16[6,48,768]{2,1,0:T(8,128)(2,1)S(1)}, u32[]{:S(2)}, u32[]{:S(2)}) collective-permute-start(bf16[6,48,768]{2,1,0:T(8,128)(2,1)} %pad_maximum_fusion.1), channel_id=1, source_target_pairs={{0,64},{64,0},{128,192},{192,128},{256,320},{320,256},{384,448},{4... | collective-permute-start | bytes 1327112 | tf_op jit(solution)/shard_map/ppermute | solution.py:527
  132.0 27.3 %all-to-all-start.5 = ((bf16[6,48,896]{2,1,0:T(8,128)(2,1)}), bf16[6,48,896]{2,1,0:T(8,128)(2,1)S(1)}, u32[]{:S(2)}, u32[]{:S(2)}) async-start(bf16[6,48,896]{2,1,0:T(8,128)(2,1)} %pad_maximum_fusion), calls=%async_computation.5 | async-start | bytes 1032192 | tf_op jit(solution)/shard_map/all_to_all | solution.py:384
  160.5 10.7 %all-to-all-start.6 = ((bf16[8,94,256]{2,1,0:T(8,128)(2,1)}), bf16[8,94,256]{2,1,0:T(8,128)(2,1)S(1)}, u32[]{:S(2)}, u32[]{:S(2)}) async-start(bf16[8,94,256]{2,1,0:T(8,128)(2,1)} %pad_maximum_fusion.2), calls=%async_computation.6 | async-start | bytes 786432 | tf_op jit(solution)/shard_map/all_to_all | solution.py:384

commit v3 on v2

--- a/solution.py
+++ b/solution.py
@@ -348,11 +348,12 @@
     )
     side = packed.shape[0]
     channels, tokens = cotangent.shape
+    order = [half * (side // 2) + place for place in range(side // 2) for half in range(2)]
     for i in range(side):
         packed[i, :, :tokens] = cotangent[...]
         pieces = [
             weight[:, (a * side + i) * channels : (a * side + i + 1) * channels]
-            for a in range(side)
+            for a in order
         ]
         packed[i, :, tokens:] = jnp.concatenate(pieces, axis=1)
 
@@ -360,7 +361,7 @@
 NEAR, FAR = pltpu.VMEM, pltpu.HBM
 
 
-def call(kernel, outs, scratch, copies, *operands):
+def call(kernel, flops, outs, scratch, copies, *operands):
     semaphores = [pltpu.SemaphoreType.DMA((copies,))] if copies else []
     return pl.pallas_call(
         kernel,
@@ -372,6 +373,9 @@
         out_specs=[pl.BlockSpec(memory_space=place) for place, _, _ in outs],
         scratch_shapes=[pltpu.VMEM(shape, kind) for shape, kind in scratch] + semaphores,
         compiler_params=pltpu.CompilerParams(vmem_limit_bytes=VMEM_LIMIT),
+        cost_estimate=pl.CostEstimate(
+            flops=flops, bytes_accessed=4 * 1024 * 1024, transcendentals=0
+        ),
     )(
         *[
             pltpu.with_memory_space_constraint(operand, FAR) if place is FAR else operand
@@ -398,14 +402,25 @@
     band_rows = filter_in.shape[0]
     side = int(math.isqrt(owners))
     near_groups = [[a * side + i for i in range(side)] for a in range(side)]
-    far_groups = [[a * side + i for a in range(side)] for i in range(side)]
+    places = side // 2
+    place_groups = [
+        [(half * places + place) * side + i for place in range(places)]
+        for half in range(2)
+        for i in range(side)
+    ]
+    half = lax.axis_index("ch") // (places * side)
+
+    def other_half(value):
+        pairs = [(j, (j + places * side) % owners) for j in range(owners)]
+        return lax.ppermute(value, "ch", pairs)
+
     group = side * channels
     pad_rows = ROWS - share
     tables = [jnp.asarray(t) for t in transform_tables()]
     features = jnp.asarray(position_features(band_rows // 2, length))
 
     (sent,) = call(
-        pack_kernel,
+        pack_kernel, 10**9,
         [(NEAR, (side, channels, tokens + group), bf16)],
         [(out_weight.shape, bf16), (grad_out.shape, bf16)],
         2,
@@ -417,7 +432,11 @@
     grad_terms = lax.dot_general(
         weight, cotangent, (((0,), (0,)), ((), ())), preferred_element_type=f32
     ).astype(bf16)
-    grad_terms = exchange(grad_terms.reshape(side, channels, tokens), "ch", far_groups)
+    grad_terms = grad_terms.reshape(places, 2, channels, tokens)
+    received = other_half(lax.dynamic_index_in_dim(grad_terms, 1 - half, 1, False))
+    grad_terms = lax.dynamic_index_in_dim(grad_terms, half, 1, False)
+    grad_terms = (grad_terms.astype(f32) + received.astype(f32)).astype(bf16)
+    grad_terms = exchange(grad_terms, "ch", place_groups)
     grad_gated = jnp.sum(grad_terms.astype(f32), axis=0).astype(bf16)
 
     by_share = streams.reshape(3, blocks, share, tokens).transpose(1, 0, 2, 3)
@@ -446,7 +465,7 @@
     spectrum = ((blocks, ROWS, 2 * tokens), f32)
     kept_waves = [wave] * 4 + [spectrum]
     *waves, spectra = call(
-        network_kernel, far_like(kept_waves), kept_waves + [((blocks * ROWS, tokens), f32)], 5,
+        network_kernel, 4 * 10**9, far_like(kept_waves), kept_waves + [((blocks * ROWS, tokens), f32)], 5,
         *near(features, filter_in, filter_mid, params, tables[0], tables[1]),
     )
     kept = [
@@ -456,7 +475,7 @@
         spectrum,
     ]
     gated, filtered, long_out, own_spectra = call(
-        forward_kernel, far_like(kept), kept + [((blocks * ROWS, 2 * tokens), f32)], 4,
+        forward_kernel, 10**9, far_like(kept), kept + [((blocks * ROWS, 2 * tokens), f32)], 4,
         *near(sequence, params, spectra, *tables),
     )
 
@@ -464,10 +483,11 @@
     turned = jnp.concatenate([gated.reshape(blocks, ROWS, tokens), turned], axis=1)
     turned = exchange(turned, "ctx")
     own_gated = turned[:, :share, :].reshape(channels, tokens)
+    there_gated = other_half(own_gated)
 
     packed_streams = ((blocks, 6 * ROWS, tokens // 2), bf16)
     grad_packed, grad_shared, grad_last = call(
-        backward_kernel,
+        backward_kernel, 4 * 10**9,
         [
             (FAR,) + packed_streams,
             (NEAR, (band_rows + hidden, hidden), bf16),
@@ -484,12 +504,19 @@
     )
 
     shared_rows = grad_shared.size // tokens
-    sent = jnp.concatenate([own_gated, grad_shared.reshape(shared_rows, tokens)], axis=0)
+    sent = jnp.concatenate(
+        [
+            jnp.where(half == 0, own_gated, there_gated),
+            jnp.where(half == 0, there_gated, own_gated),
+            grad_shared.reshape(shared_rows, tokens),
+        ],
+        axis=0,
+    )
     sent = exchange(
-        jnp.broadcast_to(sent[None], (side,) + sent.shape), "ch", far_groups
-    )
-    all_gated = sent[:, :channels].reshape(group, tokens)
-    shared = jnp.sum(sent[:, channels:].astype(f32), axis=0)
+        jnp.broadcast_to(sent[None], (places,) + sent.shape), "ch", place_groups
+    )
+    all_gated = sent[:, : 2 * channels].reshape(group, tokens)
+    shared = jnp.sum(sent[:, 2 * channels :].astype(f32), axis=0)
 
     out_terms = jnp.dot(weight, all_gated, preferred_element_type=f32).astype(bf16)
     def both_halves(value):
@@ -524,7 +551,9 @@
     last_here = jnp.broadcast_to(grad_last[None], (chips,) + grad_last.shape)
     terms, shared_part, packed = parts_for(1 - core)
     sent = joined(terms, shared_part, [last_here], [packed])
-    sent = lax.ppermute(sent, "ctx", [(k, k ^ 1) for k in range(blocks)])
+    core_pairs = [(k, k ^ 1) for k in range(blocks)]
+    chip_groups = [[2 * z + c for z in range(chips)] for c in range(2)]
+    sent = lax.ppermute(sent, "ctx", core_pairs)
     terms, shared_part, packed = parts_for(core)
     terms = terms + sent[:, :, :group].astype(f32)
     small = sent[:, :, group : group + hidden]
@@ -544,10 +573,11 @@
     sent = joined(
         terms, shared_part, in_order(last_here, last_there), in_order(packed, packed_there)
     )
-    sent = exchange(sent, "ctx", [[2 * z + c for z in range(chips)] for c in range(2)])
+    sent = exchange(sent, "ctx", chip_groups)
     weight_share = jnp.sum(sent[:, :, :group].astype(f32), axis=0).astype(bf16)
     small = sent[:, :, group : group + hidden].astype(f32)
     shared = jnp.sum(small[:, :portion] + small[:, portion : 2 * portion], axis=0)
+    shared = shared + other_half(shared)
     lasts = small[:, last_at : last_at + 4 * ROWS].reshape(blocks, 2, ROWS, hidden)[:, :, :share]
     grad_filter_out = jnp.sum(lasts, axis=1).reshape(channels, hidden).T
     packed = sent[:, :, group + hidden :].reshape(chips, 2, 3, ROWS, 2, tokens // 2)
@@ -572,7 +602,7 @@
     sent = exchange(sent, "ch", near_groups)
     layer_out = jnp.sum(sent[:, :channels].astype(f32), axis=0).astype(bf16)
     weight_rows = sent[:, channels : channels + 3 * share].reshape(side, share, width)[:, :, :group]
-    weight_rows = weight_rows.reshape(side, share, side, channels).transpose(1, 2, 0, 3)
+    weight_rows = weight_rows.reshape(side, share, places, 2, channels).transpose(1, 3, 2, 0, 4)
     weight_rows = weight_rows.reshape(share, owners * channels)
     tail = jnp.sum(sent[:, channels + 3 * share :].astype(f32), axis=0)
     tail = tail.reshape(2, portion * hidden)
@@ -581,7 +611,10 @@
     tail = jnp.concatenate([high, low])
     spare = -tail.size % (share * 128)
     tail = jnp.pad(tail, (0, spare)).reshape(share, -1)
-    sent = lax.all_gather(jnp.concatenate([weight_rows, tail], axis=1), "ctx", axis=0)
+    sent = jnp.concatenate([weight_rows, tail], axis=1)
+    here = lax.all_gather(sent, "ctx", axis=0, axis_index_groups=chip_groups)
+    there = lax.ppermute(here, "ctx", core_pairs)
+    sent = jnp.stack(in_order(here, there), axis=1).reshape(blocks, share, -1)
     grad_out_weight = sent[:, :, : weight_rows.shape[1]].reshape(channels, -1).astype(f32)
     tail = sent[:, :, weight_rows.shape[1] :].reshape(blocks, -1).astype(f32)
     size = portion * hidden

time: 202 us -> 225 us (1.11)
  starting transfers between devices: 58 us -> 98.8 us
  blocking collectives: 44.4 us -> 26 us
    ppermute x1 -> x5, starting transfers between devices: 5.75 us -> 40 us  [the longest x3 23.7 us: other_half(): return lax.ppermute(value, 'ch', pairs)]
    all_to_all x1 -> x0, blocking collectives: 18 us -> none  [exchange(): lax.all_to_all(value, axis, 0, 0, tiled=True, axis_index_groups=groups)]
    all_to_all x6 -> x7, waiting for transfers between devices: 64.9 us -> 53.8 us  [exchange(): lax.all_to_all(value, axis, 0, 0, tiled=True, axis_index_groups=groups)]
    ppermute x1 -> x5, waiting for transfers between devices: 1.5 us -> 10.5 us  [the longest x3 9.18 us: other_half(): return lax.ppermute(value, 'ch', pairs)]
    all_to_all x6 -> x7, starting transfers between devices: 52.3 us -> 58.8 us  [exchange(): lax.all_to_all(value, axis, 0, 0, tiled=True, axis_index_groups=groups)]
  transfers between devices with their start and end apart: 7 -> 12, of which waited for: 7 -> 8; matrix products, arithmetic and copies ran while one was open for 2% -> 2% of each run, Pallas kernels for 4% -> 6%
where the time goes in v3:
time: 225 us; the launch traced here: 224 us
  starting transfers between devices  98.8 us (44%)
  waiting for transfers between devices  64.3 us (29%)
  blocking collectives  26 us (12%)
  Pallas kernels  16.3 us (7%)
  local copies, waits for them, and re-layouts  9.95 us (4%)
  other arithmetic  5.67 us (3%)
    all_to_all x7, starting transfers between devices, exchange(): lax.all_to_all(value, axis, 0, 0, tiled=True, axis_index_groups=groups)  58.8 us
    all_to_all x7, waiting for transfers between devices, exchange(): lax.all_to_all(value, axis, 0, 0, tiled=True, axis_index_groups=groups)  53.8 us
    all_gather x1, blocking collectives, shards(): here = lax.all_gather(sent, 'ctx', axis=0, axis_index_groups=chip_groups)  26 us
    ppermute x3, starting transfers between devices, other_half(): return lax.ppermute(value, 'ch', pairs)  23.7 us
    pallas_call x4, Pallas kernels, call(): pl.pallas_call(kernel, out_shape=[pltpu.HBM(shape, kind) if place is FAR...  16.3 us
    ppermute x1, starting transfers between devices, shards(): there = lax.ppermute(here, 'ctx', core_pairs)  10.3 us
    ppermute x3, waiting for transfers between devices, other_half(): return lax.ppermute(value, 'ch', pairs)  9.18 us
    ppermute x1, starting transfers between devices, shards(): sent = lax.ppermute(sent, 'ctx', core_pairs)  6.04 us
  transfers between devices with their start and end apart: 12, of which 8 were waited for; matrix products, arithmetic and copies ran while one was open for 2% of the time, Pallas kernels for 6%

profile of v3, /device:TPU:1, one launch (start us, length us, event | category | flops | bytes accessed | tf_op | source)
XLA Modules:
  0.0 223.8 jit_solution(11171238319752379499)
XLA Ops:
  0.6 2.6 %shard_map.181 = bf16[8,72,832]{2,1,0:T(8,128)(2,1)} custom-call(bf16[72,4608]{1,0:T(8,128)(2,1)} %far_weight.1, bf16[72,256]{1,0:T(8,128)(2,1)} %far_cotangent.1), custom_call_target="tpu_custom_call" | custom-call | flops 1000000000 | bytes 4194304 | tf_op jit(solution)/shard_map/pallas_call | solution.py:366
  3.3 6.0 %all-to-all-start = ((bf16[8,72,832]{2,1,0:T(8,128)(2,1)}), bf16[8,72,832]{2,1,0:T(8,128)(2,1)S(1)}, u32[]{:S(2)}, u32[]{:S(2)}) async-start(bf16[8,72,832]{2,1,0:T(8,128)(2,1)} %shard_map.181), calls=%async_computation | async-start | bytes 2064384 | tf_op jit(solution)/shard_map/all_to_all | solution.py:388
  9.4 0.7 pad_bitcast_fusion
  10.1 8.6 %all-to-all-done = bf16[8,72,832]{2,1,0:T(8,128)(2,1)S(1)} async-done(((bf16[8,72,832]{2,1,0:T(8,128)(2,1)}), bf16[8,72,832]{2,1,0:T(8,128)(2,1)S(1)}, u32[]{:S(2)}, u32[]{:S(2)}) %all-to-all-start) | async-done | bytes 958496 | tf_op jit(solution)/shard_map/all_to_all | solution.py:388
  18.6 18.3 %all-to-all-start.1 = ((bf16[12,24,256]{2,1,0:T(8,128)(2,1)}), bf16[12,24,256]{2,1,0:T(8,128)(2,1)S(1)}, u32[]{:S(2)}, u32[]{:S(2)}) async-start(bf16[12,24,256]{2,1,0:T(8,128)(2,1)} %pad_bitcast_fusion), calls=%async_computation.1 | async-start | bytes 294912 | tf_op jit(solution)/shard_map/all_to_all | solution.py:388
  37.0 0.4 fusion
  37.5 9.8 %collective-permute-start = (bf16[4,72,256]{2,1,0:T(8,128)(2,1)S(1)}, bf16[4,72,256]{2,1,0:T(8,128)(2,1)S(1)}, u32[]{:S(2)}, u32[]{:S(2)}) collective-permute-start(bf16[4,72,256]{2,1,0:T(8,128)(2,1)S(1)} %dynamic-slice_bitcast_fusion.2), channel_id=1, source_target_pairs={{0,32},{1,33},{2,34},{3,35},{4,36},{5,37},{6,38},{7,39},{8,40},{9,... | collective-permute-start | bytes 442376 | tf_op jit(solution)/shard_map/ppermute | solution.py:415
  47.3 0.1 copy.88
  47.4 0.1 copy.87
  47.5 0.1 copy.89
  47.6 0.1 copy.90
  47.7 0.1 fusion.19
  47.8 4.1 %collective-permute-done = bf16[4,72,256]{2,1,0:T(8,128)(2,1)S(1)} collective-permute-done((bf16[4,72,256]{2,1,0:T(8,128)(2,1)S(1)}, bf16[4,72,256]{2,1,0:T(8,128)(2,1)S(1)}, u32[]{:S(2)}, u32[]{:S(2)}) %collective-permute-start) | collective-permute-done | bytes 147488 | tf_op jit(solution)/shard_map/ppermute | solution.py:415
  51.8 0.7 fusion.1
  52.6 5.9 %all-to-all-start.2 = ((bf16[4,72,256]{2,1,0:T(8,128)(2,1)}), bf16[4,72,256]{2,1,0:T(8,128)(2,1)S(1)}, u32[]{:S(2)}, u32[]{:S(2)}) async-start(bf16[4,72,256]{2,1,0:T(8,128)(2,1)} %fusion.1), calls=%async_computation.2 | async-start | bytes 294912 | tf_op jit(solution)/shard_map/all_to_all | solution.py:388
  58.5 6.3 %shard_map.182 = (f32[64,3072]{1,0:T(8,128)}, f32[64,3072]{1,0:T(8,128)}, f32[64,3072]{1,0:T(8,128)}, f32[64,3072]{1,0:T(8,128)}, f32[12,8,512]{2,1,0:T(8,128)}) custom-call(f32[32,3072]{1,0:T(8,128)S(1)} %copy-done.2, f32[32,64]{1,0:T(8,128)S(1)} %copy-done.1, f32[64,64]{1,0:T(8,128)S(1)} %copy-done, f32[8,128]{1,0:T(8,128)S(1)} %pad.25.params, ...), custom_call_target="tpu_custom_call" | custom-call | flops 4000000000 | bytes 4194304 | tf_op jit(solution)/shard_map/pallas_call | solution.py:366
  64.9 0.9 copy-done.7
  65.8 1.6 shard_map.183
  67.5 1.5 fusion.6
  69.0 15.4 %all-to-all-start.3 = ((bf16[12,16,256]{2,1,0:T(8,128)(2,1)}), bf16[12,16,256]{2,1,0:T(8,128)(2,1)S(1)}, u32[]{:S(2)}, u32[]{:S(2)}) async-start(bf16[12,16,256]{2,1,0:T(8,128)(2,1)} %fusion.6), calls=%async_computation.3 | async-start | bytes 196608 | tf_op jit(solution)/shard_map/all_to_all | solution.py:388
  84.4 9.2 %all-to-all-done.3.blocks = bf16[12,16,256]{2,1,0:T(8,128)(2,1)S(1)} async-done(((bf16[12,16,256]{2,1,0:T(8,128)(2,1)}), bf16[12,16,256]{2,1,0:T(8,128)(2,1)S(1)}, u32[]{:S(2)}, u32[]{:S(2)}) %all-to-all-start.3) | async-done | bytes 98336 | tf_op jit(solution)/shard_map/all_to_all | solution.py:388
  93.6 8.5 %collective-permute-start.1 = (bf16[72,256]{1,0:T(8,128)(2,1)S(1)}, bf16[72,256]{1,0:T(8,128)(2,1)S(1)}, u32[]{:S(2)}, u32[]{:S(2)}) collective-permute-start(bf16[72,256]{1,0:T(8,128)(2,1)S(1)} %reshape.122), channel_id=1, source_target_pairs={{0,32},{1,33},{2,34},{3,35},{4,36},{5,37},{6,38},{7,39},{8,40},{9,... | collective-permute-start | bytes 110600 | tf_op jit(solution)/shard_map/ppermute | solution.py:415
  102.1 5.8 %shard_map.184 = (bf16[12,48,128]{2,1,0:T(8,128)(2,1)}, bf16[96,64]{1,0:T(8,128)(2,1)S(1)}, bf16[16,64]{1,0:T(8,128)(2,1)S(1)}) custom-call(f32[12,8,512]{2,1,0:T(8,128)} %get-tuple-element.18.spectra.kept_spectra, f32[12,24,256]{2,1,0:T(8,128)} %get-tuple-element.20.kept_filtered, f32[12,8,256]{2,1,0:T(8,128)} %get-tuple-element.21.kept_long_out, ...), custom_call_target="tpu_custom_call" | custom-call | flops 4000000000 | bytes 4194304 | tf_op jit(solution)/shard_map/pallas_call | solution.py:366
  107.9 0.1 reshape.123
  108.0 0.8 broadcast_in_dim.27
  108.8 6.1 %all-to-all-start.4 = ((bf16[4,168,256]{2,1,0:T(8,128)(2,1)}), bf16[4,168,256]{2,1,0:T(8,128)(2,1)S(1)}, u32[]{:S(2)}, u32[]{:S(2)}) async-start(bf16[4,168,256]{2,1,0:T(8,128)(2,1)} %broadcast_in_dim.27), calls=%async_computation.4 | async-start | bytes 688128 | tf_op jit(solution)/shard_map/all_to_all | solution.py:388
  115.2 9.2 %all-to-all-done.4 = bf16[4,168,256]{2,1,0:T(8,128)(2,1)S(1)} async-done(((bf16[4,168,256]{2,1,0:T(8,128)(2,1)}), bf16[4,168,256]{2,1,0:T(8,128)(2,1)S(1)}, u32[]{:S(2)}, u32[]{:S(2)}) %all-to-all-start.4) | async-done | bytes 344096 | tf_op jit(solution)/shard_map/all_to_all | solution.py:388
  124.4 0.1 reshape.126
  124.5 0.3 convolution_convert_fusion
  124.9 0.1 pad_maximum_fusion.2
  125.0 6.0 %collective-permute-start.2 = (bf16[6,48,768]{2,1,0:T(8,128)(2,1)S(1)}, bf16[6,48,768]{2,1,0:T(8,128)(2,1)S(1)}, u32[]{:S(2)}, u32[]{:S(2)}) collective-permute-start(bf16[6,48,768]{2,1,0:T(8,128)(2,1)S(1)} %pad_maximum_fusion.2), channel_id=1, source_target_pairs={{0,64},{64,0},{128,192},{192,128},{256,320},{320,256},{384,448},{4... | collective-permute-start | bytes 1327112 | tf_op jit(solution)/shard_map/ppermute | solution.py:556
  131.2 1.3 collective-permute-done.2
  132.4 0.1 reduce-precision_convert_fusion
  132.5 0.1 broadcast_select_fusion.3
  132.6 0.3 add_convert_fusion
  132.9 0.9 pad_maximum_fusion.1
  133.8 3.5 %all-to-all-start.5 = ((bf16[6,48,896]{2,1,0:T(8,128)(2,1)}), bf16[6,48,896]{2,1,0:T(8,128)(2,1)S(1)}, u32[]{:S(2)}, u32[]{:S(2)}) async-start(bf16[6,48,896]{2,1,0:T(8,128)(2,1)} %pad_maximum_fusion.1), calls=%async_computation.5 | async-start | bytes 1032192 | tf_op jit(solution)/shard_map/all_to_all | solution.py:388
  137.4 0.1 slice.134
  137.4 0.4 convolution_convert_fusion.1
  137.8 20.3 %all-to-all-done.5 = bf16[6,48,896]{2,1,0:T(8,128)(2,1)S(1)} async-done(((bf16[6,48,896]{2,1,0:T(8,128)(2,1)}), bf16[6,48,896]{2,1,0:T(8,128)(2,1)S(1)}, u32[]{:S(2)}, u32[]{:S(2)}) %all-to-all-start.5) | async-done | bytes 516128 | tf_op jit(solution)/shard_map/all_to_all | solution.py:388
  158.1 0.1 slice_convert_fusion.1
  158.2 5.4 %collective-permute-start.3 = (f32[8,64]{1,0:T(8,128)S(1)}, f32[8,64]{1,0:T(8,128)S(1)}, u32[]{:S(2)}, u32[]{:S(2)}) collective-permute-start(f32[8,64]{1,0:T(8,128)S(1)} %fusion.11), channel_id=1, source_target_pairs={{0,32},{1,33},{2,34},{3,35},{4,36},{5,37},{6,38},{7,39},{8,40},{9,... | collective-permute-start | bytes 6152 | tf_op jit(solution)/shard_map/ppermute | solution.py:415
  163.8 5.1 %collective-permute-done.3 = f32[8,64]{1,0:T(8,128)S(1)} collective-permute-done((f32[8,64]{1,0:T(8,128)S(1)}, f32[8,64]{1,0:T(8,128)S(1)}, u32[]{:S(2)}, u32[]{:S(2)}) %collective-permute-start.3) | collective-permute-done | bytes 2080 | tf_op jit(solution)/shard_map/ppermute | solution.py:415
  168.9 0.1 broadcast_in_dim.29
  169.0 0.8 pad_maximum_fusion.3
  169.8 3.5 %all-to-all-start.6 = ((bf16[8,94,256]{2,1,0:T(8,128)(2,1)}), bf16[8,94,256]{2,1,0:T(8,128)(2,1)S(1)}, u32[]{:S(2)}, u32[]{:S(2)}) async-start(bf16[8,94,256]{2,1,0:T(8,128)(2,1)} %pad_maximum_fusion.3), calls=%async_computation.6 | async-start | bytes 786432 | tf_op jit(solution)/shard_map/all_to_all | solution.py:388
  173.3 6.6 %all-to-all-done.6 = bf16[8,94,256]{2,1,0:T(8,128)(2,1)S(1)} async-done(((bf16[8,94,256]{2,1,0:T(8,128)(2,1)}), bf16[8,94,256]{2,1,0:T(8,128)(2,1)S(1)}, u32[]{:S(2)}, u32[]{:S(2)}) %all-to-all-start.6) | async-done | bytes 385056 | tf_op jit(solution)/shard_map/all_to_all | solution.py:388
  180.0 0.1 reshape.133
  180.2 0.2 reshape.134
  180.4 26.0 %all-gather.1 = bf16[6,6,4864]{2,1,0:T(8,128)(2,1)S(1)} all-gather(bf16[1,6,4864]{2,1,0:T(8,128)(2,1)S(1)} %maximum_bitcast_fusion), channel_id=2, replica_groups={{0,128,256,384,512,640},{64,192,320,448,576,704},{1,129,257,385,513,641..., dimensions={0}, use_global_device_ids=true | all-gather | bytes 408576 | tf_op jit(solution)/shard_map/all_gather | solution.py:615
  206.4 10.3 %collective-permute-start.4 = (bf16[6,6,4864]{2,1,0:T(8,128)(2,1)S(1)}, bf16[6,6,4864]{2,1,0:T(8,128)(2,1)S(1)}, u32[]{:S(2)}, u32[]{:S(2)}) collective-permute-start(bf16[6,6,4864]{2,1,0:T(8,128)(2,1)S(1)} %all-gather.1), channel_id=1, source_target_pairs={{0,64},{64,0},{128,192},{192,128},{256,320},{320,256},{384,448},{4... | collective-permute-start | bytes 1050632 | tf_op jit(solution)/shard_map/ppermute | solution.py:616
  216.7 0.1 copy.96
  216.8 0.7 reshape.131
  217.6 0.7 copy.102
  218.3 0.7 slice_reduce_fusion.1
  218.9 0.1 select_bitcast_fusion.1
  219.0 0.2 pad_maximum_fusion
  219.2 0.5 copy.99
  219.8 0.3 reshape.136
  220.2 0.1 slice_convert_fusion
  220.4 0.7 slice.128
  221.1 0.7 slice.130
  221.7 0.8 copy.101
  222.6 1.3 reshape.141
  (88 shorter events, 1.1 us)
Async XLA Ops:
  3.3 6.0 %copy-start.9 = (bf16[3,72,256]{2,1,0:T(8,128)(2,1)S(1)}, bf16[3,72,256]{2,1,0:T(8,128)(2,1)}, u32[]{:S(2)}) copy-start(bf16[3,72,256]{2,1,0:T(8,128)(2,1)} %param.14) | copy-start | bytes 331780
  3.3 15.4 %all-to-all-start = ((bf16[8,72,832]{2,1,0:T(8,128)(2,1)}), bf16[8,72,832]{2,1,0:T(8,128)(2,1)S(1)}, u32[]{:S(2)}, u32[]{:S(2)}) async-start(bf16[8,72,832]{2,1,0:T(8,128)(2,1)} %shard_map.181), calls=%async_computation | async-start | bytes 2064384 | tf_op jit(solution)/shard_map/all_to_all | solution.py:388
  9.3 37.9 %copy-start.11 = (f32[3,72,3]{1,2,0:T(4,128)S(1)}, f32[3,72,3]{1,2,0:T(4,128)}, u32[]{:S(2)}) copy-start(f32[3,72,3]{1,2,0:T(4,128)} %param.15) | copy-start | bytes 7780
  9.4 38.0 %copy-start.10 = (f32[64,72]{1,0:T(8,128)S(1)}, f32[64,72]{1,0:T(8,128)}, u32[]{:S(2)}) copy-start(f32[64,72]{1,0:T(8,128)} %param.18) | copy-start | bytes 55300
  9.4 38.1 %copy-start.12 = (f32[72]{0:T(128)S(1)}, f32[72]{0:T(128)}, u32[]{:S(2)}) copy-start(f32[72]{0:T(128)} %param.19) | copy-start | bytes 868
  9.4 38.2 %copy-start.13 = (f32[72]{0:T(128)S(1)}, f32[72]{0:T(128)}, u32[]{:S(2)}) copy-start(f32[72]{0:T(128)} %param.20) | copy-start | bytes 868
  18.6 33.9 %all-to-all-start.1 = ((bf16[12,24,256]{2,1,0:T(8,128)(2,1)}), bf16[12,24,256]{2,1,0:T(8,128)(2,1)S(1)}, u32[]{:S(2)}, u32[]{:S(2)}) async-start(bf16[12,24,256]{2,1,0:T(8,128)(2,1)} %pad_bitcast_fusion), calls=%async_computation.1 | async-start | bytes 294912 | tf_op jit(solution)/shard_map/all_to_all | solution.py:388
  36.9 21.5 %copy-start = (f32[64,64]{1,0:T(8,128)S(1)}, f32[64,64]{1,0:T(8,128)}, u32[]{:S(2)}) copy-start(f32[64,64]{1,0:T(8,128)} %filter_mid.3) | copy-start | bytes 49156
  36.9 21.5 %copy-start.1 = (f32[32,64]{1,0:T(8,128)S(1)}, f32[32,64]{1,0:T(8,128)}, u32[]{:S(2)}) copy-start(f32[32,64]{1,0:T(8,128)} %filter_in.1) | copy-start | bytes 24580
  37.0 21.5 %copy-start.2 = (f32[32,3072]{1,0:T(8,128)S(1)}, f32[32,3072]{1,0:T(8,128)}, u32[]{:S(2)}) copy-start(f32[32,3072]{1,0:T(8,128)} %constant.90.clone.features) | copy-start | bytes 1179652
  37.0 21.5 %copy-start.3 = (bf16[256,512]{1,0:T(8,128)(2,1)S(1)}, bf16[256,512]{1,0:T(8,128)(2,1)}, u32[]{:S(2)}) copy-start(bf16[256,512]{1,0:T(8,128)(2,1)} %constant.87.clone.table_low) | copy-start | bytes 786436
  37.0 21.5 %copy-start.4 = (bf16[256,512]{1,0:T(8,128)(2,1)S(1)}, bf16[256,512]{1,0:T(8,128)(2,1)}, u32[]{:S(2)}) copy-start(bf16[256,512]{1,0:T(8,128)(2,1)} %constant.86.clone.table_high) | copy-start | bytes 786436
  37.5 14.4 %collective-permute-start = (bf16[4,72,256]{2,1,0:T(8,128)(2,1)S(1)}, bf16[4,72,256]{2,1,0:T(8,128)(2,1)S(1)}, u32[]{:S(2)}, u32[]{:S(2)}) collective-permute-start(bf16[4,72,256]{2,1,0:T(8,128)(2,1)S(1)} %dynamic-slice_bitcast_fusion.2), channel_id=1, source_target_pairs={{0,32},{1,33},{2,34},{3,35},{4,36},{5,37},{6,38},{7,39},{8,40},{9,... | collective-permute-start | bytes 442376 | tf_op jit(solution)/shard_map/ppermute | solution.py:415
  52.6 14.9 %all-to-all-start.2 = ((bf16[4,72,256]{2,1,0:T(8,128)(2,1)}), bf16[4,72,256]{2,1,0:T(8,128)(2,1)S(1)}, u32[]{:S(2)}, u32[]{:S(2)}) async-start(bf16[4,72,256]{2,1,0:T(8,128)(2,1)} %fusion.1), calls=%async_computation.2 | async-start | bytes 294912 | tf_op jit(solution)/shard_map/all_to_all | solution.py:388
  58.5 6.3 %copy-start.5 = (bf16[512,256]{1,0:T(8,128)(2,1)S(1)}, bf16[512,256]{1,0:T(8,128)(2,1)}, u32[]{:S(2)}) copy-start(bf16[512,256]{1,0:T(8,128)(2,1)} %constant.89.clone.back_low) | copy-start | bytes 786436
  58.5 6.3 %copy-start.6 = (bf16[512,256]{1,0:T(8,128)(2,1)S(1)}, bf16[512,256]{1,0:T(8,128)(2,1)}, u32[]{:S(2)}) copy-start(bf16[512,256]{1,0:T(8,128)(2,1)} %constant.88.clone.back_high) | copy-start | bytes 786436
  64.9 0.9 copy-start.7
  69.0 24.6 %all-to-all-start.3 = ((bf16[12,16,256]{2,1,0:T(8,128)(2,1)}), bf16[12,16,256]{2,1,0:T(8,128)(2,1)S(1)}, u32[]{:S(2)}, u32[]{:S(2)}) async-start(bf16[12,16,256]{2,1,0:T(8,128)(2,1)} %fusion.6), calls=%async_computation.3 | async-start | bytes 196608 | tf_op jit(solution)/shard_map/all_to_all | solution.py:388
  93.6 14.4 %collective-permute-start.1 = (bf16[72,256]{1,0:T(8,128)(2,1)S(1)}, bf16[72,256]{1,0:T(8,128)(2,1)S(1)}, u32[]{:S(2)}, u32[]{:S(2)}) collective-permute-start(bf16[72,256]{1,0:T(8,128)(2,1)S(1)} %reshape.122), channel_id=1, source_target_pairs={{0,32},{1,33},{2,34},{3,35},{4,36},{5,37},{6,38},{7,39},{8,40},{9,... | collective-permute-start | bytes 110600 | tf_op jit(solution)/shard_map/ppermute | solution.py:415
  108.0 7.1 %copy-start.8 = (bf16[12,48,128]{2,1,0:T(8,128)(2,1)S(1)}, bf16[12,48,128]{2,1,0:T(8,128)(2,1)}, u32[]{:S(2)}) copy-start(bf16[12,48,128]{2,1,0:T(8,128)(2,1)} %get-tuple-element.29) | copy-start | bytes 442372
  108.8 15.6 %all-to-all-start.4 = ((bf16[4,168,256]{2,1,0:T(8,128)(2,1)}), bf16[4,168,256]{2,1,0:T(8,128)(2,1)S(1)}, u32[]{:S(2)}, u32[]{:S(2)}) async-start(bf16[4,168,256]{2,1,0:T(8,128)(2,1)} %broadcast_in_dim.27), calls=%async_computation.4 | async-start | bytes 688128 | tf_op jit(solution)/shard_map/all_to_all | solution.py:388
  125.0 7.5 %collective-permute-start.2 = (bf16[6,48,768]{2,1,0:T(8,128)(2,1)S(1)}, bf16[6,48,768]{2,1,0:T(8,128)(2,1)S(1)}, u32[]{:S(2)}, u32[]{:S(2)}) collective-permute-start(bf16[6,48,768]{2,1,0:T(8,128)(2,1)S(1)} %pad_maximum_fusion.2), channel_id=1, source_target_pairs={{0,64},{64,0},{128,192},{192,128},{256,320},{320,256},{384,448},{4... | collective-permute-start | bytes 1327112 | tf_op jit(solution)/shard_map/ppermute | solution.py:556
  133.8 24.3 %all-to-all-start.5 = ((bf16[6,48,896]{2,1,0:T(8,128)(2,1)}), bf16[6,48,896]{2,1,0:T(8,128)(2,1)S(1)}, u32[]{:S(2)}, u32[]{:S(2)}) async-start(bf16[6,48,896]{2,1,0:T(8,128)(2,1)} %pad_maximum_fusion.1), calls=%async_computation.5 | async-start | bytes 1032192 | tf_op jit(solution)/shard_map/all_to_all | solution.py:388
  158.2 10.7 %collective-permute-start.3 = (f32[8,64]{1,0:T(8,128)S(1)}, f32[8,64]{1,0:T(8,128)S(1)}, u32[]{:S(2)}, u32[]{:S(2)}) collective-permute-start(f32[8,64]{1,0:T(8,128)S(1)} %fusion.11), channel_id=1, source_target_pairs={{0,32},{1,33},{2,34},{3,35},{4,36},{5,37},{6,38},{7,39},{8,40},{9,... | collective-permute-start | bytes 6152 | tf_op jit(solution)/shard_map/ppermute | solution.py:415
  169.8 10.1 %all-to-all-start.6 = ((bf16[8,94,256]{2,1,0:T(8,128)(2,1)}), bf16[8,94,256]{2,1,0:T(8,128)(2,1)S(1)}, u32[]{:S(2)}, u32[]{:S(2)}) async-start(bf16[8,94,256]{2,1,0:T(8,128)(2,1)} %pad_maximum_fusion.3), calls=%async_computation.6 | async-start | bytes 786432 | tf_op jit(solution)/shard_map/all_to_all | solution.py:388
  206.4 12.5 %collective-permute-start.4 = (bf16[6,6,4864]{2,1,0:T(8,128)(2,1)S(1)}, bf16[6,6,4864]{2,1,0:T(8,128)(2,1)S(1)}, u32[]{:S(2)}, u32[]{:S(2)}) collective-permute-start(bf16[6,6,4864]{2,1,0:T(8,128)(2,1)S(1)} %all-gather.1), channel_id=1, source_target_pairs={{0,64},{64,0},{128,192},{192,128},{256,320},{320,256},{384,448},{4... | collective-permute-start | bytes 1050632 | tf_op jit(solution)/shard_map/ppermute | solution.py:616

commit v4 on v2

--- a/solution.py
+++ b/solution.py
@@ -399,6 +399,9 @@
     side = int(math.isqrt(owners))
     near_groups = [[a * side + i for i in range(side)] for a in range(side)]
     far_groups = [[a * side + i for a in range(side)] for i in range(side)]
+    places = side // 2
+    place_groups = [group[h * places : (h + 1) * places] for group in far_groups for h in range(2)]
+    half = lax.axis_index("ch") // (places * side)
     group = side * channels
     pad_rows = ROWS - share
     tables = [jnp.asarray(t) for t in transform_tables()]
@@ -417,12 +420,16 @@
     grad_terms = lax.dot_general(
         weight, cotangent, (((0,), (0,)), ((), ())), preferred_element_type=f32
     ).astype(bf16)
-    grad_terms = exchange(grad_terms.reshape(side, channels, tokens), "ch", far_groups)
+    grad_terms = grad_terms.reshape(2, places, channels, tokens)
+    received = lax.ppermute(
+        lax.dynamic_index_in_dim(grad_terms, 1 - half, 0, False),
+        "ch",
+        [(j, (j + places * side) % owners) for j in range(owners)],
+    )
+    grad_terms = lax.dynamic_index_in_dim(grad_terms, half, 0, False)
+    grad_terms = (grad_terms.astype(f32) + received.astype(f32)).astype(bf16)
+    grad_terms = exchange(grad_terms, "ch", place_groups)
     grad_gated = jnp.sum(grad_terms.astype(f32), axis=0).astype(bf16)
-
-    by_share = streams.reshape(3, blocks, share, tokens).transpose(1, 0, 2, 3)
-    by_share = jnp.pad(by_share, ((0, 0), (0, 0), (0, pad_rows), (0, 0)))
-    sequence = exchange(by_share.reshape(blocks, 3 * ROWS, tokens), "ctx")
 
     params = jnp.concatenate(
         [
@@ -449,6 +456,11 @@
         network_kernel, far_like(kept_waves), kept_waves + [((blocks * ROWS, tokens), f32)], 5,
         *near(features, filter_in, filter_mid, params, tables[0], tables[1]),
     )
+
+    by_share = streams.reshape(3, blocks, share, tokens).transpose(1, 0, 2, 3)
+    by_share = jnp.pad(by_share, ((0, 0), (0, 0), (0, pad_rows), (0, 0)))
+    by_share, spectra = lax.optimization_barrier((by_share, spectra))
+    sequence = exchange(by_share.reshape(blocks, 3 * ROWS, tokens), "ctx")
     kept = [
         ((blocks * ROWS, tokens), bf16),
         ((blocks, 3 * ROWS, tokens), f32),

time: 202 us -> 204 us (level)
  waiting for transfers between devices: 66.4 us -> 54.4 us
  blocking collectives: 44.4 us -> 51.9 us
  starting transfers between devices: 58 us -> 64.8 us
    all_to_all x6, waiting for transfers between devices: 64.9 us -> 48.2 us  [exchange(): lax.all_to_all(value, axis, 0, 0, tiled=True, axis_index_groups=groups)]
    ppermute x0 -> x1, starting transfers between devices: none -> 9.76 us  [shards(): lax.ppermute(lax.dynamic_index_in_dim(grad_terms, 1 - half, 0, False), 'c...]
    all_to_all x1, blocking collectives: 18 us -> 25.8 us  [exchange(): lax.all_to_all(value, axis, 0, 0, tiled=True, axis_index_groups=groups)]
    ppermute x0 -> x1, waiting for transfers between devices: none -> 4.63 us  [shards(): lax.ppermute(lax.dynamic_index_in_dim(grad_terms, 1 - half, 0, False), 'c...]
    all_to_all x6, starting transfers between devices: 52.3 us -> 47.9 us  [exchange(): lax.all_to_all(value, axis, 0, 0, tiled=True, axis_index_groups=groups)]
  transfers between devices with their start and end apart: 7 -> 8, of which waited for: 7 -> 7; matrix products, arithmetic and copies ran while one was open for 2% -> 2% of each run, Pallas kernels for 4% -> 4%
where the time goes in v4:
time: 204 us; the launch traced here: 203 us
  starting transfers between devices  64.8 us (32%)
  waiting for transfers between devices  54.4 us (27%)
  blocking collectives  51.9 us (25%)
  Pallas kernels  16.3 us (8%)
  local copies, waits for them, and re-layouts  7.36 us (4%)
  other arithmetic  5.46 us (3%)
    all_to_all x6, waiting for transfers between devices, exchange(): lax.all_to_all(value, axis, 0, 0, tiled=True, axis_index_groups=groups)  48.2 us
    all_to_all x6, starting transfers between devices, exchange(): lax.all_to_all(value, axis, 0, 0, tiled=True, axis_index_groups=groups)  47.9 us
    all_gather x1, blocking collectives, shards(): lax.all_gather(jnp.concatenate([weight_rows, tail], axis=1), 'ctx', axis=0)  26.1 us
    all_to_all x1, blocking collectives, exchange(): lax.all_to_all(value, axis, 0, 0, tiled=True, axis_index_groups=groups)  25.8 us
    pallas_call x4, Pallas kernels, call(): pl.pallas_call(kernel, out_shape=[pltpu.HBM(shape, kind) if place is FAR...  16.3 us
    ppermute x1, starting transfers between devices, shards(): lax.ppermute(lax.dynamic_index_in_dim(grad_terms, 1 - half, 0, False), 'c...  9.76 us
    ppermute x1, starting transfers between devices, shards(): sent = lax.ppermute(sent, 'ctx', [(k, k ^ 1) for k in range(blocks)])  7.16 us
    ppermute x1, waiting for transfers between devices, shards(): lax.ppermute(lax.dynamic_index_in_dim(grad_terms, 1 - half, 0, False), 'c...  4.63 us
  transfers between devices with their start and end apart: 8, of which 7 were waited for; matrix products, arithmetic and copies ran while one was open for 2% of the time, Pallas kernels for 4%

profile of v4, /device:TPU:1, one launch (start us, length us, event | category | flops | bytes accessed | tf_op | source)
XLA Modules:
  0.0 202.9 jit_solution(13655146266137847958)
XLA Ops:
  0.7 2.7 %shard_map.181 = bf16[8,72,832]{2,1,0:T(8,128)(2,1)} custom-call(bf16[72,4608]{1,0:T(8,128)(2,1)} %far_weight.1, bf16[72,256]{1,0:T(8,128)(2,1)} %far_cotangent.1), custom_call_target="tpu_custom_call" | custom-call | tf_op jit(solution)/shard_map/pallas_call | solution.py:365
  3.4 0.0 copy-start
  3.4 0.0 copy-start.1
  3.4 0.0 copy-start.2
  3.4 0.0 copy-start.6
  3.4 0.0 copy-start.7
  3.4 6.0 %all-to-all-start = ((bf16[8,72,832]{2,1,0:T(8,128)(2,1)}), bf16[8,72,832]{2,1,0:T(8,128)(2,1)S(1)}, u32[]{:S(2)}, u32[]{:S(2)}) async-start(bf16[8,72,832]{2,1,0:T(8,128)(2,1)} %shard_map.181), calls=%async_computation | async-start | bytes 2064384 | tf_op jit(solution)/shard_map/all_to_all | solution.py:384
  9.4 0.1 copy.56
  9.5 0.1 copy.55
  9.6 0.0 copy-done.12
  9.6 0.1 copy.57
  9.7 0.1 copy.58
  9.9 0.1 fusion.19
  10.0 0.7 pad.24
  10.7 6.3 %shard_map.182 = (f32[64,3072]{1,0:T(8,128)}, f32[64,3072]{1,0:T(8,128)}, f32[64,3072]{1,0:T(8,128)}, f32[64,3072]{1,0:T(8,128)}, f32[12,8,512]{2,1,0:T(8,128)}) custom-call(f32[32,3072]{1,0:T(8,128)S(1)} %copy-done.2, f32[32,64]{1,0:T(8,128)S(1)} %copy-done.7, f32[64,64]{1,0:T(8,128)S(1)} %copy-done.6, f32[8,128]{1,0:T(8,128)S(1)} %pad.25.params, ...), custom_call_target="tpu_custom_call" | custom-call | tf_op jit(solution)/shard_map/pallas_call | solution.py:365
  17.0 1.8 all-to-all-done
  18.8 18.3 %all-to-all-start.1 = ((bf16[12,24,256]{2,1,0:T(8,128)(2,1)}), bf16[12,24,256]{2,1,0:T(8,128)(2,1)S(1)}, u32[]{:S(2)}, u32[]{:S(2)}) async-start(bf16[12,24,256]{2,1,0:T(8,128)(2,1)} %bitcast.6), calls=%async_computation.1 | async-start | bytes 294912 | tf_op jit(solution)/shard_map/all_to_all | solution.py:384
  37.1 0.4 fusion
  37.6 9.8 %collective-permute-start = (bf16[4,72,256]{2,1,0:T(8,128)(2,1)S(1)}, bf16[4,72,256]{2,1,0:T(8,128)(2,1)S(1)}, u32[]{:S(2)}, u32[]{:S(2)}) collective-permute-start(bf16[4,72,256]{2,1,0:T(8,128)(2,1)S(1)} %dynamic-slice_bitcast_fusion.2), channel_id=1, source_target_pairs={{0,32},{1,33},{2,34},{3,35},{4,36},{5,37},{6,38},{7,39},{8,40},{9,... | collective-permute-start | bytes 442376 | tf_op jit(solution)/shard_map/ppermute | solution.py:424
  47.4 4.6 %collective-permute-done = bf16[4,72,256]{2,1,0:T(8,128)(2,1)S(1)} collective-permute-done((bf16[4,72,256]{2,1,0:T(8,128)(2,1)S(1)}, bf16[4,72,256]{2,1,0:T(8,128)(2,1)S(1)}, u32[]{:S(2)}, u32[]{:S(2)}) %collective-permute-start) | collective-permute-done | bytes 147488 | tf_op jit(solution)/shard_map/ppermute | solution.py:424
  52.0 0.7 fusion.1
  52.7 5.9 %all-to-all-start.2 = ((bf16[4,72,256]{2,1,0:T(8,128)(2,1)}), bf16[4,72,256]{2,1,0:T(8,128)(2,1)S(1)}, u32[]{:S(2)}, u32[]{:S(2)}) async-start(bf16[4,72,256]{2,1,0:T(8,128)(2,1)} %fusion.1), calls=%async_computation.2 | async-start | bytes 294912 | tf_op jit(solution)/shard_map/all_to_all | solution.py:384
  58.6 1.6 shard_map.183
  60.3 5.9 %all-to-all-done.2 = bf16[4,72,256]{2,1,0:T(8,128)(2,1)S(1)} async-done(((bf16[4,72,256]{2,1,0:T(8,128)(2,1)}), bf16[4,72,256]{2,1,0:T(8,128)(2,1)S(1)}, u32[]{:S(2)}, u32[]{:S(2)}) %all-to-all-start.2) | async-done | bytes 147488 | tf_op jit(solution)/shard_map/all_to_all | solution.py:384
  66.2 0.8 fusion.6
  67.0 25.8 %all_to_all.35.blocks = bf16[12,16,256]{2,1,0:T(8,128)(2,1)S(1)} all-to-all(bf16[12,16,256]{2,1,0:T(8,128)(2,1)S(1)} %fusion.6), channel_id=1, replica_groups=mesh['ctx'=12,'ch'=64] {'ctx'}, dimensions={0} | all-to-all | bytes 196608 | tf_op jit(solution)/shard_map/all_to_all | solution.py:384
  92.9 5.7 %shard_map.184 = (bf16[12,48,128]{2,1,0:T(8,128)(2,1)}, bf16[96,64]{1,0:T(8,128)(2,1)S(1)}, bf16[16,64]{1,0:T(8,128)(2,1)S(1)}) custom-call(f32[12,8,512]{2,1,0:T(8,128)} %get-tuple-element.22.spectra.kept_spectra, f32[12,24,256]{2,1,0:T(8,128)} %get-tuple-element.24.kept_filtered, f32[12,8,256]{2,1,0:T(8,128)} %get-tuple-element.25.kept_long_out, ...), custom_call_target="tpu_custom_call" | custom-call | tf_op jit(solution)/shard_map/pallas_call | solution.py:365
  98.6 0.1 reshape.120
  98.7 0.8 broadcast_in_dim.27
  99.5 8.2 %all-to-all-start.4 = ((bf16[8,96,256]{2,1,0:T(8,128)(2,1)}), bf16[8,96,256]{2,1,0:T(8,128)(2,1)S(1)}, u32[]{:S(2)}, u32[]{:S(2)}) async-start(bf16[8,96,256]{2,1,0:T(8,128)(2,1)} %broadcast_in_dim.27), calls=%async_computation.4 | async-start | bytes 786432 | tf_op jit(solution)/shard_map/all_to_all | solution.py:384
  107.7 0.1 copy.59
  107.9 0.1 dot_general.20
  108.0 15.7 %all-to-all-done.4 = bf16[8,96,256]{2,1,0:T(8,128)(2,1)S(1)} async-done(((bf16[8,96,256]{2,1,0:T(8,128)(2,1)}), bf16[8,96,256]{2,1,0:T(8,128)(2,1)S(1)}, u32[]{:S(2)}, u32[]{:S(2)}) %all-to-all-start.4) | async-done | bytes 393248 | tf_op jit(solution)/shard_map/all_to_all | solution.py:384
  123.7 0.1 reshape.123
  123.9 0.3 convolution_convert_fusion
  124.2 0.9 pad_maximum_fusion.1
  125.1 7.2 %collective-permute-start.1 = (bf16[6,48,768]{2,1,0:T(8,128)(2,1)}, bf16[6,48,768]{2,1,0:T(8,128)(2,1)S(1)}, u32[]{:S(2)}, u32[]{:S(2)}) collective-permute-start(bf16[6,48,768]{2,1,0:T(8,128)(2,1)} %pad_maximum_fusion.1), channel_id=1, source_target_pairs={{0,64},{64,0},{128,192},{192,128},{256,320},{320,256},{384,448},{4... | collective-permute-start | bytes 1327112 | tf_op jit(solution)/shard_map/ppermute | solution.py:539
  132.3 0.1 dot_general.18
  132.4 1.5 collective-permute-done.1
  133.9 0.1 reduce-precision_convert_fusion
  133.9 0.1 broadcast_select_fusion.1
  134.0 0.3 add_convert_fusion
  134.4 0.9 pad_maximum_fusion
  135.3 6.0 %all-to-all-start.5 = ((bf16[6,48,896]{2,1,0:T(8,128)(2,1)}), bf16[6,48,896]{2,1,0:T(8,128)(2,1)S(1)}, u32[]{:S(2)}, u32[]{:S(2)}) async-start(bf16[6,48,896]{2,1,0:T(8,128)(2,1)} %pad_maximum_fusion), calls=%async_computation.5 | async-start | bytes 1032192 | tf_op jit(solution)/shard_map/all_to_all | solution.py:384
  141.2 0.1 slice.134
  141.3 0.4 convolution_convert_fusion.1
  141.7 19.8 %all-to-all-done.5 = bf16[6,48,896]{2,1,0:T(8,128)(2,1)S(1)} async-done(((bf16[6,48,896]{2,1,0:T(8,128)(2,1)}), bf16[6,48,896]{2,1,0:T(8,128)(2,1)S(1)}, u32[]{:S(2)}, u32[]{:S(2)}) %all-to-all-start.5) | async-done | bytes 516128 | tf_op jit(solution)/shard_map/all_to_all | solution.py:384
  161.5 0.1 slice_reduce_fusion
  161.7 0.1 slice_convert_fusion.1
  161.8 0.1 broadcast_in_dim.29
  161.9 0.8 pad_maximum_fusion.2
  162.7 3.5 %all-to-all-start.6 = ((bf16[8,94,256]{2,1,0:T(8,128)(2,1)}), bf16[8,94,256]{2,1,0:T(8,128)(2,1)S(1)}, u32[]{:S(2)}, u32[]{:S(2)}) async-start(bf16[8,94,256]{2,1,0:T(8,128)(2,1)} %pad_maximum_fusion.2), calls=%async_computation.6 | async-start | bytes 786432 | tf_op jit(solution)/shard_map/all_to_all | solution.py:384
  166.2 0.1 copy.64
  166.3 0.7 reshape.128
  167.0 0.7 copy.67
  167.7 5.0 %all-to-all-done.6 = bf16[8,94,256]{2,1,0:T(8,128)(2,1)S(1)} async-done(((bf16[8,94,256]{2,1,0:T(8,128)(2,1)}), bf16[8,94,256]{2,1,0:T(8,128)(2,1)S(1)}, u32[]{:S(2)}, u32[]{:S(2)}) %all-to-all-start.6) | async-done | bytes 385056 | tf_op jit(solution)/shard_map/all_to_all | solution.py:384
  172.9 0.1 reshape.130
  173.0 0.2 reshape.131
  173.3 26.1 %all-gather.1 = bf16[12,6,4864]{2,1,0:T(8,128)(2,1)S(1)} all-gather(bf16[1,6,4864]{2,1,0:T(8,128)(2,1)S(1)} %maximum_bitcast_fusion), channel_id=2, replica_groups=mesh['ctx'=12,'ch'=64] {'ctx'}, dimensions={0}, use_global_device_ids=true | all-gather | bytes 758784 | tf_op jit(solution)/shard_map/all_gather | solution.py:596
  199.4 0.1 slice_convert_fusion
  199.7 1.3 reshape.137
  200.9 0.7 slice.130
  201.6 0.7 slice.128
  202.3 0.7 slice_reduce_fusion.1
  (74 shorter events, 0.8 us)
Async XLA Ops:
  0.6 8.8 %copy-start.11 = (f32[3,72,3]{1,2,0:T(4,128)S(1)}, f32[3,72,3]{1,2,0:T(4,128)}, u32[]{:S(2)}) copy-start(f32[3,72,3]{1,2,0:T(4,128)} %param.15) | copy-start | bytes 7780
  0.6 8.9 %copy-start.10 = (f32[64,72]{1,0:T(8,128)S(1)}, f32[64,72]{1,0:T(8,128)}, u32[]{:S(2)}) copy-start(f32[64,72]{1,0:T(8,128)} %param.18) | copy-start | bytes 55300
  0.7 9.0 %copy-start.12 = (f32[72]{0:T(128)S(1)}, f32[72]{0:T(128)}, u32[]{:S(2)}) copy-start(f32[72]{0:T(128)} %param.19) | copy-start | bytes 868
  0.7 9.1 %copy-start.13 = (f32[72]{0:T(128)S(1)}, f32[72]{0:T(128)}, u32[]{:S(2)}) copy-start(f32[72]{0:T(128)} %param.20) | copy-start | bytes 868
  0.7 9.2 %copy-start.9 = (bf16[3,72,256]{2,1,0:T(8,128)(2,1)S(1)}, bf16[3,72,256]{2,1,0:T(8,128)(2,1)}, u32[]{:S(2)}) copy-start(bf16[3,72,256]{2,1,0:T(8,128)(2,1)} %param.14) | copy-start | bytes 331780
  3.4 7.3 %copy-start = (bf16[256,512]{1,0:T(8,128)(2,1)S(1)}, bf16[256,512]{1,0:T(8,128)(2,1)}, u32[]{:S(2)}) copy-start(bf16[256,512]{1,0:T(8,128)(2,1)} %constant.86.clone.table_high) | copy-start | bytes 786436
  3.4 7.3 %copy-start.1 = (bf16[256,512]{1,0:T(8,128)(2,1)S(1)}, bf16[256,512]{1,0:T(8,128)(2,1)}, u32[]{:S(2)}) copy-start(bf16[256,512]{1,0:T(8,128)(2,1)} %constant.87.clone.table_low) | copy-start | bytes 786436
  3.4 7.3 %copy-start.2 = (f32[32,3072]{1,0:T(8,128)S(1)}, f32[32,3072]{1,0:T(8,128)}, u32[]{:S(2)}) copy-start(f32[32,3072]{1,0:T(8,128)} %constant.90.clone.features) | copy-start | bytes 1179652
  3.4 7.3 %copy-start.6 = (f32[64,64]{1,0:T(8,128)S(1)}, f32[64,64]{1,0:T(8,128)}, u32[]{:S(2)}) copy-start(f32[64,64]{1,0:T(8,128)} %filter_mid.3) | copy-start | bytes 49156
  3.4 7.3 %copy-start.7 = (f32[32,64]{1,0:T(8,128)S(1)}, f32[32,64]{1,0:T(8,128)}, u32[]{:S(2)}) copy-start(f32[32,64]{1,0:T(8,128)} %filter_in.1) | copy-start | bytes 24580
  3.4 15.4 %all-to-all-start = ((bf16[8,72,832]{2,1,0:T(8,128)(2,1)}), bf16[8,72,832]{2,1,0:T(8,128)(2,1)S(1)}, u32[]{:S(2)}, u32[]{:S(2)}) async-start(bf16[8,72,832]{2,1,0:T(8,128)(2,1)} %shard_map.181), calls=%async_computation | async-start | bytes 2064384 | tf_op jit(solution)/shard_map/all_to_all | solution.py:384
  18.8 33.9 %all-to-all-start.1 = ((bf16[12,24,256]{2,1,0:T(8,128)(2,1)}), bf16[12,24,256]{2,1,0:T(8,128)(2,1)S(1)}, u32[]{:S(2)}, u32[]{:S(2)}) async-start(bf16[12,24,256]{2,1,0:T(8,128)(2,1)} %bitcast.6), calls=%async_computation.1 | async-start | bytes 294912 | tf_op jit(solution)/shard_map/all_to_all | solution.py:384
  37.1 21.5 %copy-start.3 = (bf16[512,256]{1,0:T(8,128)(2,1)S(1)}, bf16[512,256]{1,0:T(8,128)(2,1)}, u32[]{:S(2)}) copy-start(bf16[512,256]{1,0:T(8,128)(2,1)} %constant.88.clone.back_high) | copy-start | bytes 786436
  37.1 21.5 %copy-start.4 = (bf16[512,256]{1,0:T(8,128)(2,1)S(1)}, bf16[512,256]{1,0:T(8,128)(2,1)}, u32[]{:S(2)}) copy-start(bf16[512,256]{1,0:T(8,128)(2,1)} %constant.89.clone.back_low) | copy-start | bytes 786436
  37.1 21.5 %copy-start.5 = (f32[12,8,512]{2,1,0:T(8,128)S(1)}, f32[12,8,512]{2,1,0:T(8,128)}, u32[]{:S(2)}) copy-start(f32[12,8,512]{2,1,0:T(8,128)} %get-tuple-element.22.spectra.kept_spectra) | copy-start | bytes 589828
  37.6 14.4 %collective-permute-start = (bf16[4,72,256]{2,1,0:T(8,128)(2,1)S(1)}, bf16[4,72,256]{2,1,0:T(8,128)(2,1)S(1)}, u32[]{:S(2)}, u32[]{:S(2)}) collective-permute-start(bf16[4,72,256]{2,1,0:T(8,128)(2,1)S(1)} %dynamic-slice_bitcast_fusion.2), channel_id=1, source_target_pairs={{0,32},{1,33},{2,34},{3,35},{4,36},{5,37},{6,38},{7,39},{8,40},{9,... | collective-permute-start | bytes 442376 | tf_op jit(solution)/shard_map/ppermute | solution.py:424
  52.7 13.5 %all-to-all-start.2 = ((bf16[4,72,256]{2,1,0:T(8,128)(2,1)}), bf16[4,72,256]{2,1,0:T(8,128)(2,1)S(1)}, u32[]{:S(2)}, u32[]{:S(2)}) async-start(bf16[4,72,256]{2,1,0:T(8,128)(2,1)} %fusion.1), calls=%async_computation.2 | async-start | bytes 294912 | tf_op jit(solution)/shard_map/all_to_all | solution.py:384
  98.7 9.2 %copy-start.8 = (bf16[12,48,128]{2,1,0:T(8,128)(2,1)S(1)}, bf16[12,48,128]{2,1,0:T(8,128)(2,1)}, u32[]{:S(2)}) copy-start(bf16[12,48,128]{2,1,0:T(8,128)(2,1)} %get-tuple-element.33) | copy-start | bytes 442372
  99.5 24.2 %all-to-all-start.4 = ((bf16[8,96,256]{2,1,0:T(8,128)(2,1)}), bf16[8,96,256]{2,1,0:T(8,128)(2,1)S(1)}, u32[]{:S(2)}, u32[]{:S(2)}) async-start(bf16[8,96,256]{2,1,0:T(8,128)(2,1)} %broadcast_in_dim.27), calls=%async_computation.4 | async-start | bytes 786432 | tf_op jit(solution)/shard_map/all_to_all | solution.py:384
  125.1 8.8 %collective-permute-start.1 = (bf16[6,48,768]{2,1,0:T(8,128)(2,1)}, bf16[6,48,768]{2,1,0:T(8,128)(2,1)S(1)}, u32[]{:S(2)}, u32[]{:S(2)}) collective-permute-start(bf16[6,48,768]{2,1,0:T(8,128)(2,1)} %pad_maximum_fusion.1), channel_id=1, source_target_pairs={{0,64},{64,0},{128,192},{192,128},{256,320},{320,256},{384,448},{4... | collective-permute-start | bytes 1327112 | tf_op jit(solution)/shard_map/ppermute | solution.py:539
  135.3 26.2 %all-to-all-start.5 = ((bf16[6,48,896]{2,1,0:T(8,128)(2,1)}), bf16[6,48,896]{2,1,0:T(8,128)(2,1)S(1)}, u32[]{:S(2)}, u32[]{:S(2)}) async-start(bf16[6,48,896]{2,1,0:T(8,128)(2,1)} %pad_maximum_fusion), calls=%async_computation.5 | async-start | bytes 1032192 | tf_op jit(solution)/shard_map/all_to_all | solution.py:384
  162.7 10.0 %all-to-all-start.6 = ((bf16[8,94,256]{2,1,0:T(8,128)(2,1)}), bf16[8,94,256]{2,1,0:T(8,128)(2,1)S(1)}, u32[]{:S(2)}, u32[]{:S(2)}) async-start(bf16[8,94,256]{2,1,0:T(8,128)(2,1)} %pad_maximum_fusion.2), calls=%async_computation.6 | async-start | bytes 786432 | tf_op jit(solution)/shard_map/all_to_all | solution.py:384

commit v5 on v4

--- a/solution.py
+++ b/solution.py
@@ -402,6 +402,19 @@
     places = side // 2
     place_groups = [group[h * places : (h + 1) * places] for group in far_groups for h in range(2)]
     half = lax.axis_index("ch") // (places * side)
+    chips = blocks // 2
+    core = me % 2
+    core_pairs = [(k, k ^ 1) for k in range(blocks)]
+    chip_groups = [[2 * z + c for z in range(chips)] for c in range(2)]
+
+    def in_order(here, there):
+        second = core == 1
+        return [jnp.where(second, there, here), jnp.where(second, here, there)]
+
+    def between_cores(value, axis):
+        here = lax.dynamic_index_in_dim(value, core, axis, False)
+        there = lax.dynamic_index_in_dim(value, 1 - core, axis, False)
+        return in_order(here, lax.ppermute(there, "ctx", core_pairs))
     group = side * channels
     pad_rows = ROWS - share
     tables = [jnp.asarray(t) for t in transform_tables()]
@@ -420,7 +433,8 @@
     grad_terms = lax.dot_general(
         weight, cotangent, (((0,), (0,)), ((), ())), preferred_element_type=f32
     ).astype(bf16)
-    grad_terms = grad_terms.reshape(2, places, channels, tokens)
+    grad_terms = between_cores(grad_terms.reshape(side, chips, 2, share, tokens), 2)
+    grad_terms = jnp.stack(grad_terms, axis=1).reshape(2, places, channels, tokens)
     received = lax.ppermute(
         lax.dynamic_index_in_dim(grad_terms, 1 - half, 0, False),
         "ch",
@@ -459,8 +473,10 @@
 
     by_share = streams.reshape(3, blocks, share, tokens).transpose(1, 0, 2, 3)
     by_share = jnp.pad(by_share, ((0, 0), (0, 0), (0, pad_rows), (0, 0)))
+    by_share = between_cores(by_share.reshape(chips, 2, 3 * ROWS, tokens), 1)
+    by_share = jnp.concatenate(by_share, axis=1)
     by_share, spectra = lax.optimization_barrier((by_share, spectra))
-    sequence = exchange(by_share.reshape(blocks, 3 * ROWS, tokens), "ctx")
+    sequence = exchange(by_share, "ctx", chip_groups).reshape(blocks, 3 * ROWS, tokens)
     kept = [
         ((blocks * ROWS, tokens), bf16),
         ((blocks, 3 * ROWS, tokens), f32),
@@ -472,9 +488,11 @@
         *near(sequence, params, spectra, *tables),
     )
 
-    turned = jnp.pad(grad_gated.reshape(blocks, share, tokens), ((0, 0), (0, pad_rows), (0, 0)))
-    turned = jnp.concatenate([gated.reshape(blocks, ROWS, tokens), turned], axis=1)
-    turned = exchange(turned, "ctx")
+    turned = grad_gated.reshape(2, chips, share, tokens).transpose(1, 0, 2, 3)
+    turned = jnp.pad(turned, ((0, 0), (0, 0), (0, pad_rows), (0, 0)))
+    first, second = between_cores(gated.reshape(chips, 2, ROWS, tokens), 1)
+    turned = jnp.concatenate([first, turned[:, 0], second, turned[:, 1]], axis=1)
+    turned = exchange(turned, "ctx", chip_groups).reshape(blocks, 2 * ROWS, tokens)
     own_gated = turned[:, :share, :].reshape(channels, tokens)
 
     packed_streams = ((blocks, 6 * ROWS, tokens // 2), bf16)
@@ -508,8 +526,6 @@
         high = lax.reduce_precision(value, 8, 7)
         return high.astype(bf16), (value - high).astype(bf16)
 
-    chips = blocks // 2
-    core = me % 2
     rows = side * share
     portion = (band_rows + hidden) // blocks
     by_core = cotangent.reshape(side, chips, 2, share, tokens).transpose(2, 1, 0, 3, 4)
@@ -536,7 +552,7 @@
     last_here = jnp.broadcast_to(grad_last[None], (chips,) + grad_last.shape)
     terms, shared_part, packed = parts_for(1 - core)
     sent = joined(terms, shared_part, [last_here], [packed])
-    sent = lax.ppermute(sent, "ctx", [(k, k ^ 1) for k in range(blocks)])
+    sent = lax.ppermute(sent, "ctx", core_pairs)
     terms, shared_part, packed = parts_for(core)
     terms = terms + sent[:, :, :group].astype(f32)
     small = sent[:, :, group : group + hidden]
@@ -548,15 +564,10 @@
     last_at = 2 * portion
     last_there = small[:, last_at : last_at + 2 * ROWS]
     packed_there = sent[:, :, group + hidden :]
-    second = core == 1
-
-    def in_order(here, there):
-        return [jnp.where(second, there, here), jnp.where(second, here, there)]
-
     sent = joined(
         terms, shared_part, in_order(last_here, last_there), in_order(packed, packed_there)
     )
-    sent = exchange(sent, "ctx", [[2 * z + c for z in range(chips)] for c in range(2)])
+    sent = exchange(sent, "ctx", chip_groups)
     weight_share = jnp.sum(sent[:, :, :group].astype(f32), axis=0).astype(bf16)
     small = sent[:, :, group : group + hidden].astype(f32)
     shared = jnp.sum(small[:, :portion] + small[:, portion : 2 * portion], axis=0)

time: 204 us -> 203 us (level)
  starting transfers between devices: 64.8 us -> 74 us
  waiting for transfers between devices: 54.4 us -> 48.6 us
  blocking collectives: 51.9 us -> 46.3 us
    ppermute x1 -> x4, starting transfers between devices: 7.16 us -> 25.4 us  [the longest x3 16.9 us: between_cores(): return in_order(here, lax.ppermute(there, 'ctx', core_pairs))]
    all_to_all x6, starting transfers between devices: 47.9 us -> 38.8 us  [exchange(): lax.all_to_all(value, axis, 0, 0, tiled=True, axis_index_groups=groups)]
    all_to_all x1, blocking collectives: 25.8 us -> 20.2 us  [exchange(): lax.all_to_all(value, axis, 0, 0, tiled=True, axis_index_groups=groups)]
    ppermute x1, waiting for transfers between devices: 4.63 us -> 0.01 us  [shards(): lax.ppermute(lax.dynamic_index_in_dim(grad_terms, 1 - half, 0, False), 'c...]
  transfers between devices with their start and end apart: 8 -> 11, of which waited for: 7 -> 5; matrix products, arithmetic and copies ran while one was open for 2% -> 3% of each run, Pallas kernels for 4% -> 4%
where the time goes in v5:
time: 203 us; the launch traced here: 202 us
  starting transfers between devices  74 us (36%)
  waiting for transfers between devices  48.6 us (24%)
  blocking collectives  46.3 us (23%)
  Pallas kernels  16.3 us (8%)
  local copies, waits for them, and re-layouts  8.49 us (4%)
  other arithmetic  5.57 us (3%)
    all_to_all x6, waiting for transfers between devices, exchange(): lax.all_to_all(value, axis, 0, 0, tiled=True, axis_index_groups=groups)  47.1 us
    all_to_all x6, starting transfers between devices, exchange(): lax.all_to_all(value, axis, 0, 0, tiled=True, axis_index_groups=groups)  38.8 us
    all_gather x1, blocking collectives, shards(): lax.all_gather(jnp.concatenate([weight_rows, tail], axis=1), 'ctx', axis=0)  26.1 us
    all_to_all x1, blocking collectives, exchange(): lax.all_to_all(value, axis, 0, 0, tiled=True, axis_index_groups=groups)  20.2 us
    ppermute x3, starting transfers between devices, between_cores(): return in_order(here, lax.ppermute(there, 'ctx', core_pairs))  16.9 us
    pallas_call x4, Pallas kernels, call(): pl.pallas_call(kernel, out_shape=[pltpu.HBM(shape, kind) if place is FAR...  16.3 us
    ppermute x1, starting transfers between devices, shards(): lax.ppermute(lax.dynamic_index_in_dim(grad_terms, 1 - half, 0, False), 'c...  9.76 us
    ppermute x1, starting transfers between devices, shards(): sent = lax.ppermute(sent, 'ctx', core_pairs)  8.5 us
  transfers between devices with their start and end apart: 11, of which 5 were waited for; matrix products, arithmetic and copies ran while one was open for 3% of the time, Pallas kernels for 4%

profile of v5, /device:TPU:1, one launch (start us, length us, event | category | flops | bytes accessed | tf_op | source)
XLA Modules:
  0.0 202.1 jit_solution(2433152480844828999)
XLA Ops:
  0.6 2.7 %shard_map.181 = bf16[8,72,832]{2,1,0:T(8,128)(2,1)} custom-call(bf16[72,4608]{1,0:T(8,128)(2,1)} %far_weight.1, bf16[72,256]{1,0:T(8,128)(2,1)} %far_cotangent.1), custom_call_target="tpu_custom_call" | custom-call | tf_op jit(solution)/shard_map/pallas_call | solution.py:365
  3.4 6.0 %all-to-all-start = ((bf16[8,72,832]{2,1,0:T(8,128)(2,1)}), bf16[8,72,832]{2,1,0:T(8,128)(2,1)S(1)}, u32[]{:S(2)}, u32[]{:S(2)}) async-start(bf16[8,72,832]{2,1,0:T(8,128)(2,1)} %shard_map.181), calls=%async_computation | async-start | bytes 2064384 | tf_op jit(solution)/shard_map/all_to_all | solution.py:384
  9.6 10.2 %collective-permute-start = (bf16[6,24,256]{2,1,0:T(8,128)(2,1)S(1)}, bf16[6,24,256]{2,1,0:T(8,128)(2,1)S(1)}, u32[]{:S(2)}, u32[]{:S(2)}) collective-permute-start(bf16[6,24,256]{2,1,0:T(8,128)(2,1)S(1)} %dynamic-slice_bitcast_fusion.4), channel_id=1, source_target_pairs={{0,64},{64,0},{128,192},{192,128},{256,320},{320,256},{384,448},{4... | collective-permute-start | bytes 221192 | tf_op jit(solution)/shard_map/ppermute | solution.py:417
  19.8 0.1 copy.56
  19.9 0.1 copy.55
  20.0 0.1 copy.57
  20.1 0.1 copy.58
  20.2 0.1 fusion.21
  20.3 6.3 %shard_map.182 = (f32[64,3072]{1,0:T(8,128)}, f32[64,3072]{1,0:T(8,128)}, f32[64,3072]{1,0:T(8,128)}, f32[64,3072]{1,0:T(8,128)}, f32[12,8,512]{2,1,0:T(8,128)}) custom-call(f32[32,3072]{1,0:T(8,128)S(1)} %copy-done.2, f32[32,64]{1,0:T(8,128)S(1)} %copy-done.7, f32[64,64]{1,0:T(8,128)S(1)} %copy-done.6, f32[8,128]{1,0:T(8,128)S(1)} %pad.25.params, ...), custom_call_target="tpu_custom_call" | custom-call | tf_op jit(solution)/shard_map/pallas_call | solution.py:365
  26.6 0.4 fusion
  27.0 0.1 reshape.127
  27.3 3.5 %collective-permute-start.2 = (bf16[8,6,6,256]{3,0,2,1:T(8,128)(2,1)S(1)}, bf16[8,6,6,256]{3,0,2,1:T(8,128)(2,1)S(1)}, u32[]{:S(2)}, u32[]{:S(2)}) collective-permute-start(bf16[8,6,6,256]{3,0,2,1:T(8,128)(2,1)S(1)} %bitcast.130), channel_id=1, source_target_pairs={{0,64},{64,0},{128,192},{192,128},{256,320},{320,256},{384,448},{4... | collective-permute-start | bytes 442376 | tf_op jit(solution)/shard_map/ppermute | solution.py:417
  30.8 0.7 pad_maximum_fusion.4
  31.5 8.7 %all-to-all-start.1 = ((bf16[6,48,256]{2,1,0:T(8,128)(2,1)}), bf16[6,48,256]{2,1,0:T(8,128)(2,1)S(1)}, u32[]{:S(2)}, u32[]{:S(2)}) async-start(bf16[6,48,256]{2,1,0:T(8,128)(2,1)} %pad_maximum_fusion.4), calls=%async_computation.1 | async-start | bytes 294912 | tf_op jit(solution)/shard_map/all_to_all | solution.py:384
  40.3 0.1 fusion.5
  40.4 0.1 reshape.128
  40.4 0.1 dynamic-slice_bitcast_fusion.2
  40.5 9.8 %collective-permute-start.3 = (bf16[4,72,256]{2,0,1:T(4,128)(2,1)S(1)}, bf16[4,72,256]{2,0,1:T(4,128)(2,1)S(1)}, u32[]{:S(2)}, u32[]{:S(2)}) collective-permute-start(bf16[4,72,256]{2,0,1:T(4,128)(2,1)S(1)} %dynamic-slice_bitcast_fusion.2), channel_id=1, source_target_pairs={{0,32},{1,33},{2,34},{3,35},{4,36},{5,37},{6,38},{7,39},{8,40},{9,... | collective-permute-start | bytes 442376 | tf_op jit(solution)/shard_map/ppermute | solution.py:438
  50.3 1.6 shard_map.183
  52.0 0.7 dynamic-slice_bitcast_fusion.5
  52.7 3.3 %collective-permute-start.1 = (bf16[6,8,256]{2,1,0:T(8,128)(2,1)S(1)}, bf16[6,8,256]{2,1,0:T(8,128)(2,1)S(1)}, u32[]{:S(2)}, u32[]{:S(2)}) collective-permute-start(bf16[6,8,256]{2,1,0:T(8,128)(2,1)S(1)} %dynamic-slice_bitcast_fusion.5), channel_id=1, source_target_pairs={{0,64},{64,0},{128,192},{192,128},{256,320},{320,256},{384,448},{4... | collective-permute-start | bytes 73736 | tf_op jit(solution)/shard_map/ppermute | solution.py:417
  56.0 0.1 fusion.1
  56.1 0.7 copy.61
  56.8 5.9 %all-to-all-start.2 = ((bf16[4,72,256]{2,1,0:T(8,128)(2,1)}), bf16[4,72,256]{2,1,0:T(8,128)(2,1)S(1)}, u32[]{:S(2)}, u32[]{:S(2)}) async-start(bf16[4,72,256]{2,1,0:T(8,128)(2,1)} %copy.61), calls=%async_computation.2 | async-start | bytes 294912 | tf_op jit(solution)/shard_map/all_to_all | solution.py:384
  62.7 0.7 bitcast_select_fusion.7
  63.5 6.9 %all-to-all-done.2 = bf16[4,72,256]{2,1,0:T(8,128)(2,1)S(1)} async-done(((bf16[4,72,256]{2,1,0:T(8,128)(2,1)}), bf16[4,72,256]{2,1,0:T(8,128)(2,1)S(1)}, u32[]{:S(2)}, u32[]{:S(2)}) %all-to-all-start.2) | async-done | bytes 147488 | tf_op jit(solution)/shard_map/all_to_all | solution.py:384
  70.4 20.2 %all_to_all.35 = bf16[6,32,256]{2,1,0:T(8,128)(2,1)S(1)} all-to-all(bf16[6,32,256]{2,1,0:T(8,128)(2,1)S(1)} %pad_maximum_fusion.5), channel_id=1, replica_groups={{0,128,256,384,512,640},{64,192,320,448,576,704},{1,129,257,385,513,641..., dimensions={0} | all-to-all | bytes 196608 | tf_op jit(solution)/shard_map/all_to_all | solution.py:384
  90.7 5.7 %shard_map.184 = (bf16[12,48,128]{2,1,0:T(8,128)(2,1)}, bf16[96,64]{1,0:T(8,128)(2,1)S(1)}, bf16[16,64]{1,0:T(8,128)(2,1)S(1)}) custom-call(f32[12,8,512]{2,1,0:T(8,128)} %get-tuple-element.22.spectra.kept_spectra, f32[12,24,256]{2,1,0:T(8,128)} %get-tuple-element.24.kept_filtered, f32[12,8,256]{2,1,0:T(8,128)} %get-tuple-element.25.kept_long_out, ...), custom_call_target="tpu_custom_call" | custom-call | tf_op jit(solution)/shard_map/pallas_call | solution.py:365
  96.4 0.1 reshape.132
  96.5 0.8 broadcast_in_dim.27
  97.3 9.2 %all-to-all-start.4 = ((bf16[8,96,256]{2,1,0:T(8,128)(2,1)}), bf16[8,96,256]{2,1,0:T(8,128)(2,1)S(1)}, u32[]{:S(2)}, u32[]{:S(2)}) async-start(bf16[8,96,256]{2,1,0:T(8,128)(2,1)} %broadcast_in_dim.27), calls=%async_computation.4 | async-start | bytes 786432 | tf_op jit(solution)/shard_map/all_to_all | solution.py:384
  106.4 0.1 copy.62
  106.6 0.1 dot_general.20
  106.7 15.4 %all-to-all-done.4 = bf16[8,96,256]{2,1,0:T(8,128)(2,1)S(1)} async-done(((bf16[8,96,256]{2,1,0:T(8,128)(2,1)}), bf16[8,96,256]{2,1,0:T(8,128)(2,1)S(1)}, u32[]{:S(2)}, u32[]{:S(2)}) %all-to-all-start.4) | async-done | bytes 393248 | tf_op jit(solution)/shard_map/all_to_all | solution.py:384
  122.1 0.1 reshape.135
  122.2 0.3 convolution_convert_fusion
  122.5 0.9 pad_maximum_fusion.1
  123.4 8.5 %collective-permute-start.4 = (bf16[6,48,768]{2,1,0:T(8,128)(2,1)}, bf16[6,48,768]{2,1,0:T(8,128)(2,1)S(1)}, u32[]{:S(2)}, u32[]{:S(2)}) collective-permute-start(bf16[6,48,768]{2,1,0:T(8,128)(2,1)} %pad_maximum_fusion.1), channel_id=1, source_target_pairs={{0,64},{64,0},{128,192},{192,128},{256,320},{320,256},{384,448},{4... | collective-permute-start | bytes 1327112 | tf_op jit(solution)/shard_map/ppermute | solution.py:555
  132.0 1.5 collective-permute-done.4
  133.5 0.1 reduce-precision_convert_fusion
  133.6 0.1 broadcast_select_fusion.1
  133.7 0.3 add_convert_fusion
  134.0 0.9 pad_maximum_fusion
  134.9 5.5 %all-to-all-start.5 = ((bf16[6,48,896]{2,1,0:T(8,128)(2,1)}), bf16[6,48,896]{2,1,0:T(8,128)(2,1)S(1)}, u32[]{:S(2)}, u32[]{:S(2)}) async-start(bf16[6,48,896]{2,1,0:T(8,128)(2,1)} %pad_maximum_fusion), calls=%async_computation.5 | async-start | bytes 1032192 | tf_op jit(solution)/shard_map/all_to_all | solution.py:384
  140.5 0.1 slice.142
  140.5 0.4 convolution_convert_fusion.1
  140.9 19.8 %all-to-all-done.5 = bf16[6,48,896]{2,1,0:T(8,128)(2,1)S(1)} async-done(((bf16[6,48,896]{2,1,0:T(8,128)(2,1)}), bf16[6,48,896]{2,1,0:T(8,128)(2,1)S(1)}, u32[]{:S(2)}, u32[]{:S(2)}) %all-to-all-start.5) | async-done | bytes 516128 | tf_op jit(solution)/shard_map/all_to_all | solution.py:384
  160.7 0.1 slice_reduce_fusion
  160.9 0.1 slice_convert_fusion.1
  161.0 0.1 broadcast_in_dim.29
  161.1 0.8 pad_maximum_fusion.2
  161.9 3.5 %all-to-all-start.6 = ((bf16[8,94,256]{2,1,0:T(8,128)(2,1)}), bf16[8,94,256]{2,1,0:T(8,128)(2,1)S(1)}, u32[]{:S(2)}, u32[]{:S(2)}) async-start(bf16[8,94,256]{2,1,0:T(8,128)(2,1)} %pad_maximum_fusion.2), calls=%async_computation.6 | async-start | bytes 786432 | tf_op jit(solution)/shard_map/all_to_all | solution.py:384
  165.4 0.1 copy.67
  165.5 0.7 reshape.140
  166.2 0.7 copy.70
  166.9 5.0 %all-to-all-done.6 = bf16[8,94,256]{2,1,0:T(8,128)(2,1)S(1)} async-done(((bf16[8,94,256]{2,1,0:T(8,128)(2,1)}), bf16[8,94,256]{2,1,0:T(8,128)(2,1)S(1)}, u32[]{:S(2)}, u32[]{:S(2)}) %all-to-all-start.6) | async-done | bytes 385056 | tf_op jit(solution)/shard_map/all_to_all | solution.py:384
  172.1 0.1 reshape.142
  172.2 0.2 reshape.143
  172.5 26.1 %all-gather.1 = bf16[12,6,4864]{2,1,0:T(8,128)(2,1)S(1)} all-gather(bf16[1,6,4864]{2,1,0:T(8,128)(2,1)S(1)} %maximum_bitcast_fusion), channel_id=2, replica_groups=mesh['ctx'=12,'ch'=64] {'ctx'}, dimensions={0}, use_global_device_ids=true | all-gather | bytes 758784 | tf_op jit(solution)/shard_map/all_gather | solution.py:607
  198.7 0.1 slice_convert_fusion
  198.9 0.7 slice.136
  199.5 0.7 slice.138
  200.2 1.3 reshape.149
  201.5 0.7 slice_reduce_fusion.1
  (93 shorter events, 1.1 us)
Async XLA Ops:
  0.6 8.8 %copy-start.9 = (bf16[3,72,256]{2,1,0:T(8,128)(2,1)S(1)}, bf16[3,72,256]{2,1,0:T(8,128)(2,1)}, u32[]{:S(2)}) copy-start(bf16[3,72,256]{2,1,0:T(8,128)(2,1)} %param.14) | copy-start | bytes 331780
  3.3 16.4 %copy-start.11 = (f32[3,72,3]{1,2,0:T(4,128)S(1)}, f32[3,72,3]{1,2,0:T(4,128)}, u32[]{:S(2)}) copy-start(f32[3,72,3]{1,2,0:T(4,128)} %param.15) | copy-start | bytes 7780
  3.3 16.6 %copy-start.10 = (f32[64,72]{1,0:T(8,128)S(1)}, f32[64,72]{1,0:T(8,128)}, u32[]{:S(2)}) copy-start(f32[64,72]{1,0:T(8,128)} %param.18) | copy-start | bytes 55300
  3.3 16.6 %copy-start.12 = (f32[72]{0:T(128)S(1)}, f32[72]{0:T(128)}, u32[]{:S(2)}) copy-start(f32[72]{0:T(128)} %param.19) | copy-start | bytes 868
  3.3 16.7 %copy-start.13 = (f32[72]{0:T(128)S(1)}, f32[72]{0:T(128)}, u32[]{:S(2)}) copy-start(f32[72]{0:T(128)} %param.20) | copy-start | bytes 868
  3.4 16.9 %copy-start = (bf16[256,512]{1,0:T(8,128)(2,1)S(1)}, bf16[256,512]{1,0:T(8,128)(2,1)}, u32[]{:S(2)}) copy-start(bf16[256,512]{1,0:T(8,128)(2,1)} %constant.105.clone.table_low) | copy-start | bytes 786436
  3.4 16.9 %copy-start.1 = (bf16[256,512]{1,0:T(8,128)(2,1)S(1)}, bf16[256,512]{1,0:T(8,128)(2,1)}, u32[]{:S(2)}) copy-start(bf16[256,512]{1,0:T(8,128)(2,1)} %constant.104.clone.table_high) | copy-start | bytes 786436
  3.4 16.9 %copy-start.2 = (f32[32,3072]{1,0:T(8,128)S(1)}, f32[32,3072]{1,0:T(8,128)}, u32[]{:S(2)}) copy-start(f32[32,3072]{1,0:T(8,128)} %constant.108.clone.features) | copy-start | bytes 1179652
  3.4 16.9 %copy-start.6 = (f32[64,64]{1,0:T(8,128)S(1)}, f32[64,64]{1,0:T(8,128)}, u32[]{:S(2)}) copy-start(f32[64,64]{1,0:T(8,128)} %filter_mid.3) | copy-start | bytes 49156
  3.4 16.9 %copy-start.7 = (f32[32,64]{1,0:T(8,128)S(1)}, f32[32,64]{1,0:T(8,128)}, u32[]{:S(2)}) copy-start(f32[32,64]{1,0:T(8,128)} %filter_in.1) | copy-start | bytes 24580
  3.4 23.2 %all-to-all-start = ((bf16[8,72,832]{2,1,0:T(8,128)(2,1)}), bf16[8,72,832]{2,1,0:T(8,128)(2,1)S(1)}, u32[]{:S(2)}, u32[]{:S(2)}) async-start(bf16[8,72,832]{2,1,0:T(8,128)(2,1)} %shard_map.181), calls=%async_computation | async-start | bytes 2064384 | tf_op jit(solution)/shard_map/all_to_all | solution.py:384
  9.6 21.2 %collective-permute-start = (bf16[6,24,256]{2,1,0:T(8,128)(2,1)S(1)}, bf16[6,24,256]{2,1,0:T(8,128)(2,1)S(1)}, u32[]{:S(2)}, u32[]{:S(2)}) collective-permute-start(bf16[6,24,256]{2,1,0:T(8,128)(2,1)S(1)} %dynamic-slice_bitcast_fusion.4), channel_id=1, source_target_pairs={{0,64},{64,0},{128,192},{192,128},{256,320},{320,256},{384,448},{4... | collective-permute-start | bytes 221192 | tf_op jit(solution)/shard_map/ppermute | solution.py:417
  27.2 23.1 %copy-start.3 = (bf16[512,256]{1,0:T(8,128)(2,1)S(1)}, bf16[512,256]{1,0:T(8,128)(2,1)}, u32[]{:S(2)}) copy-start(bf16[512,256]{1,0:T(8,128)(2,1)} %constant.107.clone.back_low) | copy-start | bytes 786436
  27.2 23.1 %copy-start.4 = (bf16[512,256]{1,0:T(8,128)(2,1)S(1)}, bf16[512,256]{1,0:T(8,128)(2,1)}, u32[]{:S(2)}) copy-start(bf16[512,256]{1,0:T(8,128)(2,1)} %constant.106.clone.back_high) | copy-start | bytes 786436
  27.2 23.1 %copy-start.5 = (f32[12,8,512]{2,1,0:T(8,128)S(1)}, f32[12,8,512]{2,1,0:T(8,128)}, u32[]{:S(2)}) copy-start(f32[12,8,512]{2,1,0:T(8,128)} %get-tuple-element.22.spectra.kept_spectra) | copy-start | bytes 589828
  27.3 13.0 %collective-permute-start.2 = (bf16[8,6,6,256]{3,0,2,1:T(8,128)(2,1)S(1)}, bf16[8,6,6,256]{3,0,2,1:T(8,128)(2,1)S(1)}, u32[]{:S(2)}, u32[]{:S(2)}) collective-permute-start(bf16[8,6,6,256]{3,0,2,1:T(8,128)(2,1)S(1)} %bitcast.130), channel_id=1, source_target_pairs={{0,64},{64,0},{128,192},{192,128},{256,320},{320,256},{384,448},{4... | collective-permute-start | bytes 442376 | tf_op jit(solution)/shard_map/ppermute | solution.py:417
  31.5 18.8 %all-to-all-start.1 = ((bf16[6,48,256]{2,1,0:T(8,128)(2,1)}), bf16[6,48,256]{2,1,0:T(8,128)(2,1)S(1)}, u32[]{:S(2)}, u32[]{:S(2)}) async-start(bf16[6,48,256]{2,1,0:T(8,128)(2,1)} %pad_maximum_fusion.4), calls=%async_computation.1 | async-start | bytes 294912 | tf_op jit(solution)/shard_map/all_to_all | solution.py:384
  40.5 15.5 %collective-permute-start.3 = (bf16[4,72,256]{2,0,1:T(4,128)(2,1)S(1)}, bf16[4,72,256]{2,0,1:T(4,128)(2,1)S(1)}, u32[]{:S(2)}, u32[]{:S(2)}) collective-permute-start(bf16[4,72,256]{2,0,1:T(4,128)(2,1)S(1)} %dynamic-slice_bitcast_fusion.2), channel_id=1, source_target_pairs={{0,32},{1,33},{2,34},{3,35},{4,36},{5,37},{6,38},{7,39},{8,40},{9,... | collective-permute-start | bytes 442376 | tf_op jit(solution)/shard_map/ppermute | solution.py:438
  52.7 10.0 %collective-permute-start.1 = (bf16[6,8,256]{2,1,0:T(8,128)(2,1)S(1)}, bf16[6,8,256]{2,1,0:T(8,128)(2,1)S(1)}, u32[]{:S(2)}, u32[]{:S(2)}) collective-permute-start(bf16[6,8,256]{2,1,0:T(8,128)(2,1)S(1)} %dynamic-slice_bitcast_fusion.5), channel_id=1, source_target_pairs={{0,64},{64,0},{128,192},{192,128},{256,320},{320,256},{384,448},{4... | collective-permute-start | bytes 73736 | tf_op jit(solution)/shard_map/ppermute | solution.py:417
  56.8 13.6 %all-to-all-start.2 = ((bf16[4,72,256]{2,1,0:T(8,128)(2,1)}), bf16[4,72,256]{2,1,0:T(8,128)(2,1)S(1)}, u32[]{:S(2)}, u32[]{:S(2)}) async-start(bf16[4,72,256]{2,1,0:T(8,128)(2,1)} %copy.61), calls=%async_computation.2 | async-start | bytes 294912 | tf_op jit(solution)/shard_map/all_to_all | solution.py:384
  96.5 10.2 %copy-start.8 = (bf16[12,48,128]{2,1,0:T(8,128)(2,1)S(1)}, bf16[12,48,128]{2,1,0:T(8,128)(2,1)}, u32[]{:S(2)}) copy-start(bf16[12,48,128]{2,1,0:T(8,128)(2,1)} %get-tuple-element.33) | copy-start | bytes 442372
  97.3 24.8 %all-to-all-start.4 = ((bf16[8,96,256]{2,1,0:T(8,128)(2,1)}), bf16[8,96,256]{2,1,0:T(8,128)(2,1)S(1)}, u32[]{:S(2)}, u32[]{:S(2)}) async-start(bf16[8,96,256]{2,1,0:T(8,128)(2,1)} %broadcast_in_dim.27), calls=%async_computation.4 | async-start | bytes 786432 | tf_op jit(solution)/shard_map/all_to_all | solution.py:384
  123.4 10.1 %collective-permute-start.4 = (bf16[6,48,768]{2,1,0:T(8,128)(2,1)}, bf16[6,48,768]{2,1,0:T(8,128)(2,1)S(1)}, u32[]{:S(2)}, u32[]{:S(2)}) collective-permute-start(bf16[6,48,768]{2,1,0:T(8,128)(2,1)} %pad_maximum_fusion.1), channel_id=1, source_target_pairs={{0,64},{64,0},{128,192},{192,128},{256,320},{320,256},{384,448},{4... | collective-permute-start | bytes 1327112 | tf_op jit(solution)/shard_map/ppermute | solution.py:555
  134.9 25.8 %all-to-all-start.5 = ((bf16[6,48,896]{2,1,0:T(8,128)(2,1)}), bf16[6,48,896]{2,1,0:T(8,128)(2,1)S(1)}, u32[]{:S(2)}, u32[]{:S(2)}) async-start(bf16[6,48,896]{2,1,0:T(8,128)(2,1)} %pad_maximum_fusion), calls=%async_computation.5 | async-start | bytes 1032192 | tf_op jit(solution)/shard_map/all_to_all | solution.py:384
  161.9 10.0 %all-to-all-start.6 = ((bf16[8,94,256]{2,1,0:T(8,128)(2,1)}), bf16[8,94,256]{2,1,0:T(8,128)(2,1)S(1)}, u32[]{:S(2)}, u32[]{:S(2)}) async-start(bf16[8,94,256]{2,1,0:T(8,128)(2,1)} %pad_maximum_fusion.2), calls=%async_computation.6 | async-start | bytes 786432 | tf_op jit(solution)/shard_map/all_to_all | solution.py:384

commit v6 on v5

--- a/solution.py
+++ b/solution.py
@@ -402,6 +402,11 @@
     places = side // 2
     place_groups = [group[h * places : (h + 1) * places] for group in far_groups for h in range(2)]
     half = lax.axis_index("ch") // (places * side)
+
+    def other_half(value):
+        pairs = [(j, (j + places * side) % owners) for j in range(owners)]
+        return lax.ppermute(value, "ch", pairs)
+
     chips = blocks // 2
     core = me % 2
     core_pairs = [(k, k ^ 1) for k in range(blocks)]
@@ -435,15 +440,11 @@
     ).astype(bf16)
     grad_terms = between_cores(grad_terms.reshape(side, chips, 2, share, tokens), 2)
     grad_terms = jnp.stack(grad_terms, axis=1).reshape(2, places, channels, tokens)
-    received = lax.ppermute(
-        lax.dynamic_index_in_dim(grad_terms, 1 - half, 0, False),
-        "ch",
-        [(j, (j + places * side) % owners) for j in range(owners)],
-    )
-    grad_terms = lax.dynamic_index_in_dim(grad_terms, half, 0, False)
-    grad_terms = (grad_terms.astype(f32) + received.astype(f32)).astype(bf16)
-    grad_terms = exchange(grad_terms, "ch", place_groups)
-    grad_gated = jnp.sum(grad_terms.astype(f32), axis=0).astype(bf16)
+    grad_terms = exchange(grad_terms.transpose(1, 0, 2, 3), "ch", place_groups)
+    grad_terms = jnp.sum(grad_terms.astype(f32), axis=0)
+    received = other_half(lax.dynamic_index_in_dim(grad_terms, 1 - half, 0, False).astype(bf16))
+    grad_gated = lax.dynamic_index_in_dim(grad_terms, half, 0, False)
+    grad_gated = (grad_gated + received.astype(f32)).astype(bf16)
 
     params = jnp.concatenate(
         [

time: 203 us -> 202 us (level)
  blocking collectives: 46.3 us -> 37.4 us
  waiting for transfers between devices: 48.6 us -> 53.3 us
  starting transfers between devices: 74 us -> 76.6 us
    all_to_all x1, blocking collectives: 20.2 us -> 11.1 us  [exchange(): lax.all_to_all(value, axis, 0, 0, tiled=True, axis_index_groups=groups)]
    all_to_all x6, waiting for transfers between devices: 47.1 us -> 51.2 us  [exchange(): lax.all_to_all(value, axis, 0, 0, tiled=True, axis_index_groups=groups)]
  transfers between devices with their start and end apart: 11 -> 11, of which waited for: 5 -> 7; matrix products, arithmetic and copies ran while one was open for 3% -> 3% of each run, Pallas kernels for 4% -> 4%
where the time goes in v6:
time: 202 us; the launch traced here: 201 us
  starting transfers between devices  76.6 us (38%)
  waiting for transfers between devices  53.3 us (26%)
  blocking collectives  37.4 us (19%)
  Pallas kernels  16.3 us (8%)
  local copies, waits for them, and re-layouts  8.79 us (4%)
  other arithmetic  5.5 us (3%)
    all_to_all x6, waiting for transfers between devices, exchange(): lax.all_to_all(value, axis, 0, 0, tiled=True, axis_index_groups=groups)  51.2 us
    all_to_all x6, starting transfers between devices, exchange(): lax.all_to_all(value, axis, 0, 0, tiled=True, axis_index_groups=groups)  40.7 us
    all_gather x1, blocking collectives, shards(): lax.all_gather(jnp.concatenate([weight_rows, tail], axis=1), 'ctx', axis=0)  26.4 us
    ppermute x3, starting transfers between devices, between_cores(): return in_order(here, lax.ppermute(there, 'ctx', core_pairs))  17.4 us
    pallas_call x4, Pallas kernels, call(): pl.pallas_call(kernel, out_shape=[pltpu.HBM(shape, kind) if place is FAR...  16.3 us
    all_to_all x1, blocking collectives, exchange(): lax.all_to_all(value, axis, 0, 0, tiled=True, axis_index_groups=groups)  11.1 us
    ppermute x1, starting transfers between devices, other_half(): return lax.ppermute(value, 'ch', pairs)  9.76 us
    ppermute x1, starting transfers between devices, shards(): sent = lax.ppermute(sent, 'ctx', core_pairs)  8.8 us
  transfers between devices with their start and end apart: 11, of which 7 were waited for; matrix products, arithmetic and copies ran while one was open for 3% of the time, Pallas kernels for 4%

profile of v6, /device:TPU:1, one launch (start us, length us, event | category | flops | bytes accessed | tf_op | source)
XLA Modules:
  0.0 200.8 jit_solution(15345687665614582992)
XLA Ops:
  0.6 2.7 %shard_map.181 = bf16[8,72,832]{2,1,0:T(8,128)(2,1)} custom-call(bf16[72,4608]{1,0:T(8,128)(2,1)} %far_weight.1, bf16[72,256]{1,0:T(8,128)(2,1)} %far_cotangent.1), custom_call_target="tpu_custom_call" | custom-call | tf_op jit(solution)/shard_map/pallas_call | solution.py:365
  3.4 6.0 %all-to-all-start = ((bf16[8,72,832]{2,1,0:T(8,128)(2,1)}), bf16[8,72,832]{2,1,0:T(8,128)(2,1)S(1)}, u32[]{:S(2)}, u32[]{:S(2)}) async-start(bf16[8,72,832]{2,1,0:T(8,128)(2,1)} %shard_map.181), calls=%async_computation | async-start | bytes 2064384 | tf_op jit(solution)/shard_map/all_to_all | solution.py:384
  9.6 10.2 %collective-permute-start = (bf16[6,24,256]{2,1,0:T(8,128)(2,1)S(1)}, bf16[6,24,256]{2,1,0:T(8,128)(2,1)S(1)}, u32[]{:S(2)}, u32[]{:S(2)}) collective-permute-start(bf16[6,24,256]{2,1,0:T(8,128)(2,1)S(1)} %dynamic-slice_bitcast_fusion.3), channel_id=1, source_target_pairs={{0,64},{64,0},{128,192},{192,128},{256,320},{320,256},{384,448},{4... | collective-permute-start | bytes 221192 | tf_op jit(solution)/shard_map/ppermute | solution.py:422
  19.8 0.1 copy.92
  19.9 0.1 copy.91
  19.9 0.1 copy.93
  20.0 0.1 copy.94
  20.1 0.1 fusion.21
  20.3 6.3 %shard_map.182 = (f32[64,3072]{1,0:T(8,128)}, f32[64,3072]{1,0:T(8,128)}, f32[64,3072]{1,0:T(8,128)}, f32[64,3072]{1,0:T(8,128)}, f32[12,8,512]{2,1,0:T(8,128)}) custom-call(f32[32,3072]{1,0:T(8,128)S(1)} %copy-done.2, f32[32,64]{1,0:T(8,128)S(1)} %copy-done.7, f32[64,64]{1,0:T(8,128)S(1)} %copy-done.6, f32[8,128]{1,0:T(8,128)S(1)} %pad.25.params, ...), custom_call_target="tpu_custom_call" | custom-call | tf_op jit(solution)/shard_map/pallas_call | solution.py:365
  26.6 0.4 fusion
  27.0 0.1 reshape.126
  27.2 3.4 %collective-permute-start.2 = (bf16[8,6,6,256]{3,0,2,1:T(8,128)(2,1)S(1)}, bf16[8,6,6,256]{3,0,2,1:T(8,128)(2,1)S(1)}, u32[]{:S(2)}, u32[]{:S(2)}) collective-permute-start(bf16[8,6,6,256]{3,0,2,1:T(8,128)(2,1)S(1)} %bitcast.135), channel_id=1, source_target_pairs={{0,64},{64,0},{128,192},{192,128},{256,320},{320,256},{384,448},{4... | collective-permute-start | bytes 442376 | tf_op jit(solution)/shard_map/ppermute | solution.py:422
  30.7 0.7 pad_maximum_fusion.4
  31.4 8.7 %all-to-all-start.1 = ((bf16[6,48,256]{2,1,0:T(8,128)(2,1)}), bf16[6,48,256]{2,1,0:T(8,128)(2,1)S(1)}, u32[]{:S(2)}, u32[]{:S(2)}) async-start(bf16[6,48,256]{2,1,0:T(8,128)(2,1)} %pad_maximum_fusion.4), calls=%async_computation.1 | async-start | bytes 294912 | tf_op jit(solution)/shard_map/all_to_all | solution.py:384
  40.1 0.1 fusion.4
  40.2 0.1 reshape.127
  40.3 1.0 copy.97
  41.3 8.6 %all-to-all-done.1 = bf16[6,48,256]{2,1,0:T(8,128)(2,1)S(1)} async-done(((bf16[6,48,256]{2,1,0:T(8,128)(2,1)}), bf16[6,48,256]{2,1,0:T(8,128)(2,1)S(1)}, u32[]{:S(2)}, u32[]{:S(2)}) %all-to-all-start.1) | async-done | bytes 147488 | tf_op jit(solution)/shard_map/all_to_all | solution.py:384
  49.9 5.9 %all-to-all-start.2 = ((bf16[4,2,72,256]{3,1,2,0:T(2,128)(2,1)}), bf16[4,2,72,256]{3,1,2,0:T(2,128)(2,1)S(1)}, u32[]{:S(2)}, u32[]{:S(2)}) async-start(bf16[4,2,72,256]{3,1,2,0:T(2,128)(2,1)} %copy.97), calls=%async_computation.2 | async-start | bytes 589824 | tf_op jit(solution)/shard_map/all_to_all | solution.py:384
  55.8 1.6 shard_map.183
  57.5 0.7 dynamic-slice_bitcast_fusion.4
  58.2 3.8 %collective-permute-start.1 = (bf16[6,8,256]{2,1,0:T(8,128)(2,1)S(1)}, bf16[6,8,256]{2,1,0:T(8,128)(2,1)S(1)}, u32[]{:S(2)}, u32[]{:S(2)}) collective-permute-start(bf16[6,8,256]{2,1,0:T(8,128)(2,1)S(1)} %dynamic-slice_bitcast_fusion.4), channel_id=1, source_target_pairs={{0,64},{64,0},{128,192},{192,128},{256,320},{320,256},{384,448},{4... | collective-permute-start | bytes 73736 | tf_op jit(solution)/shard_map/ppermute | solution.py:422
  62.1 2.6 %all-to-all-done.2 = bf16[4,2,72,256]{3,1,2,0:T(2,128)(2,1)S(1)} async-done(((bf16[4,2,72,256]{3,1,2,0:T(2,128)(2,1)}), bf16[4,2,72,256]{3,1,2,0:T(2,128)(2,1)S(1)}, u32[]{:S(2)}, u32[]{:S(2)}) %all-to-all-start.2) | async-done | bytes 294944 | tf_op jit(solution)/shard_map/all_to_all | solution.py:384
  64.7 0.1 copy.119
  64.8 9.8 %collective-permute-start.3 = (bf16[72,256]{1,0:T(8,128)(2,1)S(1)}, bf16[72,256]{1,0:T(8,128)(2,1)S(1)}, u32[]{:S(2)}, u32[]{:S(2)}) collective-permute-start(bf16[72,256]{1,0:T(8,128)(2,1)S(1)} %bitcast.138), channel_id=1, source_target_pairs={{0,32},{1,33},{2,34},{3,35},{4,36},{5,37},{6,38},{7,39},{8,40},{9,... | collective-permute-start | bytes 110600 | tf_op jit(solution)/shard_map/ppermute | solution.py:408
  74.6 0.8 bitcast_select_fusion.7
  75.3 0.6 collective-permute-done.3
  76.0 11.1 %all_to_all.35 = bf16[6,32,256]{2,1,0:T(8,128)(2,1)S(1)} all-to-all(bf16[6,32,256]{2,1,0:T(8,128)(2,1)S(1)} %pad_maximum_fusion.5), channel_id=1, replica_groups={{0,128,256,384,512,640},{64,192,320,448,576,704},{1,129,257,385,513,641..., dimensions={0} | all-to-all | bytes 196608 | tf_op jit(solution)/shard_map/all_to_all | solution.py:384
  87.1 5.7 %shard_map.184 = (bf16[12,48,128]{2,1,0:T(8,128)(2,1)}, bf16[96,64]{1,0:T(8,128)(2,1)S(1)}, bf16[16,64]{1,0:T(8,128)(2,1)S(1)}) custom-call(f32[12,8,512]{2,1,0:T(8,128)} %get-tuple-element.22.spectra.kept_spectra, f32[12,24,256]{2,1,0:T(8,128)} %get-tuple-element.24.kept_filtered, f32[12,8,256]{2,1,0:T(8,128)} %get-tuple-element.25.kept_long_out, ...), custom_call_target="tpu_custom_call" | custom-call | tf_op jit(solution)/shard_map/pallas_call | solution.py:365
  92.8 0.1 reshape.131
  92.9 0.8 broadcast_in_dim.27
  93.7 11.8 %all-to-all-start.4 = ((bf16[8,96,256]{2,1,0:T(8,128)(2,1)}), bf16[8,96,256]{2,1,0:T(8,128)(2,1)S(1)}, u32[]{:S(2)}, u32[]{:S(2)}) async-start(bf16[8,96,256]{2,1,0:T(8,128)(2,1)} %broadcast_in_dim.27), calls=%async_computation.4 | async-start | bytes 786432 | tf_op jit(solution)/shard_map/all_to_all | solution.py:384
  105.5 0.1 copy.100
  105.7 15.2 %all-to-all-done.4 = bf16[8,96,256]{2,1,0:T(8,128)(2,1)S(1)} async-done(((bf16[8,96,256]{2,1,0:T(8,128)(2,1)}), bf16[8,96,256]{2,1,0:T(8,128)(2,1)S(1)}, u32[]{:S(2)}, u32[]{:S(2)}) %all-to-all-start.4) | async-done | bytes 393248 | tf_op jit(solution)/shard_map/all_to_all | solution.py:384
  120.9 0.1 reshape.134
  121.0 0.3 convolution_convert_fusion
  121.3 0.9 pad_maximum_fusion.1
  122.2 8.8 %collective-permute-start.4 = (bf16[6,48,768]{2,1,0:T(8,128)(2,1)}, bf16[6,48,768]{2,1,0:T(8,128)(2,1)S(1)}, u32[]{:S(2)}, u32[]{:S(2)}) collective-permute-start(bf16[6,48,768]{2,1,0:T(8,128)(2,1)} %pad_maximum_fusion.1), channel_id=1, source_target_pairs={{0,64},{64,0},{128,192},{192,128},{256,320},{320,256},{384,448},{4... | collective-permute-start | bytes 1327112 | tf_op jit(solution)/shard_map/ppermute | solution.py:556
  131.1 1.5 collective-permute-done.4
  132.6 0.1 reduce-precision_convert_fusion
  132.7 0.1 broadcast_select_fusion.1
  132.8 0.3 add_convert_fusion
  133.1 0.9 pad_maximum_fusion
  134.0 4.8 %all-to-all-start.5 = ((bf16[6,48,896]{2,1,0:T(8,128)(2,1)}), bf16[6,48,896]{2,1,0:T(8,128)(2,1)S(1)}, u32[]{:S(2)}, u32[]{:S(2)}) async-start(bf16[6,48,896]{2,1,0:T(8,128)(2,1)} %pad_maximum_fusion), calls=%async_computation.5 | async-start | bytes 1032192 | tf_op jit(solution)/shard_map/all_to_all | solution.py:384
  138.8 0.1 slice.142
  138.9 0.4 convolution_convert_fusion.1
  139.3 19.8 %all-to-all-done.5 = bf16[6,48,896]{2,1,0:T(8,128)(2,1)S(1)} async-done(((bf16[6,48,896]{2,1,0:T(8,128)(2,1)}), bf16[6,48,896]{2,1,0:T(8,128)(2,1)S(1)}, u32[]{:S(2)}, u32[]{:S(2)}) %all-to-all-start.5) | async-done | bytes 516128 | tf_op jit(solution)/shard_map/all_to_all | solution.py:384
  159.1 0.1 slice_reduce_fusion
  159.2 0.1 slice_convert_fusion.1
  159.3 0.1 broadcast_in_dim.29
  159.4 0.8 pad_maximum_fusion.2
  160.2 3.5 %all-to-all-start.6 = ((bf16[8,94,256]{2,1,0:T(8,128)(2,1)}), bf16[8,94,256]{2,1,0:T(8,128)(2,1)S(1)}, u32[]{:S(2)}, u32[]{:S(2)}) async-start(bf16[8,94,256]{2,1,0:T(8,128)(2,1)} %pad_maximum_fusion.2), calls=%async_computation.6 | async-start | bytes 786432 | tf_op jit(solution)/shard_map/all_to_all | solution.py:384
  163.8 0.1 copy.105
  163.9 0.7 reshape.139
  164.6 0.7 copy.108
  165.3 5.0 %all-to-all-done.6 = bf16[8,94,256]{2,1,0:T(8,128)(2,1)S(1)} async-done(((bf16[8,94,256]{2,1,0:T(8,128)(2,1)}), bf16[8,94,256]{2,1,0:T(8,128)(2,1)S(1)}, u32[]{:S(2)}, u32[]{:S(2)}) %all-to-all-start.6) | async-done | bytes 385056 | tf_op jit(solution)/shard_map/all_to_all | solution.py:384
  170.5 0.1 reshape.141
  170.6 0.2 reshape.142
  170.9 26.4 %all-gather.1 = bf16[12,6,4864]{2,1,0:T(8,128)(2,1)S(1)} all-gather(bf16[1,6,4864]{2,1,0:T(8,128)(2,1)S(1)} %maximum_bitcast_fusion), channel_id=2, replica_groups=mesh['ctx'=12,'ch'=64] {'ctx'}, dimensions={0}, use_global_device_ids=true | all-gather | bytes 758784 | tf_op jit(solution)/shard_map/all_gather | solution.py:608
  197.4 0.1 slice_convert_fusion
  197.5 0.7 slice.136
  198.2 0.7 slice.138
  198.9 1.3 reshape.147
  200.1 0.7 slice_reduce_fusion.1
  (95 shorter events, 1.2 us)
Async XLA Ops:
  0.6 8.8 %copy-start.9 = (bf16[3,72,256]{2,1,0:T(8,128)(2,1)S(1)}, bf16[3,72,256]{2,1,0:T(8,128)(2,1)}, u32[]{:S(2)}) copy-start(bf16[3,72,256]{2,1,0:T(8,128)(2,1)} %param.14) | copy-start | bytes 331780
  3.3 16.4 %copy-start.11 = (f32[3,72,3]{1,2,0:T(4,128)S(1)}, f32[3,72,3]{1,2,0:T(4,128)}, u32[]{:S(2)}) copy-start(f32[3,72,3]{1,2,0:T(4,128)} %param.15) | copy-start | bytes 7780
  3.3 16.5 %copy-start.10 = (f32[64,72]{1,0:T(8,128)S(1)}, f32[64,72]{1,0:T(8,128)}, u32[]{:S(2)}) copy-start(f32[64,72]{1,0:T(8,128)} %param.18) | copy-start | bytes 55300
  3.3 16.6 %copy-start.12 = (f32[72]{0:T(128)S(1)}, f32[72]{0:T(128)}, u32[]{:S(2)}) copy-start(f32[72]{0:T(128)} %param.19) | copy-start | bytes 868
  3.3 16.7 %copy-start.13 = (f32[72]{0:T(128)S(1)}, f32[72]{0:T(128)}, u32[]{:S(2)}) copy-start(f32[72]{0:T(128)} %param.20) | copy-start | bytes 868
  3.4 16.9 %copy-start = (bf16[256,512]{1,0:T(8,128)(2,1)S(1)}, bf16[256,512]{1,0:T(8,128)(2,1)}, u32[]{:S(2)}) copy-start(bf16[256,512]{1,0:T(8,128)(2,1)} %constant.104.clone.table_low) | copy-start | bytes 786436
  3.4 16.9 %copy-start.1 = (bf16[256,512]{1,0:T(8,128)(2,1)S(1)}, bf16[256,512]{1,0:T(8,128)(2,1)}, u32[]{:S(2)}) copy-start(bf16[256,512]{1,0:T(8,128)(2,1)} %constant.103.clone.table_high) | copy-start | bytes 786436
  3.4 16.9 %copy-start.2 = (f32[32,3072]{1,0:T(8,128)S(1)}, f32[32,3072]{1,0:T(8,128)}, u32[]{:S(2)}) copy-start(f32[32,3072]{1,0:T(8,128)} %constant.107.clone.features) | copy-start | bytes 1179652
  3.4 16.9 %copy-start.6 = (f32[64,64]{1,0:T(8,128)S(1)}, f32[64,64]{1,0:T(8,128)}, u32[]{:S(2)}) copy-start(f32[64,64]{1,0:T(8,128)} %filter_mid.3) | copy-start | bytes 49156
  3.4 16.9 %copy-start.7 = (f32[32,64]{1,0:T(8,128)S(1)}, f32[32,64]{1,0:T(8,128)}, u32[]{:S(2)}) copy-start(f32[32,64]{1,0:T(8,128)} %filter_in.1) | copy-start | bytes 24580
  3.4 23.1 %all-to-all-start = ((bf16[8,72,832]{2,1,0:T(8,128)(2,1)}), bf16[8,72,832]{2,1,0:T(8,128)(2,1)S(1)}, u32[]{:S(2)}, u32[]{:S(2)}) async-start(bf16[8,72,832]{2,1,0:T(8,128)(2,1)} %shard_map.181), calls=%async_computation | async-start | bytes 2064384 | tf_op jit(solution)/shard_map/all_to_all | solution.py:384
  9.6 21.1 %collective-permute-start = (bf16[6,24,256]{2,1,0:T(8,128)(2,1)S(1)}, bf16[6,24,256]{2,1,0:T(8,128)(2,1)S(1)}, u32[]{:S(2)}, u32[]{:S(2)}) collective-permute-start(bf16[6,24,256]{2,1,0:T(8,128)(2,1)S(1)} %dynamic-slice_bitcast_fusion.3), channel_id=1, source_target_pairs={{0,64},{64,0},{128,192},{192,128},{256,320},{320,256},{384,448},{4... | collective-permute-start | bytes 221192 | tf_op jit(solution)/shard_map/ppermute | solution.py:422
  27.2 12.9 %collective-permute-start.2 = (bf16[8,6,6,256]{3,0,2,1:T(8,128)(2,1)S(1)}, bf16[8,6,6,256]{3,0,2,1:T(8,128)(2,1)S(1)}, u32[]{:S(2)}, u32[]{:S(2)}) collective-permute-start(bf16[8,6,6,256]{3,0,2,1:T(8,128)(2,1)S(1)} %bitcast.135), channel_id=1, source_target_pairs={{0,64},{64,0},{128,192},{192,128},{256,320},{320,256},{384,448},{4... | collective-permute-start | bytes 442376 | tf_op jit(solution)/shard_map/ppermute | solution.py:422
  30.7 25.1 %copy-start.3 = (bf16[512,256]{1,0:T(8,128)(2,1)S(1)}, bf16[512,256]{1,0:T(8,128)(2,1)}, u32[]{:S(2)}) copy-start(bf16[512,256]{1,0:T(8,128)(2,1)} %constant.106.clone.back_low) | copy-start | bytes 786436
  30.7 25.1 %copy-start.4 = (bf16[512,256]{1,0:T(8,128)(2,1)S(1)}, bf16[512,256]{1,0:T(8,128)(2,1)}, u32[]{:S(2)}) copy-start(bf16[512,256]{1,0:T(8,128)(2,1)} %constant.105.clone.back_high) | copy-start | bytes 786436
  30.7 25.1 %copy-start.5 = (f32[12,8,512]{2,1,0:T(8,128)S(1)}, f32[12,8,512]{2,1,0:T(8,128)}, u32[]{:S(2)}) copy-start(f32[12,8,512]{2,1,0:T(8,128)} %get-tuple-element.22.spectra.kept_spectra) | copy-start | bytes 589828
  31.4 18.5 %all-to-all-start.1 = ((bf16[6,48,256]{2,1,0:T(8,128)(2,1)}), bf16[6,48,256]{2,1,0:T(8,128)(2,1)S(1)}, u32[]{:S(2)}, u32[]{:S(2)}) async-start(bf16[6,48,256]{2,1,0:T(8,128)(2,1)} %pad_maximum_fusion.4), calls=%async_computation.1 | async-start | bytes 294912 | tf_op jit(solution)/shard_map/all_to_all | solution.py:384
  49.9 14.8 %all-to-all-start.2 = ((bf16[4,2,72,256]{3,1,2,0:T(2,128)(2,1)}), bf16[4,2,72,256]{3,1,2,0:T(2,128)(2,1)S(1)}, u32[]{:S(2)}, u32[]{:S(2)}) async-start(bf16[4,2,72,256]{3,1,2,0:T(2,128)(2,1)} %copy.97), calls=%async_computation.2 | async-start | bytes 589824 | tf_op jit(solution)/shard_map/all_to_all | solution.py:384
  58.2 16.4 %collective-permute-start.1 = (bf16[6,8,256]{2,1,0:T(8,128)(2,1)S(1)}, bf16[6,8,256]{2,1,0:T(8,128)(2,1)S(1)}, u32[]{:S(2)}, u32[]{:S(2)}) collective-permute-start(bf16[6,8,256]{2,1,0:T(8,128)(2,1)S(1)} %dynamic-slice_bitcast_fusion.4), channel_id=1, source_target_pairs={{0,64},{64,0},{128,192},{192,128},{256,320},{320,256},{384,448},{4... | collective-permute-start | bytes 73736 | tf_op jit(solution)/shard_map/ppermute | solution.py:422
  64.8 11.1 %collective-permute-start.3 = (bf16[72,256]{1,0:T(8,128)(2,1)S(1)}, bf16[72,256]{1,0:T(8,128)(2,1)S(1)}, u32[]{:S(2)}, u32[]{:S(2)}) collective-permute-start(bf16[72,256]{1,0:T(8,128)(2,1)S(1)} %bitcast.138), channel_id=1, source_target_pairs={{0,32},{1,33},{2,34},{3,35},{4,36},{5,37},{6,38},{7,39},{8,40},{9,... | collective-permute-start | bytes 110600 | tf_op jit(solution)/shard_map/ppermute | solution.py:408
  92.9 12.8 %copy-start.8 = (bf16[12,48,128]{2,1,0:T(8,128)(2,1)S(1)}, bf16[12,48,128]{2,1,0:T(8,128)(2,1)}, u32[]{:S(2)}) copy-start(bf16[12,48,128]{2,1,0:T(8,128)(2,1)} %get-tuple-element.33) | copy-start | bytes 442372
  93.7 27.2 %all-to-all-start.4 = ((bf16[8,96,256]{2,1,0:T(8,128)(2,1)}), bf16[8,96,256]{2,1,0:T(8,128)(2,1)S(1)}, u32[]{:S(2)}, u32[]{:S(2)}) async-start(bf16[8,96,256]{2,1,0:T(8,128)(2,1)} %broadcast_in_dim.27), calls=%async_computation.4 | async-start | bytes 786432 | tf_op jit(solution)/shard_map/all_to_all | solution.py:384
  122.2 10.4 %collective-permute-start.4 = (bf16[6,48,768]{2,1,0:T(8,128)(2,1)}, bf16[6,48,768]{2,1,0:T(8,128)(2,1)S(1)}, u32[]{:S(2)}, u32[]{:S(2)}) collective-permute-start(bf16[6,48,768]{2,1,0:T(8,128)(2,1)} %pad_maximum_fusion.1), channel_id=1, source_target_pairs={{0,64},{64,0},{128,192},{192,128},{256,320},{320,256},{384,448},{4... | collective-permute-start | bytes 1327112 | tf_op jit(solution)/shard_map/ppermute | solution.py:556
  134.0 25.0 %all-to-all-start.5 = ((bf16[6,48,896]{2,1,0:T(8,128)(2,1)}), bf16[6,48,896]{2,1,0:T(8,128)(2,1)S(1)}, u32[]{:S(2)}, u32[]{:S(2)}) async-start(bf16[6,48,896]{2,1,0:T(8,128)(2,1)} %pad_maximum_fusion), calls=%async_computation.5 | async-start | bytes 1032192 | tf_op jit(solution)/shard_map/all_to_all | solution.py:384
  160.2 10.1 %all-to-all-start.6 = ((bf16[8,94,256]{2,1,0:T(8,128)(2,1)}), bf16[8,94,256]{2,1,0:T(8,128)(2,1)S(1)}, u32[]{:S(2)}, u32[]{:S(2)}) async-start(bf16[8,94,256]{2,1,0:T(8,128)(2,1)} %pad_maximum_fusion.2), calls=%async_computation.6 | async-start | bytes 786432 | tf_op jit(solution)/shard_map/all_to_all | solution.py:384

commit v7 on v6

--- a/solution.py
+++ b/solution.py
@@ -336,7 +336,7 @@
         total_mid = total_mid + close_dot(hidden_one[:, at], grad_two, across)
         grad_one = close_dot(filter_mid[...], grad_two) * slope_one[:, at]
         total_in = total_in + close_dot(features[:, at], grad_one, across)
-    grad_shared[...] = jnp.concatenate([total_in, total_mid], axis=0).astype(bf16)
+    grad_shared[...] = jnp.concatenate([total_in, total_mid], axis=0)
     high, low = halves(total_last)
     grad_last[...] = jnp.concatenate([high.astype(f32), low.astype(f32)], axis=0).astype(bf16)
     streams_copy.wait()
@@ -495,13 +495,16 @@
     turned = jnp.concatenate([first, turned[:, 0], second, turned[:, 1]], axis=1)
     turned = exchange(turned, "ctx", chip_groups).reshape(blocks, 2 * ROWS, tokens)
     own_gated = turned[:, :share, :].reshape(channels, tokens)
+    all_gated = exchange(
+        jnp.broadcast_to(own_gated[None], (side, channels, tokens)), "ch", far_groups
+    ).reshape(group, tokens)
 
     packed_streams = ((blocks, 6 * ROWS, tokens // 2), bf16)
     grad_packed, grad_shared, grad_last = call(
         backward_kernel,
         [
             (FAR,) + packed_streams,
-            (NEAR, (band_rows + hidden, hidden), bf16),
+            (NEAR, (band_rows + hidden, hidden), f32),
             (NEAR, (2 * ROWS, hidden), bf16),
         ],
         [spectrum, kept[1], kept[2], spectrum]
@@ -514,13 +517,10 @@
         *near(turned, params, features, filter_mid, *tables),
     )
 
-    shared_rows = grad_shared.size // tokens
-    sent = jnp.concatenate([own_gated, grad_shared.reshape(shared_rows, tokens)], axis=0)
-    sent = exchange(
-        jnp.broadcast_to(sent[None], (side,) + sent.shape), "ch", far_groups
-    )
-    all_gated = sent[:, :channels].reshape(group, tokens)
-    shared = jnp.sum(sent[:, channels:].astype(f32), axis=0)
+    shared = grad_shared
+    for stride in (side, 2 * side, 4 * side):
+        pairs = [(j, j ^ stride) for j in range(owners)]
+        shared = shared + lax.ppermute(shared, "ch", pairs)
 
     out_terms = jnp.dot(weight, all_gated, preferred_element_type=f32).astype(bf16)
     def both_halves(value):

time: 202 us -> 213 us (1.054)
  starting transfers between devices: 76.6 us -> 96.6 us
  waiting for transfers between devices: 53.3 us -> 45.1 us
    ppermute x0 -> x3, starting transfers between devices: none -> 20.3 us  [shards(): shared = shared + lax.ppermute(shared, 'ch', pairs)]
    all_to_all x6, waiting for transfers between devices: 51.2 us -> 36.5 us  [exchange(): lax.all_to_all(value, axis, 0, 0, tiled=True, axis_index_groups=groups)]
    ppermute x0 -> x3, waiting for transfers between devices: none -> 6.66 us  [shards(): shared = shared + lax.ppermute(shared, 'ch', pairs)]
  transfers between devices with their start and end apart: 11 -> 14, of which waited for: 7 -> 9; matrix products, arithmetic and copies ran while one was open for 3% -> 4% of each run, Pallas kernels for 4% -> 6%
where the time goes in v7:
time: 213 us; the launch traced here: 212 us
  starting transfers between devices  96.6 us (45%)
  waiting for transfers between devices  45.1 us (21%)
  blocking collectives  37 us (17%)
  Pallas kernels  16.3 us (8%)
  local copies, waits for them, and re-layouts  8.52 us (4%)
  other arithmetic  5.62 us (3%)
    all_to_all x6, starting transfers between devices, exchange(): lax.all_to_all(value, axis, 0, 0, tiled=True, axis_index_groups=groups)  39.4 us
    all_to_all x6, waiting for transfers between devices, exchange(): lax.all_to_all(value, axis, 0, 0, tiled=True, axis_index_groups=groups)  36.5 us
    all_gather x1, blocking collectives, shards(): lax.all_gather(jnp.concatenate([weight_rows, tail], axis=1), 'ctx', axis=0)  26 us
    ppermute x3, starting transfers between devices, shards(): shared = shared + lax.ppermute(shared, 'ch', pairs)  20.3 us
    ppermute x3, starting transfers between devices, between_cores(): return in_order(here, lax.ppermute(there, 'ctx', core_pairs))  17.4 us
    pallas_call x4, Pallas kernels, call(): pl.pallas_call(kernel, out_shape=[pltpu.HBM(shape, kind) if place is FAR...  16.3 us
    all_to_all x1, blocking collectives, exchange(): lax.all_to_all(value, axis, 0, 0, tiled=True, axis_index_groups=groups)  11.1 us
    ppermute x1, starting transfers between devices, shards(): sent = lax.ppermute(sent, 'ctx', core_pairs)  9.78 us
  transfers between devices with their start and end apart: 14, of which 9 were waited for; matrix products, arithmetic and copies ran while one was open for 4% of the time, Pallas kernels for 6%

profile of v7, /device:TPU:1, one launch (start us, length us, event | category | flops | bytes accessed | tf_op | source)
XLA Modules:
  0.0 212.1 jit_solution(10522569867291083291)
XLA Ops:
  0.6 2.7 %shard_map.181 = bf16[8,72,832]{2,1,0:T(8,128)(2,1)} custom-call(bf16[72,4608]{1,0:T(8,128)(2,1)} %far_weight.1, bf16[72,256]{1,0:T(8,128)(2,1)} %far_cotangent.1), custom_call_target="tpu_custom_call" | custom-call | tf_op jit(solution)/shard_map/pallas_call | solution.py:365
  3.4 6.0 %all-to-all-start = ((bf16[8,72,832]{2,1,0:T(8,128)(2,1)}), bf16[8,72,832]{2,1,0:T(8,128)(2,1)S(1)}, u32[]{:S(2)}, u32[]{:S(2)}) async-start(bf16[8,72,832]{2,1,0:T(8,128)(2,1)} %shard_map.181), calls=%async_computation | async-start | bytes 2064384 | tf_op jit(solution)/shard_map/all_to_all | solution.py:384
  9.6 10.2 %collective-permute-start = (bf16[6,24,256]{2,1,0:T(8,128)(2,1)S(1)}, bf16[6,24,256]{2,1,0:T(8,128)(2,1)}, u32[]{:S(2)}, u32[]{:S(2)}) collective-permute-start(bf16[6,24,256]{2,1,0:T(8,128)(2,1)S(1)} %dynamic-slice_bitcast_fusion.3), channel_id=1, source_target_pairs={{0,64},{64,0},{128,192},{192,128},{256,320},{320,256},{384,448},{4... | collective-permute-start | bytes 221192 | tf_op jit(solution)/shard_map/ppermute | solution.py:422
  19.8 0.1 copy.92
  19.9 0.1 copy.91
  19.9 0.1 copy.93
  20.0 0.1 copy.94
  20.1 0.1 fusion.21
  20.3 6.3 %shard_map.182 = (f32[64,3072]{1,0:T(8,128)}, f32[64,3072]{1,0:T(8,128)}, f32[64,3072]{1,0:T(8,128)}, f32[64,3072]{1,0:T(8,128)}, f32[12,8,512]{2,1,0:T(8,128)}) custom-call(f32[32,3072]{1,0:T(8,128)S(1)} %copy-done.2, f32[32,64]{1,0:T(8,128)S(1)} %copy-done.7, f32[64,64]{1,0:T(8,128)S(1)} %copy-done.6, f32[8,128]{1,0:T(8,128)S(1)} %pad.25.params, ...), custom_call_target="tpu_custom_call" | custom-call | tf_op jit(solution)/shard_map/pallas_call | solution.py:365
  26.6 0.4 fusion
  27.0 0.1 reshape.120
  27.3 3.4 %collective-permute-start.2 = (bf16[8,6,6,256]{3,0,2,1:T(8,128)(2,1)S(1)}, bf16[8,6,6,256]{3,0,2,1:T(8,128)(2,1)S(1)}, u32[]{:S(2)}, u32[]{:S(2)}) collective-permute-start(bf16[8,6,6,256]{3,0,2,1:T(8,128)(2,1)S(1)} %bitcast.138), channel_id=1, source_target_pairs={{0,64},{64,0},{128,192},{192,128},{256,320},{320,256},{384,448},{4... | collective-permute-start | bytes 442376 | tf_op jit(solution)/shard_map/ppermute | solution.py:422
  30.6 0.9 bitcast_select_fusion.5
  31.6 0.7 pad_maximum_fusion.4
  32.3 8.7 %all-to-all-start.1 = ((bf16[6,48,256]{2,1,0:T(8,128)(2,1)}), bf16[6,48,256]{2,1,0:T(8,128)(2,1)S(1)}, u32[]{:S(2)}, u32[]{:S(2)}) async-start(bf16[6,48,256]{2,1,0:T(8,128)(2,1)} %pad_maximum_fusion.4), calls=%async_computation.1 | async-start | bytes 294912 | tf_op jit(solution)/shard_map/all_to_all | solution.py:384
  41.1 0.1 reshape.121
  41.2 0.9 copy.97
  42.1 8.6 %all-to-all-done.1 = bf16[6,48,256]{2,1,0:T(8,128)(2,1)S(1)} async-done(((bf16[6,48,256]{2,1,0:T(8,128)(2,1)}), bf16[6,48,256]{2,1,0:T(8,128)(2,1)S(1)}, u32[]{:S(2)}, u32[]{:S(2)}) %all-to-all-start.1) | async-done | bytes 147488 | tf_op jit(solution)/shard_map/all_to_all | solution.py:384
  50.8 5.9 %all-to-all-start.2 = ((bf16[4,2,72,256]{3,1,2,0:T(2,128)(2,1)}), bf16[4,2,72,256]{3,1,2,0:T(2,128)(2,1)S(1)}, u32[]{:S(2)}, u32[]{:S(2)}) async-start(bf16[4,2,72,256]{3,1,2,0:T(2,128)(2,1)} %copy.97), calls=%async_computation.2 | async-start | bytes 589824 | tf_op jit(solution)/shard_map/all_to_all | solution.py:384
  56.7 1.6 shard_map.183
  58.3 0.7 dynamic-slice_bitcast_fusion.4
  59.1 3.8 %collective-permute-start.1 = (bf16[6,8,256]{2,1,0:T(8,128)(2,1)S(1)}, bf16[6,8,256]{2,1,0:T(8,128)(2,1)S(1)}, u32[]{:S(2)}, u32[]{:S(2)}) collective-permute-start(bf16[6,8,256]{2,1,0:T(8,128)(2,1)S(1)} %dynamic-slice_bitcast_fusion.4), channel_id=1, source_target_pairs={{0,64},{64,0},{128,192},{192,128},{256,320},{320,256},{384,448},{4... | collective-permute-start | bytes 73736 | tf_op jit(solution)/shard_map/ppermute | solution.py:422
  62.9 2.6 %all-to-all-done.2 = bf16[4,2,72,256]{3,1,2,0:T(2,128)(2,1)S(1)} async-done(((bf16[4,2,72,256]{3,1,2,0:T(2,128)(2,1)}), bf16[4,2,72,256]{3,1,2,0:T(2,128)(2,1)S(1)}, u32[]{:S(2)}, u32[]{:S(2)}) %all-to-all-start.2) | async-done | bytes 294944 | tf_op jit(solution)/shard_map/all_to_all | solution.py:384
  65.7 9.8 %collective-permute-start.3 = (bf16[72,256]{1,0:T(8,128)(2,1)S(1)}, bf16[72,256]{1,0:T(8,128)(2,1)S(1)}, u32[]{:S(2)}, u32[]{:S(2)}) collective-permute-start(bf16[72,256]{1,0:T(8,128)(2,1)S(1)} %bitcast.141), channel_id=1, source_target_pairs={{0,32},{1,33},{2,34},{3,35},{4,36},{5,37},{6,38},{7,39},{8,40},{9,... | collective-permute-start | bytes 110600 | tf_op jit(solution)/shard_map/ppermute | solution.py:408
  75.4 0.8 bitcast_select_fusion.7
  76.2 0.6 collective-permute-done.3
  76.8 11.1 %all_to_all.35 = bf16[6,32,256]{2,1,0:T(8,128)(2,1)S(1)} all-to-all(bf16[6,32,256]{2,1,0:T(8,128)(2,1)S(1)} %pad_maximum_fusion.5), channel_id=1, replica_groups={{0,128,256,384,512,640},{64,192,320,448,576,704},{1,129,257,385,513,641..., dimensions={0} | all-to-all | bytes 196608 | tf_op jit(solution)/shard_map/all_to_all | solution.py:384
  87.9 0.7 broadcast_in_dim.29
  88.7 11.8 %all-to-all-start.4 = ((bf16[8,72,256]{2,1,0:T(8,128)(2,1)}), bf16[8,72,256]{2,1,0:T(8,128)(2,1)S(1)}, u32[]{:S(2)}, u32[]{:S(2)}) async-start(bf16[8,72,256]{2,1,0:T(8,128)(2,1)} %broadcast_in_dim.29), calls=%async_computation.4 | async-start | bytes 589824 | tf_op jit(solution)/shard_map/all_to_all | solution.py:384
  100.4 5.7 %shard_map.184 = (bf16[12,48,128]{2,1,0:T(8,128)(2,1)}, f32[96,64]{1,0:T(8,128)S(1)}, bf16[16,64]{1,0:T(8,128)(2,1)S(1)}) custom-call(f32[12,8,512]{2,1,0:T(8,128)} %get-tuple-element.22.spectra.kept_spectra, f32[12,24,256]{2,1,0:T(8,128)} %get-tuple-element.24.kept_filtered, f32[12,8,256]{2,1,0:T(8,128)} %get-tuple-element.25.kept_long_out, ...), custom_call_target="tpu_custom_call" | custom-call | tf_op jit(solution)/shard_map/pallas_call | solution.py:365
  106.1 4.4 %collective-permute-start.4 = (f32[96,64]{1,0:T(8,128)S(1)}, f32[96,64]{1,0:T(8,128)S(1)}, u32[]{:S(2)}, u32[]{:S(2)}) collective-permute-start(f32[96,64]{1,0:T(8,128)S(1)} %get-tuple-element.31), channel_id=1, source_target_pairs={{0,8},{1,9},{2,10},{3,11},{4,12},{5,13},{6,14},{7,15},{8,0},{9,1},... | collective-permute-start | bytes 73736 | tf_op jit(solution)/shard_map/ppermute | solution.py:523
  110.6 1.7 collective-permute-done.4
  112.4 7.2 %collective-permute-start.5 = (f32[96,64]{1,0:T(8,128)S(1)}, f32[96,64]{1,0:T(8,128)S(1)}, u32[]{:S(2)}, u32[]{:S(2)}) collective-permute-start(f32[96,64]{1,0:T(8,128)S(1)} %add.91), channel_id=1, source_target_pairs={{0,16},{1,17},{2,18},{3,19},{4,20},{5,21},{6,22},{7,23},{8,24},{9,... | collective-permute-start | bytes 73736 | tf_op jit(solution)/shard_map/ppermute | solution.py:523
  119.7 2.5 %collective-permute-done.5 = f32[96,64]{1,0:T(8,128)S(1)} collective-permute-done((f32[96,64]{1,0:T(8,128)S(1)}, f32[96,64]{1,0:T(8,128)S(1)}, u32[]{:S(2)}, u32[]{:S(2)}) %collective-permute-start.5) | collective-permute-done | bytes 24608 | tf_op jit(solution)/shard_map/ppermute | solution.py:523
  122.3 8.7 %collective-permute-start.6 = (f32[96,64]{1,0:T(8,128)S(1)}, f32[96,64]{1,0:T(8,128)S(1)}, u32[]{:S(2)}, u32[]{:S(2)}) collective-permute-start(f32[96,64]{1,0:T(8,128)S(1)} %add.92), channel_id=1, source_target_pairs={{0,32},{1,33},{2,34},{3,35},{4,36},{5,37},{6,38},{7,39},{8,40},{9,... | collective-permute-start | bytes 73736 | tf_op jit(solution)/shard_map/ppermute | solution.py:523
  131.0 2.4 %collective-permute-done.6 = f32[96,64]{1,0:T(8,128)S(1)} collective-permute-done((f32[96,64]{1,0:T(8,128)S(1)}, f32[96,64]{1,0:T(8,128)S(1)}, u32[]{:S(2)}, u32[]{:S(2)}) %collective-permute-start.6) | collective-permute-done | bytes 24608 | tf_op jit(solution)/shard_map/ppermute | solution.py:523
  133.5 0.3 convolution_convert_fusion
  133.8 0.1 pad_maximum_fusion.1
  133.9 9.8 %collective-permute-start.7 = (bf16[6,48,768]{2,1,0:T(8,128)(2,1)S(1)}, bf16[6,48,768]{2,1,0:T(8,128)(2,1)S(1)}, u32[]{:S(2)}, u32[]{:S(2)}) collective-permute-start(bf16[6,48,768]{2,1,0:T(8,128)(2,1)S(1)} %pad_maximum_fusion.1), channel_id=1, source_target_pairs={{0,64},{64,0},{128,192},{192,128},{256,320},{320,256},{384,448},{4... | collective-permute-start | bytes 1327112 | tf_op jit(solution)/shard_map/ppermute | solution.py:556
  143.8 1.3 collective-permute-done.7
  145.1 0.1 reduce-precision_convert_fusion
  145.2 0.1 broadcast_select_fusion.1
  145.3 0.3 add_convert_fusion
  145.6 0.9 pad_maximum_fusion
  146.5 3.5 %all-to-all-start.5 = ((bf16[6,48,896]{2,1,0:T(8,128)(2,1)}), bf16[6,48,896]{2,1,0:T(8,128)(2,1)S(1)}, u32[]{:S(2)}, u32[]{:S(2)}) async-start(bf16[6,48,896]{2,1,0:T(8,128)(2,1)} %pad_maximum_fusion), calls=%async_computation.5 | async-start | bytes 1032192 | tf_op jit(solution)/shard_map/all_to_all | solution.py:384
  150.0 0.1 slice.134
  150.1 0.4 convolution_convert_fusion.1
  150.5 20.3 %all-to-all-done.5 = bf16[6,48,896]{2,1,0:T(8,128)(2,1)S(1)} async-done(((bf16[6,48,896]{2,1,0:T(8,128)(2,1)}), bf16[6,48,896]{2,1,0:T(8,128)(2,1)S(1)}, u32[]{:S(2)}, u32[]{:S(2)}) %all-to-all-start.5) | async-done | bytes 516128 | tf_op jit(solution)/shard_map/all_to_all | solution.py:384
  170.9 0.1 slice_convert_fusion.1
  171.1 0.1 broadcast_in_dim.31
  171.2 0.8 pad_maximum_fusion.2
  171.9 3.5 %all-to-all-start.6 = ((bf16[8,94,256]{2,1,0:T(8,128)(2,1)}), bf16[8,94,256]{2,1,0:T(8,128)(2,1)S(1)}, u32[]{:S(2)}, u32[]{:S(2)}) async-start(bf16[8,94,256]{2,1,0:T(8,128)(2,1)} %pad_maximum_fusion.2), calls=%async_computation.6 | async-start | bytes 786432 | tf_op jit(solution)/shard_map/all_to_all | solution.py:384
  175.5 0.1 copy.105
  175.6 0.7 reshape.131
  176.3 0.7 copy.108
  177.0 5.0 %all-to-all-done.6 = bf16[8,94,256]{2,1,0:T(8,128)(2,1)S(1)} async-done(((bf16[8,94,256]{2,1,0:T(8,128)(2,1)}), bf16[8,94,256]{2,1,0:T(8,128)(2,1)S(1)}, u32[]{:S(2)}, u32[]{:S(2)}) %all-to-all-start.6) | async-done | bytes 385056 | tf_op jit(solution)/shard_map/all_to_all | solution.py:384
  182.2 0.1 reshape.133
  182.3 0.2 reshape.134
  182.6 26.0 %all-gather.1 = bf16[12,6,4864]{2,1,0:T(8,128)(2,1)S(1)} all-gather(bf16[1,6,4864]{2,1,0:T(8,128)(2,1)S(1)} %maximum_bitcast_fusion), channel_id=2, replica_groups=mesh['ctx'=12,'ch'=64] {'ctx'}, dimensions={0}, use_global_device_ids=true | all-gather | bytes 758784 | tf_op jit(solution)/shard_map/all_gather | solution.py:608
  208.7 0.1 slice_convert_fusion
  208.8 0.7 slice.128
  209.5 0.7 slice.130
  210.2 1.3 reshape.139
  211.4 0.7 slice_reduce_fusion.1
  (99 shorter events, 1.3 us)
Async XLA Ops:
  0.6 8.8 %copy-start.9 = (bf16[3,72,256]{2,1,0:T(8,128)(2,1)S(1)}, bf16[3,72,256]{2,1,0:T(8,128)(2,1)}, u32[]{:S(2)}) copy-start(bf16[3,72,256]{2,1,0:T(8,128)(2,1)} %param.14) | copy-start | bytes 331780
  3.3 16.4 %copy-start.11 = (f32[3,72,3]{1,2,0:T(4,128)S(1)}, f32[3,72,3]{1,2,0:T(4,128)}, u32[]{:S(2)}) copy-start(f32[3,72,3]{1,2,0:T(4,128)} %param.15) | copy-start | bytes 7780
  3.3 16.5 %copy-start.10 = (f32[64,72]{1,0:T(8,128)S(1)}, f32[64,72]{1,0:T(8,128)}, u32[]{:S(2)}) copy-start(f32[64,72]{1,0:T(8,128)} %param.18) | copy-start | bytes 55300
  3.3 16.6 %copy-start.12 = (f32[72]{0:T(128)S(1)}, f32[72]{0:T(128)}, u32[]{:S(2)}) copy-start(f32[72]{0:T(128)} %param.19) | copy-start | bytes 868
  3.3 16.7 %copy-start.13 = (f32[72]{0:T(128)S(1)}, f32[72]{0:T(128)}, u32[]{:S(2)}) copy-start(f32[72]{0:T(128)} %param.20) | copy-start | bytes 868
  3.4 16.9 %copy-start = (bf16[256,512]{1,0:T(8,128)(2,1)S(1)}, bf16[256,512]{1,0:T(8,128)(2,1)}, u32[]{:S(2)}) copy-start(bf16[256,512]{1,0:T(8,128)(2,1)} %constant.104.clone.table_low) | copy-start | bytes 786436
  3.4 16.9 %copy-start.1 = (bf16[256,512]{1,0:T(8,128)(2,1)S(1)}, bf16[256,512]{1,0:T(8,128)(2,1)}, u32[]{:S(2)}) copy-start(bf16[256,512]{1,0:T(8,128)(2,1)} %constant.103.clone.table_high) | copy-start | bytes 786436
  3.4 16.9 %copy-start.2 = (f32[32,3072]{1,0:T(8,128)S(1)}, f32[32,3072]{1,0:T(8,128)}, u32[]{:S(2)}) copy-start(f32[32,3072]{1,0:T(8,128)} %constant.107.clone.features) | copy-start | bytes 1179652
  3.4 16.9 %copy-start.6 = (f32[64,64]{1,0:T(8,128)S(1)}, f32[64,64]{1,0:T(8,128)}, u32[]{:S(2)}) copy-start(f32[64,64]{1,0:T(8,128)} %filter_mid.3) | copy-start | bytes 49156
  3.4 16.9 %copy-start.7 = (f32[32,64]{1,0:T(8,128)S(1)}, f32[32,64]{1,0:T(8,128)}, u32[]{:S(2)}) copy-start(f32[32,64]{1,0:T(8,128)} %filter_in.1) | copy-start | bytes 24580
  3.4 23.2 %all-to-all-start = ((bf16[8,72,832]{2,1,0:T(8,128)(2,1)}), bf16[8,72,832]{2,1,0:T(8,128)(2,1)S(1)}, u32[]{:S(2)}, u32[]{:S(2)}) async-start(bf16[8,72,832]{2,1,0:T(8,128)(2,1)} %shard_map.181), calls=%async_computation | async-start | bytes 2064384 | tf_op jit(solution)/shard_map/all_to_all | solution.py:384
  9.6 21.1 %collective-permute-start = (bf16[6,24,256]{2,1,0:T(8,128)(2,1)S(1)}, bf16[6,24,256]{2,1,0:T(8,128)(2,1)}, u32[]{:S(2)}, u32[]{:S(2)}) collective-permute-start(bf16[6,24,256]{2,1,0:T(8,128)(2,1)S(1)} %dynamic-slice_bitcast_fusion.3), channel_id=1, source_target_pairs={{0,64},{64,0},{128,192},{192,128},{256,320},{320,256},{384,448},{4... | collective-permute-start | bytes 221192 | tf_op jit(solution)/shard_map/ppermute | solution.py:422
  27.3 13.8 %collective-permute-start.2 = (bf16[8,6,6,256]{3,0,2,1:T(8,128)(2,1)S(1)}, bf16[8,6,6,256]{3,0,2,1:T(8,128)(2,1)S(1)}, u32[]{:S(2)}, u32[]{:S(2)}) collective-permute-start(bf16[8,6,6,256]{3,0,2,1:T(8,128)(2,1)S(1)} %bitcast.138), channel_id=1, source_target_pairs={{0,64},{64,0},{128,192},{192,128},{256,320},{320,256},{384,448},{4... | collective-permute-start | bytes 442376 | tf_op jit(solution)/shard_map/ppermute | solution.py:422
  31.6 25.1 %copy-start.3 = (bf16[512,256]{1,0:T(8,128)(2,1)S(1)}, bf16[512,256]{1,0:T(8,128)(2,1)}, u32[]{:S(2)}) copy-start(bf16[512,256]{1,0:T(8,128)(2,1)} %constant.106.clone.back_low) | copy-start | bytes 786436
  31.6 25.1 %copy-start.4 = (bf16[512,256]{1,0:T(8,128)(2,1)S(1)}, bf16[512,256]{1,0:T(8,128)(2,1)}, u32[]{:S(2)}) copy-start(bf16[512,256]{1,0:T(8,128)(2,1)} %constant.105.clone.back_high) | copy-start | bytes 786436
  31.6 25.1 %copy-start.5 = (f32[12,8,512]{2,1,0:T(8,128)S(1)}, f32[12,8,512]{2,1,0:T(8,128)}, u32[]{:S(2)}) copy-start(f32[12,8,512]{2,1,0:T(8,128)} %get-tuple-element.22.spectra.kept_spectra) | copy-start | bytes 589828
  32.3 18.5 %all-to-all-start.1 = ((bf16[6,48,256]{2,1,0:T(8,128)(2,1)}), bf16[6,48,256]{2,1,0:T(8,128)(2,1)S(1)}, u32[]{:S(2)}, u32[]{:S(2)}) async-start(bf16[6,48,256]{2,1,0:T(8,128)(2,1)} %pad_maximum_fusion.4), calls=%async_computation.1 | async-start | bytes 294912 | tf_op jit(solution)/shard_map/all_to_all | solution.py:384
  50.8 14.8 %all-to-all-start.2 = ((bf16[4,2,72,256]{3,1,2,0:T(2,128)(2,1)}), bf16[4,2,72,256]{3,1,2,0:T(2,128)(2,1)S(1)}, u32[]{:S(2)}, u32[]{:S(2)}) async-start(bf16[4,2,72,256]{3,1,2,0:T(2,128)(2,1)} %copy.97), calls=%async_computation.2 | async-start | bytes 589824 | tf_op jit(solution)/shard_map/all_to_all | solution.py:384
  59.1 16.4 %collective-permute-start.1 = (bf16[6,8,256]{2,1,0:T(8,128)(2,1)S(1)}, bf16[6,8,256]{2,1,0:T(8,128)(2,1)S(1)}, u32[]{:S(2)}, u32[]{:S(2)}) collective-permute-start(bf16[6,8,256]{2,1,0:T(8,128)(2,1)S(1)} %dynamic-slice_bitcast_fusion.4), channel_id=1, source_target_pairs={{0,64},{64,0},{128,192},{192,128},{256,320},{320,256},{384,448},{4... | collective-permute-start | bytes 73736 | tf_op jit(solution)/shard_map/ppermute | solution.py:422
  65.7 11.1 %collective-permute-start.3 = (bf16[72,256]{1,0:T(8,128)(2,1)S(1)}, bf16[72,256]{1,0:T(8,128)(2,1)S(1)}, u32[]{:S(2)}, u32[]{:S(2)}) collective-permute-start(bf16[72,256]{1,0:T(8,128)(2,1)S(1)} %bitcast.141), channel_id=1, source_target_pairs={{0,32},{1,33},{2,34},{3,35},{4,36},{5,37},{6,38},{7,39},{8,40},{9,... | collective-permute-start | bytes 110600 | tf_op jit(solution)/shard_map/ppermute | solution.py:408
  88.7 44.8 %all-to-all-start.4 = ((bf16[8,72,256]{2,1,0:T(8,128)(2,1)}), bf16[8,72,256]{2,1,0:T(8,128)(2,1)S(1)}, u32[]{:S(2)}, u32[]{:S(2)}) async-start(bf16[8,72,256]{2,1,0:T(8,128)(2,1)} %broadcast_in_dim.29), calls=%async_computation.4 | async-start | bytes 589824 | tf_op jit(solution)/shard_map/all_to_all | solution.py:384
  106.1 24.8 %copy-start.8 = (bf16[12,48,128]{2,1,0:T(8,128)(2,1)S(1)}, bf16[12,48,128]{2,1,0:T(8,128)(2,1)}, u32[]{:S(2)}) copy-start(bf16[12,48,128]{2,1,0:T(8,128)(2,1)} %get-tuple-element.33) | copy-start | bytes 442372
  106.1 6.2 %collective-permute-start.4 = (f32[96,64]{1,0:T(8,128)S(1)}, f32[96,64]{1,0:T(8,128)S(1)}, u32[]{:S(2)}, u32[]{:S(2)}) collective-permute-start(f32[96,64]{1,0:T(8,128)S(1)} %get-tuple-element.31), channel_id=1, source_target_pairs={{0,8},{1,9},{2,10},{3,11},{4,12},{5,13},{6,14},{7,15},{8,0},{9,1},... | collective-permute-start | bytes 73736 | tf_op jit(solution)/shard_map/ppermute | solution.py:523
  112.4 9.9 %collective-permute-start.5 = (f32[96,64]{1,0:T(8,128)S(1)}, f32[96,64]{1,0:T(8,128)S(1)}, u32[]{:S(2)}, u32[]{:S(2)}) collective-permute-start(f32[96,64]{1,0:T(8,128)S(1)} %add.91), channel_id=1, source_target_pairs={{0,16},{1,17},{2,18},{3,19},{4,20},{5,21},{6,22},{7,23},{8,24},{9,... | collective-permute-start | bytes 73736 | tf_op jit(solution)/shard_map/ppermute | solution.py:523
  122.3 11.1 %collective-permute-start.6 = (f32[96,64]{1,0:T(8,128)S(1)}, f32[96,64]{1,0:T(8,128)S(1)}, u32[]{:S(2)}, u32[]{:S(2)}) collective-permute-start(f32[96,64]{1,0:T(8,128)S(1)} %add.92), channel_id=1, source_target_pairs={{0,32},{1,33},{2,34},{3,35},{4,36},{5,37},{6,38},{7,39},{8,40},{9,... | collective-permute-start | bytes 73736 | tf_op jit(solution)/shard_map/ppermute | solution.py:523
  133.9 11.2 %collective-permute-start.7 = (bf16[6,48,768]{2,1,0:T(8,128)(2,1)S(1)}, bf16[6,48,768]{2,1,0:T(8,128)(2,1)S(1)}, u32[]{:S(2)}, u32[]{:S(2)}) collective-permute-start(bf16[6,48,768]{2,1,0:T(8,128)(2,1)S(1)} %pad_maximum_fusion.1), channel_id=1, source_target_pairs={{0,64},{64,0},{128,192},{192,128},{256,320},{320,256},{384,448},{4... | collective-permute-start | bytes 1327112 | tf_op jit(solution)/shard_map/ppermute | solution.py:556
  146.5 24.3 %all-to-all-start.5 = ((bf16[6,48,896]{2,1,0:T(8,128)(2,1)}), bf16[6,48,896]{2,1,0:T(8,128)(2,1)S(1)}, u32[]{:S(2)}, u32[]{:S(2)}) async-start(bf16[6,48,896]{2,1,0:T(8,128)(2,1)} %pad_maximum_fusion), calls=%async_computation.5 | async-start | bytes 1032192 | tf_op jit(solution)/shard_map/all_to_all | solution.py:384
  171.9 10.1 %all-to-all-start.6 = ((bf16[8,94,256]{2,1,0:T(8,128)(2,1)}), bf16[8,94,256]{2,1,0:T(8,128)(2,1)S(1)}, u32[]{:S(2)}, u32[]{:S(2)}) async-start(bf16[8,94,256]{2,1,0:T(8,128)(2,1)} %pad_maximum_fusion.2), calls=%async_computation.6 | async-start | bytes 786432 | tf_op jit(solution)/shard_map/all_to_all | solution.py:384
